TPU v7x, 32 devices: a whole 2x2x4 slice. The times are simulated.
32 devices in a mesh: seq: 4 (over y, x), fsdp: 8 (over z, core).
Axes of the slice: x: 2, y: 2, z: 4, core: 2. Of those that a mesh axis runs over, the one named last changes fastest.
Arguments:
- images: bfloat16 [16, 1024, 1024], P('fsdp', 'seq'), may hold values from -20 to 20
- out_grad: bfloat16 [16, 1024, 1024], P('fsdp', 'seq'), may hold values from -6 to 6
- lengths: int32 [16], P('fsdp'), may hold values from 512 to 1024, as said below
- images_held: int32 [8], replicated, may hold values from 1 to 2, as said below
- first_gain: bfloat16 [1024], P('fsdp'), may hold values from 0.5 to 1.5
- first_shift: bfloat16 [1024], P('fsdp'), may hold values from -4 to 4
- entry_weight: bfloat16 [1024, 3072], P('fsdp'), may hold values from -1 to 1
- entry_bias: bfloat16 [2048], P('fsdp'), may hold values from -6 to 6
- exit_weight: bfloat16 [1024, 1024], P('fsdp'), may hold values from -1.5 to 1.5
- exit_bias: bfloat16 [1024], P('fsdp'), may hold values from -4 to 4
- first_scale: bfloat16 [1024], P('fsdp'), may hold values from 0.5 to 2
- second_gain: bfloat16 [1024], P('fsdp'), may hold values from 0.5 to 1.5
- second_shift: bfloat16 [1024], P('fsdp'), may hold values from -4 to 4
- up_weight: bfloat16 [1024, 4096], P('fsdp'), may hold values from -0.1875 to 0.1875
- up_bias: bfloat16 [4096], P('fsdp'), may hold values from -6 to 6
- down_weight: bfloat16 [4096, 1024], P('fsdp'), may hold values from -0.09375 to 0.09375
- down_bias: bfloat16 [1024], P('fsdp'), may hold values from -4 to 4
- second_scale: bfloat16 [1024], P('fsdp'), may hold values from 0.5 to 2
Outputs:
- layer_out: bfloat16 [16, 1024, 1024], P('fsdp', 'seq')
- input_grad: float32 [16, 1024, 1024], P('fsdp', 'seq')
- first_gain_grad: float32 [1024], P('fsdp')
- first_shift_grad: float32 [1024], P('fsdp')
- entry_weight_grad: float32 [1024, 3072], P('fsdp')
- entry_bias_grad: float32 [2048], P('fsdp')
- exit_weight_grad: float32 [1024, 1024], P('fsdp')
- exit_bias_grad: float32 [1024], P('fsdp')
- first_scale_grad: float32 [1024], P('fsdp')
- second_gain_grad: float32 [1024], P('fsdp')
- second_shift_grad: float32 [1024], P('fsdp')
- up_weight_grad: float32 [1024, 4096], P('fsdp')
- up_bias_grad: float32 [4096], P('fsdp')
- down_weight_grad: float32 [4096, 1024], P('fsdp')
- down_bias_grad: float32 [1024], P('fsdp')
- second_scale_grad: float32 [1024], P('fsdp')
Inputs may be any that keep to these rules, and one draw needn't show every extreme that they name: `images_held`: entry g is how many images fsdp group g holds; they fill its first slots. `lengths`: positions from the length on are padding.
All inputs are finite; a program needn't handle non-finite values.
Results may differ from a plain program's by a relative error of at most 0.017.
The roundings to bfloat16 on the way count: a program that leaves them out, or rounds other values in their place, can miss the bound.
Values may be sent and summed in bfloat16 or wider, within the bound.
A program may use at most 320 MiB of HBM per device.

v0:
```python
import math

import jax
import jax.numpy as jnp
from jax import lax
from jax.sharding import PartitionSpec as P

HEADS = 16
HEAD_DIM = 64


EPSILON = 1e-06
NEG_LARGE = -1e30


def layer_norm(values):
    centre = jnp.mean(values, axis=-1, keepdims=True)
    shifted = values - centre
    spread = jnp.mean(shifted * shifted, axis=-1, keepdims=True)
    inverse = lax.rsqrt(spread + EPSILON)
    return (shifted * inverse, inverse)


def norm_back(normed_cot, normed, inverse):
    return inverse * (
        normed_cot
        - jnp.mean(normed_cot, axis=-1, keepdims=True)
        - normed * jnp.mean(normed_cot * normed, axis=-1, keepdims=True)
    )


def gelu_parts(pre_act):
    cumul = 0.5 * (1.0 + lax.erf(pre_act * (1.0 / math.sqrt(2.0))))
    density = jnp.exp(-0.5 * pre_act * pre_act) * (1.0 / math.sqrt(2.0 * math.pi))
    return (pre_act * cumul, cumul + pre_act * density)


def score_rows(queries, key_rows, key_valid, score_scale):
    scores = (
        jnp.einsum("qhd,khd->hqk", queries, key_rows, preferred_element_type=jnp.float32)
        * score_scale
    )
    return jnp.where(key_valid[None, None, :], scores, NEG_LARGE)


def attend(queries, key_rows, value_rows, key_valid, score_scale):
    scores = score_rows(queries, key_rows, key_valid, score_scale)
    highest = jnp.max(scores, axis=2, keepdims=True)
    logsum = highest + jnp.log(jnp.sum(jnp.exp(scores - highest), axis=2, keepdims=True))
    weights = jnp.exp(scores - logsum).astype(jnp.bfloat16)
    attended = jnp.einsum("hqk,khd->qhd", weights, value_rows, preferred_element_type=jnp.float32)
    return (attended.astype(jnp.bfloat16), logsum)


def attend_back(
    queries, key_rows, value_rows, attended, attended_cot, logsum, key_valid, score_scale
):
    scores = score_rows(queries, key_rows, key_valid, score_scale)
    probability = jnp.exp(scores - logsum)
    weights = probability.astype(jnp.bfloat16)
    row_delta = jnp.sum(attended.astype(jnp.float32) * attended_cot.astype(jnp.float32), axis=2)
    score_grad = jnp.einsum(
        "qhd,khd->hqk", attended_cot, value_rows, preferred_element_type=jnp.float32
    )
    score_cot = probability * (score_grad - jnp.transpose(row_delta)[:, :, None])
    scaled = (score_cot * score_scale).astype(jnp.bfloat16)
    query_cot = jnp.einsum("hqk,khd->qhd", scaled, key_rows, preferred_element_type=jnp.float32)
    key_cot = jnp.einsum("hqk,qhd->khd", scaled, queries, preferred_element_type=jnp.float32)
    value_cot = jnp.einsum(
        "hqk,qhd->khd", weights, attended_cot, preferred_element_type=jnp.float32
    )
    return (
        query_cot.astype(jnp.bfloat16),
        key_cot.astype(jnp.bfloat16),
        value_cot.astype(jnp.bfloat16),
    )


def body(
    images,
    out_grad,
    lengths,
    images_held,
    first_gain,
    first_shift,
    entry_weight,
    entry_bias,
    exit_weight,
    exit_bias,
    first_scale,
    second_gain,
    second_shift,
    up_weight,
    up_bias,
    down_weight,
    down_bias,
    second_scale,
):
    gathered = (
        lax.all_gather(first_gain, "fsdp", axis=0, tiled=True),
        lax.all_gather(first_shift, "fsdp", axis=0, tiled=True),
        lax.all_gather(entry_weight, "fsdp", axis=0, tiled=True),
        lax.all_gather(entry_bias, "fsdp", axis=0, tiled=True),
        lax.all_gather(exit_weight, "fsdp", axis=0, tiled=True),
        lax.all_gather(exit_bias, "fsdp", axis=0, tiled=True),
        lax.all_gather(first_scale, "fsdp", axis=0, tiled=True),
        lax.all_gather(second_gain, "fsdp", axis=0, tiled=True),
        lax.all_gather(second_shift, "fsdp", axis=0, tiled=True),
        lax.all_gather(up_weight, "fsdp", axis=0, tiled=True),
        lax.all_gather(up_bias, "fsdp", axis=0, tiled=True),
        lax.all_gather(down_weight, "fsdp", axis=0, tiled=True),
        lax.all_gather(down_bias, "fsdp", axis=0, tiled=True),
        lax.all_gather(second_scale, "fsdp", axis=0, tiled=True),
    )
    (
        gain_low,
        shift_low,
        entry_full,
        entry_vec,
        exit_full,
        exit_low,
        scale_low,
        gain_low_two,
        shift_low_two,
        up_full,
        up_low,
        down_full,
        down_low,
        scale_low_two,
    ) = gathered
    model_width = entry_full.shape[0]
    gain_one = gain_low.astype(jnp.float32)
    shift_one = shift_low.astype(jnp.float32)
    query_bias = entry_vec[:model_width].astype(jnp.float32)
    value_bias = entry_vec[model_width:].astype(jnp.float32)
    exit_vec = exit_low.astype(jnp.float32)
    scale_one = scale_low.astype(jnp.float32)
    gain_two = gain_low_two.astype(jnp.float32)
    shift_two = shift_low_two.astype(jnp.float32)
    up_vec = up_low.astype(jnp.float32)
    down_vec = down_low.astype(jnp.float32)
    scale_two = scale_low_two.astype(jnp.float32)
    seq_count = lax.axis_size("seq")
    seq_index = lax.axis_index("seq")
    group_index = lax.axis_index("fsdp")
    slot_count = images.shape[0]
    tok_rows = images.shape[1]
    pad_len = tok_rows * seq_count
    heads_here = HEADS // seq_count
    score_scale = HEAD_DIM ** (-0.5)
    head_shape = (pad_len, heads_here, HEAD_DIM)
    flat_shape = (pad_len, heads_here * HEAD_DIM)
    held_count = lax.dynamic_index_in_dim(images_held, group_index, 0, keepdims=False)
    positions = seq_index * tok_rows + jnp.arange(tok_rows, dtype=jnp.int32)
    key_positions = jnp.arange(pad_len, dtype=jnp.int32)
    zero_grads = tuple((jnp.zeros(portion.shape, jnp.float32) for portion in gathered))

    def one_image(slot_index, carried):
        layer_buf, input_buf, weight_cotangent_bundle = carried
        picture = lax.dynamic_index_in_dim(images, slot_index, 0, keepdims=False).astype(
            jnp.float32
        )
        cotangent = lax.dynamic_index_in_dim(out_grad, slot_index, 0, keepdims=False).astype(
            jnp.float32
        )
        length = lax.dynamic_index_in_dim(lengths, slot_index, 0, keepdims=False)
        alive = slot_index < held_count
        token_mask = jnp.where((positions < length) & alive, 1.0, 0.0).astype(jnp.float32)[:, None]
        key_valid = key_positions < length
        leading_standardize_result, first_inverse = layer_norm(picture)
        leading_standardize_source = (leading_standardize_result * gain_one + shift_one).astype(
            jnp.bfloat16
        )
        projected = jnp.dot(
            leading_standardize_source, entry_full, preferred_element_type=jnp.float32
        )
        queries = (projected[:, :model_width] + query_bias).astype(jnp.bfloat16)
        key_rows = projected[:, model_width : 2 * model_width].astype(jnp.bfloat16)
        value_rows = (projected[:, 2 * model_width :] + value_bias).astype(jnp.bfloat16)
        by_heads = lax.all_to_all(
            jnp.stack([queries, key_rows, value_rows]),
            "seq",
            split_axis=2,
            concat_axis=1,
            tiled=True,
        )
        head_queries = by_heads[0].reshape(head_shape)
        head_keys = by_heads[1].reshape(head_shape)
        head_values = by_heads[2].reshape(head_shape)
        attended, logsum = attend(head_queries, head_keys, head_values, key_valid, score_scale)
        softmax_blend_tokens_out = lax.all_to_all(
            attended.reshape(flat_shape), "seq", split_axis=0, concat_axis=1, tiled=True
        )
        softmax_blend_result = (
            jnp.dot(softmax_blend_tokens_out, exit_full, preferred_element_type=jnp.float32)
            + exit_vec
        )
        residual = picture + scale_one * softmax_blend_result
        later_standardize_result, second_inverse = layer_norm(residual)
        later_standardize_source = (later_standardize_result * gain_two + shift_two).astype(
            jnp.bfloat16
        )
        hidden_pre = (
            jnp.dot(later_standardize_source, up_full, preferred_element_type=jnp.float32) + up_vec
        )
        activated_full, slope = gelu_parts(hidden_pre)
        gelu_applied_inner = activated_full.astype(jnp.bfloat16)
        contract_map_result = (
            jnp.dot(gelu_applied_inner, down_full, preferred_element_type=jnp.float32) + down_vec
        )
        layer_rows = (token_mask * (residual + scale_two * contract_map_result)).astype(
            jnp.bfloat16
        )
        incoming_cotangent = token_mask * cotangent
        contract_map_piece = incoming_cotangent * scale_two
        contract_map_cotangent = contract_map_piece.astype(jnp.bfloat16)
        act_cot = jnp.dot(contract_map_cotangent, down_full.T, preferred_element_type=jnp.float32)
        before_gelu_cotangent = act_cot * slope
        before_gelu_narrowed = before_gelu_cotangent.astype(jnp.bfloat16)
        later_standardize_cotangent = jnp.dot(
            before_gelu_narrowed, up_full.T, preferred_element_type=jnp.float32
        )
        skip_path_cotangent = incoming_cotangent + norm_back(
            later_standardize_cotangent * gain_two, later_standardize_result, second_inverse
        )
        softmax_blend_cotangent_sum = skip_path_cotangent * scale_one
        softmax_blend_narrowed = softmax_blend_cotangent_sum.astype(jnp.bfloat16)
        attended_cot = jnp.dot(
            softmax_blend_narrowed, exit_full.T, preferred_element_type=jnp.float32
        ).astype(jnp.bfloat16)
        cot_by_heads = lax.all_to_all(attended_cot, "seq", split_axis=1, concat_axis=0, tiled=True)
        query_cot, key_cot, value_cot = attend_back(
            head_queries,
            head_keys,
            head_values,
            attended,
            cot_by_heads.reshape(head_shape),
            logsum,
            key_valid,
            score_scale,
        )
        back_rows = lax.all_to_all(
            jnp.stack(
                [
                    query_cot.reshape(flat_shape),
                    key_cot.reshape(flat_shape),
                    value_cot.reshape(flat_shape),
                ]
            ),
            "seq",
            split_axis=1,
            concat_axis=2,
            tiled=True,
        )
        expand_map_cotangent = jnp.concatenate([back_rows[0], back_rows[1], back_rows[2]], axis=1)
        leading_standardize_cotangent = jnp.dot(
            expand_map_cotangent, entry_full.T, preferred_element_type=jnp.float32
        )
        input_rows = skip_path_cotangent + norm_back(
            leading_standardize_cotangent * gain_one, leading_standardize_result, first_inverse
        )
        cotangent_pieces_list = (
            jnp.sum(leading_standardize_cotangent * leading_standardize_result, axis=0),
            jnp.sum(leading_standardize_cotangent, axis=0),
            jnp.dot(
                leading_standardize_source.T,
                expand_map_cotangent,
                preferred_element_type=jnp.float32,
            ),
            jnp.concatenate(
                [
                    jnp.sum(back_rows[0].astype(jnp.float32), axis=0),
                    jnp.sum(back_rows[2].astype(jnp.float32), axis=0),
                ]
            ),
            jnp.dot(
                softmax_blend_tokens_out.T,
                softmax_blend_narrowed,
                preferred_element_type=jnp.float32,
            ),
            jnp.sum(softmax_blend_cotangent_sum, axis=0),
            jnp.sum(skip_path_cotangent * softmax_blend_result, axis=0),
            jnp.sum(later_standardize_cotangent * later_standardize_result, axis=0),
            jnp.sum(later_standardize_cotangent, axis=0),
            jnp.dot(
                later_standardize_source.T, before_gelu_narrowed, preferred_element_type=jnp.float32
            ),
            jnp.sum(before_gelu_cotangent, axis=0),
            jnp.dot(
                gelu_applied_inner.T, contract_map_cotangent, preferred_element_type=jnp.float32
            ),
            jnp.sum(contract_map_piece, axis=0),
            jnp.sum(incoming_cotangent * contract_map_result, axis=0),
        )
        weight_cotangent_bundle = tuple(
            (
                accumulated_sum + cotangent_piece
                for accumulated_sum, cotangent_piece in zip(
                    weight_cotangent_bundle, cotangent_pieces_list
                )
            )
        )
        layer_buf = lax.dynamic_update_index_in_dim(layer_buf, layer_rows, slot_index, 0)
        input_buf = lax.dynamic_update_index_in_dim(input_buf, input_rows, slot_index, 0)
        return (layer_buf, input_buf, weight_cotangent_bundle)

    start_state = (
        jnp.zeros(images.shape, jnp.bfloat16),
        jnp.zeros(images.shape, jnp.float32),
        zero_grads,
    )
    layer_buf, input_buf, weight_cotangent_bundle = lax.fori_loop(
        0, slot_count, one_image, start_state
    )
    shards = (
        lax.psum_scatter(
            weight_cotangent_bundle[0].astype(jnp.bfloat16), "fsdp", scatter_dimension=0, tiled=True
        ).astype(jnp.float32),
        lax.psum_scatter(
            weight_cotangent_bundle[1].astype(jnp.bfloat16), "fsdp", scatter_dimension=0, tiled=True
        ).astype(jnp.float32),
        lax.psum_scatter(
            weight_cotangent_bundle[2].astype(jnp.bfloat16), "fsdp", scatter_dimension=0, tiled=True
        ).astype(jnp.float32),
        lax.psum_scatter(
            weight_cotangent_bundle[3].astype(jnp.bfloat16), "fsdp", scatter_dimension=0, tiled=True
        ).astype(jnp.float32),
        lax.psum_scatter(
            weight_cotangent_bundle[4].astype(jnp.bfloat16), "fsdp", scatter_dimension=0, tiled=True
        ).astype(jnp.float32),
        lax.psum_scatter(
            weight_cotangent_bundle[5].astype(jnp.bfloat16), "fsdp", scatter_dimension=0, tiled=True
        ).astype(jnp.float32),
        lax.psum_scatter(
            weight_cotangent_bundle[6].astype(jnp.bfloat16), "fsdp", scatter_dimension=0, tiled=True
        ).astype(jnp.float32),
        lax.psum_scatter(
            weight_cotangent_bundle[7].astype(jnp.bfloat16), "fsdp", scatter_dimension=0, tiled=True
        ).astype(jnp.float32),
        lax.psum_scatter(
            weight_cotangent_bundle[8].astype(jnp.bfloat16), "fsdp", scatter_dimension=0, tiled=True
        ).astype(jnp.float32),
        lax.psum_scatter(
            weight_cotangent_bundle[9].astype(jnp.bfloat16), "fsdp", scatter_dimension=0, tiled=True
        ).astype(jnp.float32),
        lax.psum_scatter(
            weight_cotangent_bundle[10].astype(jnp.bfloat16),
            "fsdp",
            scatter_dimension=0,
            tiled=True,
        ).astype(jnp.float32),
        lax.psum_scatter(
            weight_cotangent_bundle[11].astype(jnp.bfloat16),
            "fsdp",
            scatter_dimension=0,
            tiled=True,
        ).astype(jnp.float32),
        lax.psum_scatter(
            weight_cotangent_bundle[12].astype(jnp.bfloat16),
            "fsdp",
            scatter_dimension=0,
            tiled=True,
        ).astype(jnp.float32),
        lax.psum_scatter(
            weight_cotangent_bundle[13].astype(jnp.bfloat16),
            "fsdp",
            scatter_dimension=0,
            tiled=True,
        ).astype(jnp.float32),
    )
    reduced = (
        lax.psum(shards[0].astype(jnp.bfloat16), "seq").astype(jnp.float32),
        lax.psum(shards[1].astype(jnp.bfloat16), "seq").astype(jnp.float32),
        lax.psum(shards[2].astype(jnp.bfloat16), "seq").astype(jnp.float32),
        lax.psum(shards[3].astype(jnp.bfloat16), "seq").astype(jnp.float32),
        lax.psum(shards[4].astype(jnp.bfloat16), "seq").astype(jnp.float32),
        lax.psum(shards[5].astype(jnp.bfloat16), "seq").astype(jnp.float32),
        lax.psum(shards[6].astype(jnp.bfloat16), "seq").astype(jnp.float32),
        lax.psum(shards[7].astype(jnp.bfloat16), "seq").astype(jnp.float32),
        lax.psum(shards[8].astype(jnp.bfloat16), "seq").astype(jnp.float32),
        lax.psum(shards[9].astype(jnp.bfloat16), "seq").astype(jnp.float32),
        lax.psum(shards[10].astype(jnp.bfloat16), "seq").astype(jnp.float32),
        lax.psum(shards[11].astype(jnp.bfloat16), "seq").astype(jnp.float32),
        lax.psum(shards[12].astype(jnp.bfloat16), "seq").astype(jnp.float32),
        lax.psum(shards[13].astype(jnp.bfloat16), "seq").astype(jnp.float32),
    )
    return (
        layer_buf,
        input_buf,
        reduced[0],
        reduced[1],
        reduced[2],
        reduced[3],
        reduced[4],
        reduced[5],
        reduced[6],
        reduced[7],
        reduced[8],
        reduced[9],
        reduced[10],
        reduced[11],
        reduced[12],
        reduced[13],
    )


def solution(mesh):
    return jax.shard_map(
        body,
        mesh=mesh,
        in_specs=(
            P("fsdp", "seq", None),
            P("fsdp", "seq", None),
            P("fsdp"),
            P(),
            P("fsdp"),
            P("fsdp"),
            P("fsdp", None),
            P("fsdp"),
            P("fsdp", None),
            P("fsdp"),
            P("fsdp"),
            P("fsdp"),
            P("fsdp"),
            P("fsdp", None),
            P("fsdp"),
            P("fsdp", None),
            P("fsdp"),
            P("fsdp"),
        ),
        out_specs=(
            P("fsdp", "seq", None),
            P("fsdp", "seq", None),
            P("fsdp"),
            P("fsdp"),
            P("fsdp", None),
            P("fsdp"),
            P("fsdp", None),
            P("fsdp"),
            P("fsdp"),
            P("fsdp"),
            P("fsdp"),
            P("fsdp", None),
            P("fsdp"),
            P("fsdp", None),
            P("fsdp"),
            P("fsdp"),
        ),
        check_vma=False,
    )
```

profile of v0, /device:TPU:0, one launch (start us, length us, event | category | flops | bytes accessed | tf_op | source)
XLA Modules:
  0.0 1089.8 jit_solution(18319881491968613642)
XLA Ops:
  11.5 14.4 %all-gather.8 = bf16[8,1,512]{2,1,0:T(2,128)(2,1)S(1)} all-gather(bf16[1,1,512]{2,1,0:T(2,128)(2,1)S(1)} %reshape.206), channel_id=1, replica_groups=mesh['seq'=4,'fsdp'=8] {'fsdp'}, dimensions={0}, use_global_device_ids=true | all-gather | bytes 9216 | tf_op jit(solution)/shard_map/all_gather | solution.py:110
  26.0 11.1 %all-gather.4 = bf16[8,1,128]{2,1,0:T(2,128)(2,1)S(1)} all-gather(bf16[1,1,128]{2,1,0:T(2,128)(2,1)} %bitcast.297), channel_id=1, replica_groups=mesh['seq'=4,'fsdp'=8] {'fsdp'}, dimensions={0}, use_global_device_ids=true | all-gather | bytes 2304 | tf_op jit(solution)/shard_map/all_gather | solution.py:105
  37.1 8.8 all-gather.5
  45.8 10.4 all-gather.6
  56.2 9.0 all-gather.7
  65.2 10.1 all-gather.9
  75.3 10.9 %all-gather = bf16[8,1,128]{2,1,0:T(2,128)(2,1)S(1)} all-gather(bf16[1,1,128]{2,1,0:T(2,128)(2,1)} %bitcast.302), channel_id=1, replica_groups=mesh['seq'=4,'fsdp'=8] {'fsdp'}, dimensions={0}, use_global_device_ids=true | all-gather | bytes 2304 | tf_op jit(solution)/shard_map/all_gather | solution.py:106
  86.3 9.0 all-gather.1
  95.3 10.1 all-gather.2
  106.6 8.8 all-gather.3
  115.5 74.3 %all-gather.19.cloned.1.call-done = bf16[1024,4096]{1,0:T(8,128)(2,1)} async-done(((bf16[128,4096]{1,0:T(8,128)(2,1)}), bf16[1024,4096]{1,0:T(8,128)(2,1)}) %all-gather.19.cloned.1.call-update) | async-done | bytes 8388624 | tf_op jit(solution)/shard_map/all_gather | solution.py:109
  189.8 82.1 %all-gather.21.cloned.1.call-done = bf16[4096,1024]{1,0:T(8,128)(2,1)} async-done(((bf16[512,1024]{1,0:T(8,128)(2,1)}), bf16[4096,1024]{1,0:T(8,128)(2,1)}) %all-gather.21.cloned.1.call-update) | async-done | bytes 8388624 | tf_op jit(solution)/shard_map/all_gather | solution.py:111
  271.9 425.1 %while.44 = (s32[]{:T(128)}, bf16[2,256,1024]{2,1,0:T(8,128)(2,1)}, f32[2,256,1024]{2,1,0:T(8,128)}, f32[1024]{0:T(1024)S(1)}, f32[1024]{0:T(1024)S(1)}, /*index...) while((s32[]{:T(128)}, bf16[2,256,1024]{2,1,0:T(8,128)(2,1)}, ...), condition=%wide.region_23.24_spmd.clone, body=%wide.region_0.23_spmd.clone.sunk | while | flops 22718457856 | bytes 612951424 | solution.py:312
  274.5 4.9 fusion.155
  282.4 4.0 all-to-all-start
  287.7 24.2 %all-to-all-done = bf16[3,256,1024]{1,0,2:T(4,128)(2,1)S(1)} async-done(((bf16[3,256,1024]{1,0,2:T(4,128)(2,1)}), bf16[3,256,1024]{1,0,2:T(4,128)(2,1)S(1)}, u32[]{:S(2)}, u32[]{:S(2)}) %all-to-all-start) | async-done | bytes 1572896 | tf_op jit(solution)/shard_map/while/body/eval_jaxpr/all_to_all | solution.py:180
  318.0 4.0 exponential_reduce_fusion.2
  323.7 5.7 fusion.160
  329.8 5.2 fusion.161
  338.0 4.1 all-to-all-start.1
  343.4 6.4 all-to-all-done.1
  353.0 6.0 convolution_add_fusion.4
  359.0 7.5 fusion.164
  369.3 5.8 fusion.163
  382.5 9.9 select_add_fusion.27
  398.0 9.8 multiply_convert_fusion.15
  423.1 5.6 pad_maximum_fusion.10
  428.8 4.9 all-to-all-start.3
  433.6 8.9 select_add_fusion.29
  442.5 14.9 %all-to-all-done.3 = bf16[3,1024,256]{2,0,1:T(4,128)(2,1)} async-done(((bf16[3,1024,256]{2,0,1:T(4,128)(2,1)}), bf16[3,1024,256]{2,0,1:T(4,128)(2,1)}, u32[]{:S(2)}, u32[]{:S(2)}) %all-to-all-start.3) | async-done | bytes 1572896 | tf_op jit(solution)/shard_map/while/body/eval_jaxpr/all_to_all | solution.py:242
  463.6 5.3 fusion.167
  469.0 7.8 select_add_fusion.23
  481.4 4.9 fusion.155
  489.4 4.1 all-to-all-start
  494.8 23.1 %all-to-all-done = bf16[3,256,1024]{1,0,2:T(4,128)(2,1)S(1)} async-done(((bf16[3,256,1024]{1,0,2:T(4,128)(2,1)}), bf16[3,256,1024]{1,0,2:T(4,128)(2,1)S(1)}, u32[]{:S(2)}, u32[]{:S(2)}) %all-to-all-start) | async-done | bytes 1572896 | tf_op jit(solution)/shard_map/while/body/eval_jaxpr/all_to_all | solution.py:180
  523.9 4.0 exponential_reduce_fusion.2
  529.6 5.7 fusion.160
  535.7 5.2 fusion.161
  544.0 3.6 all-to-all-start.1
  549.0 6.1 all-to-all-done.1
  558.2 6.0 convolution_add_fusion.4
  564.3 7.5 fusion.164
  574.5 5.8 fusion.163
  584.1 3.7 all-to-all-start.2
  587.8 14.7 %select_add_fusion.27 = f32[1024,4096]{1,0:T(8,128)} fusion(f32[1024,4096]{1,0:T(8,128)} %get-tuple-element.1266, pred[]{:T(512)S(6)} %compare.3, bf16[256,4096]{1,0:T(8,128)(2,1)} %copy-done.13, f32[256,1024]{1,0:T(8,128)S(1)} %get-tuple-element.1178, f32[1024]{0:T(1024)S(1)} %get-tuple-element.1323, f32[1024]{0:T(1024)S(1)} %get-tuple-element.1322, ...), kind=kOutput, calls=%fused_computation.3.clone.1 | convolution fusion | flops 2157182976 | bytes 36710400 | tf_op jit(solution)/shard_map/while/body/eval_jaxpr/dot_general | solution.py:285
  602.5 5.0 select_add_fusion.24
  610.4 9.8 multiply_convert_fusion.15
  635.6 5.6 pad_maximum_fusion.10
  641.2 5.1 all-to-all-start.3
  646.3 12.8 %select_add_fusion.29 = f32[4096,1024]{1,0:T(8,128)} fusion(f32[4096,1024]{1,0:T(8,128)} %get-tuple-element.1268, pred[]{:T(512)S(6)} %compare.3, f32[1024]{0:T(1024)S(1)} %get-tuple-element.1321, f32[256]{0:T(256)S(1)} %and_select_fusion.2, bf16[2,256,1024]{2,1,0:T(8,128)(2,1)S(1)} %copy-done.19, s32[]{:T(128)S(6)} %copy.143, f32[256,4096]{1,0:T(8,128)} %copy-done.1), kind=kOutput, calls=%fused_computation.2.clone.1 | convolution fusion | flops 2162163712 | bytes 38278148 | tf_op jit(solution)/shard_map/while/body/eval_jaxpr/dot_general | solution.py:289
  659.1 10.7 all-to-all-done.3
  676.0 5.3 fusion.167
  681.3 10.7 select_add_fusion.23
  697.0 3.8 convert_element_type.344
  700.9 8.3 convert_element_type.340
  709.3 9.2 convert_element_type.358
  718.6 9.1 convert_element_type.354
  727.7 6.7 reduce-scatter.7.cloned.1.call-done
  734.5 70.6 %reduce-scatter.5.cloned.1.call-done = bf16[128,3072]{1,0:T(8,128)(2,1)} async-done(((bf16[1024,3072]{1,0:T(8,128)(2,1)}), bf16[128,3072]{1,0:T(8,128)(2,1)}) %reduce-scatter.5.cloned.1.call-update) | async-done | bytes 786448 | tf_op jit(solution)/shard_map/reduce_scatter | solution.py:322
  805.1 90.3 %reduce-scatter.11.cloned.1.call-done = bf16[512,1024]{1,0:T(8,128)(2,1)} async-done(((bf16[4096,1024]{1,0:T(8,128)(2,1)}), bf16[512,1024]{1,0:T(8,128)(2,1)}) %reduce-scatter.11.cloned.1.call-update) | async-done | bytes 1048592 | tf_op jit(solution)/shard_map/reduce_scatter | solution.py:352
  895.4 90.3 %reduce-scatter.9.cloned.1.call-done = bf16[128,4096]{1,0:T(8,128)(2,1)} async-done(((bf16[1024,4096]{1,0:T(8,128)(2,1)}), bf16[128,4096]{1,0:T(8,128)(2,1)}) %reduce-scatter.9.cloned.1.call-update) | async-done | bytes 1048592 | tf_op jit(solution)/shard_map/reduce_scatter | solution.py:343
  988.4 26.1 %all-reduce.10 = (bf16[1024]{0:T(1024)(128)(2,1)S(1)}, bf16[1024]{0:T(1024)(128)(2,1)S(1)}, bf16[2048]{0:T(1024)(128)(2,1)S(1)}, bf16[1024]{0:T(1024)(128)(2,1)S...) all-reduce(bf16[1024]{0:T(1024)(128)(2,1)S(1)} %convert_element_typ, ...), channel_id=2, replica_groups=mesh['seq'=4,'fsdp'=8] {'fsdp'}, use_global_device_ids=true, to_apply=%region_24.25.clone | all-reduce | flops 14336 | bytes 57344
  1015.2 10.2 all-reduce.11
  1030.6 44.6 %all-reduce.15.cloned.1.call-done = (bf16[128,3072]{1,0:T(8,128)(2,1)}, bf16[128,1024]{1,0:T(8,128)(2,1)}, bf16[128,4096]{1,0:T(8,128)(2,1)}, bf16[512,1024]{1,0:T(8,128)(2,1)}) async-done(((bf16[128,3072]{1,0:T(8,128)(2,1)}, bf16[128,1024]{1,0:T(8,128)(2,1)}, bf16[128,4096]{1,0:T(8,128)(2,1)}, bf16[512,1024]{1,0:T(8,128)(2,1)}), (bf16[128,3072]{1,0:T(8,128)(2,1)}, bf16[128,1024]{1,0:T(8,128)(2,1)}, ...) | async-done | bytes 3145744 | tf_op jit(solution)/shard_map/psum | solution.py:374
  (324 shorter events, 135.0 us)
Async XLA Ops:
  7.2 108.3 %all-gather.17.cloned.1.call-start = ((), (), s32[]{:S(2)}) async-start(), calls=%async_computation.9 | async-start | bytes 2359296 | tf_op jit(solution)/shard_map/all_gather | solution.py:104
  7.9 107.6 %all-gather.15.cloned.1.call-start = ((), (), s32[]{:S(2)}) async-start(), calls=%async_computation.8 | async-start | bytes 7077888 | tf_op jit(solution)/shard_map/all_gather | solution.py:102
  8.7 181.2 %all-gather.19.cloned.1.call-start = ((), (), s32[]{:S(2)}) async-start(), calls=%async_computation.10 | async-start | bytes 9437184 | tf_op jit(solution)/shard_map/all_gather | solution.py:109
  9.4 262.5 %all-gather.21.cloned.1.call-start = ((), (), s32[]{:S(2)}) async-start(), calls=%async_computation.11 | async-start | bytes 9437184 | tf_op jit(solution)/shard_map/all_gather | solution.py:111
  10.0 724.5 %reduce-scatter.7.cloned.1.call-start = ((), (), s32[]{:S(2)}) async-start(), calls=%async_computation.13 | async-start | bytes 2359296 | tf_op jit(solution)/shard_map/reduce_scatter | solution.py:328
  279.9 6.6 copy-start.24
  282.4 29.5 %all-to-all-start = ((bf16[3,256,1024]{1,0,2:T(4,128)(2,1)}), bf16[3,256,1024]{1,0,2:T(4,128)(2,1)S(1)}, u32[]{:S(2)}, u32[]{:S(2)}) async-start(bf16[3,256,1024]{1,0,2:T(4,128)(2,1)} %copy.110), calls=%async_computation | async-start | bytes 4194304 | tf_op jit(solution)/shard_map/while/body/eval_jaxpr/all_to_all | solution.py:180
  314.3 3.6 copy-start.5
  314.7 3.3 copy-start.7
  317.9 5.7 copy-start
  329.7 5.2 copy-start.14
  329.8 20.9 %copy-start.2 = (bf16[1024,1024]{1,0:T(8,128)(2,1)S(1)}, bf16[1024,1024]{1,0:T(8,128)(2,1)}, u32[]{:S(2)}) copy-start(bf16[1024,1024]{1,0:T(8,128)(2,1)} %get-tuple-element.1319) | copy-start | bytes 6291460 | tf_op jit(solution)/shard_map/while
  335.0 14.9 %copy-start.9 = (bf16[1024,4,64]{0,2,1:T(8,128)(2,1)}, bf16[1024,4,64]{0,2,1:T(8,128)(2,1)S(1)}, u32[]{:S(2)}) copy-start(bf16[1024,4,64]{0,2,1:T(8,128)(2,1)S(1)} %fusion.161) | copy-start | bytes 1572868 | tf_op jit(solution)/shard_map/while
  338.0 11.8 %all-to-all-start.1 = ((bf16[4,256,256]{1,2,0:T(8,128)(2,1)}), bf16[4,256,256]{1,2,0:T(8,128)(2,1)S(1)}, u32[]{:S(2)}, u32[]{:S(2)}) async-start(bf16[4,256,256]{1,2,0:T(8,128)(2,1)} %copy.112), calls=%async_computation.1 | async-start | bytes 1048576 | tf_op jit(solution)/shard_map/while/body/eval_jaxpr/all_to_all | solution.py:191
  353.0 6.0 copy-start.18
  353.0 13.5 %slice-start.2 = ((s8[8388608]{0:T(1024)(128)(4,1)}), s8[4194304]{0:T(1024)(128)(4,1)S(1)}, s32[]{:S(2)}) async-start(s8[8388608]{0:T(1024)(128)(4,1)} %bitcast.305), calls=%async_computation.19 | async-start | bytes 8388608 | tf_op jit(solution)/shard_map/while
  359.0 10.3 copy-start.1
  359.0 7.5 slice-start.3
  378.8 16.4 %all-to-all-start.2 = ((bf16[256,4,256]{0,2,1:T(8,128)(2,1)}), bf16[256,4,256]{0,2,1:T(8,128)(2,1)S(1)}, u32[]{:S(2)}, u32[]{:S(2)}) async-start(bf16[256,4,256]{0,2,1:T(8,128)(2,1)} %bitcast.249), calls=%async_computation.2 | async-start | bytes 1048576 | tf_op jit(solution)/shard_map/while/body/eval_jaxpr/all_to_all | solution.py:231
  382.4 9.9 copy-start.12
  392.4 5.4 copy-start.10
  392.4 5.5 copy-start.15
  398.0 9.8 copy-start.8
  407.8 5.1 slice-start
  409.4 3.5 slice-start.1
  428.8 4.9 copy-start.19
  428.8 28.7 %all-to-all-start.3 = ((bf16[3,1024,256]{2,0,1:T(4,128)(2,1)}), bf16[3,1024,256]{2,0,1:T(4,128)(2,1)}, u32[]{:S(2)}, u32[]{:S(2)}) async-start(bf16[3,1024,256]{2,0,1:T(4,128)(2,1)} %pad_maximum_fusion.10), calls=%async_computation.3 | async-start | bytes 4194304 | tf_op jit(solution)/shard_map/while/body/eval_jaxpr/all_to_all | solution.py:242
  459.2 4.3 copy-start.4
  463.6 5.4 copy-start.16
  463.6 5.4 copy-start.17
  469.0 7.9 copy-start.22
  486.8 6.7 copy-start.24
  489.4 28.5 %all-to-all-start = ((bf16[3,256,1024]{1,0,2:T(4,128)(2,1)}), bf16[3,256,1024]{1,0,2:T(4,128)(2,1)S(1)}, u32[]{:S(2)}, u32[]{:S(2)}) async-start(bf16[3,256,1024]{1,0,2:T(4,128)(2,1)} %copy.110), calls=%async_computation | async-start | bytes 4194304 | tf_op jit(solution)/shard_map/while/body/eval_jaxpr/all_to_all | solution.py:180
  520.2 3.6 copy-start.5
  520.6 3.3 copy-start.7
  523.9 5.7 copy-start
  535.7 5.2 copy-start.14
  535.7 20.2 %copy-start.2 = (bf16[1024,1024]{1,0:T(8,128)(2,1)S(1)}, bf16[1024,1024]{1,0:T(8,128)(2,1)}, u32[]{:S(2)}) copy-start(bf16[1024,1024]{1,0:T(8,128)(2,1)} %get-tuple-element.1319) | copy-start | bytes 6291460 | tf_op jit(solution)/shard_map/while
  540.9 14.2 %copy-start.9 = (bf16[1024,4,64]{0,2,1:T(8,128)(2,1)}, bf16[1024,4,64]{0,2,1:T(8,128)(2,1)S(1)}, u32[]{:S(2)}) copy-start(bf16[1024,4,64]{0,2,1:T(8,128)(2,1)S(1)} %fusion.161) | copy-start | bytes 1572868 | tf_op jit(solution)/shard_map/while
  544.0 11.1 %all-to-all-start.1 = ((bf16[4,256,256]{1,2,0:T(8,128)(2,1)}), bf16[4,256,256]{1,2,0:T(8,128)(2,1)S(1)}, u32[]{:S(2)}, u32[]{:S(2)}) async-start(bf16[4,256,256]{1,2,0:T(8,128)(2,1)} %copy.112), calls=%async_computation.1 | async-start | bytes 1048576 | tf_op jit(solution)/shard_map/while/body/eval_jaxpr/all_to_all | solution.py:191
  558.2 6.0 copy-start.18
  558.2 13.5 %slice-start.2 = ((s8[8388608]{0:T(1024)(128)(4,1)}), s8[4194304]{0:T(1024)(128)(4,1)S(1)}, s32[]{:S(2)}) async-start(s8[8388608]{0:T(1024)(128)(4,1)} %bitcast.305), calls=%async_computation.19 | async-start | bytes 8388608 | tf_op jit(solution)/shard_map/while
  564.2 10.3 copy-start.1
  564.2 7.5 slice-start.3
  584.1 23.5 %all-to-all-start.2 = ((bf16[256,4,256]{0,2,1:T(8,128)(2,1)}), bf16[256,4,256]{0,2,1:T(8,128)(2,1)S(1)}, u32[]{:S(2)}, u32[]{:S(2)}) async-start(bf16[256,4,256]{0,2,1:T(8,128)(2,1)} %bitcast.249), calls=%async_computation.2 | async-start | bytes 1048576 | tf_op jit(solution)/shard_map/while/body/eval_jaxpr/all_to_all | solution.py:231
  587.8 14.8 %copy-start.12 = (bf16[4,256,256]{1,2,0:T(8,128)(2,1)S(1)}, bf16[4,256,256]{1,2,0:T(8,128)(2,1)}, u32[]{:S(2)}) copy-start(bf16[4,256,256]{1,2,0:T(8,128)(2,1)} %copy-done.11) | copy-start | bytes 1572868 | tf_op jit(solution)/shard_map/while
  602.5 7.6 copy-start.10
  602.5 7.8 copy-start.15
  610.4 9.8 copy-start.8
  620.2 5.1 slice-start
  621.8 3.5 slice-start.1
  641.2 5.1 copy-start.19
  641.2 28.6 %all-to-all-start.3 = ((bf16[3,1024,256]{2,0,1:T(4,128)(2,1)}), bf16[3,1024,256]{2,0,1:T(4,128)(2,1)}, u32[]{:S(2)}, u32[]{:S(2)}) async-start(bf16[3,1024,256]{2,0,1:T(4,128)(2,1)} %pad_maximum_fusion.10), calls=%async_computation.3 | async-start | bytes 4194304 | tf_op jit(solution)/shard_map/while/body/eval_jaxpr/all_to_all | solution.py:242
  671.6 4.3 copy-start.4
  675.9 5.4 copy-start.16
  676.0 5.4 copy-start.17
  681.3 10.8 copy-start.22
  700.8 104.3 %reduce-scatter.5.cloned.1.call-start = ((), (), s32[]{:S(2)}) async-start(), calls=%async_computation.12 | async-start | bytes 7077888 | tf_op jit(solution)/shard_map/reduce_scatter | solution.py:322
  709.2 186.2 %reduce-scatter.11.cloned.1.call-start = ((), (), s32[]{:S(2)}) async-start(), calls=%async_computation.15 | async-start | bytes 9437184 | tf_op jit(solution)/shard_map/reduce_scatter | solution.py:352
  718.5 267.2 %reduce-scatter.9.cloned.1.call-start = ((), (), s32[]{:S(2)}) async-start(), calls=%async_computation.14 | async-start | bytes 9437184 | tf_op jit(solution)/shard_map/reduce_scatter | solution.py:343
  727.7 258.1 %copy-start.27 = (u32[32]{0:T(128)S(1)}, u32[32]{0:T(128)}, u32[]{:S(2)}) copy-start(u32[32]{0:T(128)} %constant.160) | copy-start | bytes 388
  727.7 347.5 %all-reduce.15.cloned.1.call-start = ((), (), s32[]{:S(2)}) async-start(), calls=%async_computation.16 | async-start | bytes 6291456 | tf_op jit(solution)/shard_map/psum | solution.py:374
  1075.2 5.6 copy-start.20
  1075.2 6.9 copy-start.21
  (14 other events, 24.3 us)
Sparse Core Ops, SparseCore 0:
  9.6 31.8 all-gather.16
  43.2 64.2 all-gather.14
  109.1 80.6 all-gather.18
  191.3 80.5 all-gather.20
  701.0 33.4 reduce-scatter.6
  736.6 68.4 reduce-scatter.4
  807.4 87.9 reduce-scatter.10
  897.7 87.9 reduce-scatter.8
  989.0 86.1 all-reduce.14
where the time goes:
time: 1090 us
  waiting for transfers between devices  547 us (50%)
  matrix products  196 us (18%)
  blocking collectives  139 us (13%)
  other arithmetic  86.6 us (8%)
  local copies, waits for them, and re-layouts  65.6 us (6%)
  starting transfers between devices  33.5 us (3%)
  between operations  16.3 us (1%)
    reduce_scatter x1, waiting for transfers between devices, body(): lax.psum_scatter(weight_cotangent_bundle[11].astype(jnp.bfloat16), 'fsdp'...  90.3 us
    reduce_scatter x1, waiting for transfers between devices, body(): lax.psum_scatter(weight_cotangent_bundle[9].astype(jnp.bfloat16), 'fsdp',...  90.3 us
    all_gather x1, waiting for transfers between devices, body(): lax.all_gather(down_weight, 'fsdp', axis=0, tiled=True)  82.1 us
    all_gather x1, waiting for transfers between devices, body(): lax.all_gather(up_weight, 'fsdp', axis=0, tiled=True)  74.3 us
    reduce_scatter x1, waiting for transfers between devices, body(): lax.psum_scatter(weight_cotangent_bundle[2].astype(jnp.bfloat16), 'fsdp',...  70.6 us
    all_to_all x2, waiting for transfers between devices, one_image(): lax.all_to_all(jnp.stack([queries, key_rows, value_rows]), 'seq', split_a...  47.2 us
    psum x1, waiting for transfers between devices, body(): lax.psum(shards[2].astype(jnp.bfloat16), 'seq').astype(jnp.float32)  44.6 us
    unnamed x1, blocking collectives  26.1 us
  transfers between devices with their start and end apart: 17, of which 13 were waited for; matrix products, arithmetic and copies ran while one was open for 9% of the time, Pallas kernels for 0%

commit v1 on v0

v1 whole, which is shorter than its diff:
```python
import functools
import math

import jax
import jax.numpy as jnp
from jax import lax
from jax.experimental import pallas as pl
from jax.experimental.pallas import tpu as pltpu
from jax.sharding import PartitionSpec as P

HEAD_DIM = 64
EPSILON = 1e-06
NEG_LARGE = -1e30

MESH = pl.DeviceIdType.MESH
DMA = pltpu.SemaphoreType.DMA
ANY = pl.BlockSpec(memory_space=pl.ANY)
VM = pl.BlockSpec(memory_space=pltpu.VMEM)


def remote(src, dst, ssem, rsem, dev):
    return pltpu.make_async_remote_copy(
        src_ref=src, dst_ref=dst, send_sem=ssem, recv_sem=rsem, device_id=dev, device_id_type=MESH
    )


class Place:
    def __init__(self, S, F):
        self.S, self.F, self.Z = S, F, F // 2
        self.bits = [1 << b for b in range(S.bit_length() - 1)]
        self.nbits = len(self.bits)
        self.order = [self.bits, self.bits[1:] + self.bits[:1]]
        self.s = lax.axis_index("seq")
        self.f = lax.axis_index("fsdp")
        self.z, self.c = self.f // 2, lax.rem(self.f, 2)
        self.mate = (self.s, self.f ^ 1)

    def at(self, zz):
        return (self.s, zz * 2 + self.c)

    def meet(self, fsdp=True, seq=True):
        bar = pltpu.get_barrier_semaphore()
        count = 0
        if fsdp:
            for k in range(1, self.F):
                pl.semaphore_signal(bar, inc=1, device_id=(self.s, lax.rem(self.f + k, self.F)), device_id_type=MESH)
            count += self.F - 1
        if seq:
            for k in range(1, self.S):
                pl.semaphore_signal(bar, inc=1, device_id=(self.s ^ k, self.f), device_id_type=MESH)
            count += self.S - 1
        pl.semaphore_wait(bar, count)


def span(bits):
    out = [0]
    for b in bits:
        out = out + [m | b for m in out]
    return out


def ds(start, size):
    return pl.ds(pl.multiple_of(start, size), size)


class Gather:
    LAG = 8

    def __init__(self, g, NB, own, full, bounce, sems):
        self.g, self.NB, self.own, self.full, self.bounce = g, NB, own, full, bounce
        self.zs, self.zr, self.xs, self.xr, self.cs, self.cr, self.ls = sems
        self.R, self.D = full.shape[2:]
        self.C = self.D // g.S
        self.nitems = (g.Z - 1) * NB * 2
        self.steps = self.nitems + self.LAG * g.nbits

    @staticmethod
    def scratch(S, F, NB, R, D, dtype=jnp.bfloat16):
        Z, nb = F // 2, S.bit_length() - 1
        return [pltpu.VMEM((NB, R, D), dtype), DMA((2, NB, Z)), DMA((NB, Z)), DMA((NB, Z, 2, nb)), DMA((NB, Z, 2, nb)),
                DMA((NB, Z)), DMA((NB, Z)), DMA((NB,))]

    def cols(self, q):
        return ds(q * self.C, self.C)

    def half(self, p):
        return pl.ds(p * (self.R // 2), self.R // 2)

    def zcopy(self, src, b, zz, way, to):
        g = self.g
        return remote(src, self.full.at[zz * 2 + g.c, b, :, self.cols(g.s)], self.zs.at[way, b, zz], self.zr.at[b, zz], g.at(to))

    def zfull(self, b, zz):
        return self.full.at[zz * 2 + self.g.c, b, :, self.cols(self.g.s)]

    def mate_copy(self, src, b, zz, core):
        return remote(src, self.full.at[zz * 2 + core, b], self.cs.at[b, zz], self.cr.at[b, zz], self.g.mate)

    def start(self):
        g = self.g
        for b in range(self.NB):
            piece = self.own(b, self.cols(g.s))
            @pl.when(g.z < g.Z - 1)
            def _():
                self.zcopy(piece, b, g.z, 0, g.z + 1).start()
            @pl.when(g.z > 0)
            def _():
                self.zcopy(piece, b, g.z, 1, g.z - 1).start()
        for b in range(self.NB):
            pltpu.make_async_copy(self.own(b, slice(None)), self.bounce.at[b], self.ls.at[b]).start()
        for b in range(self.NB):
            self.mate_copy(self.own(b, slice(None)), b, g.z, g.c).start()
        for b in range(self.NB):
            pltpu.make_async_copy(self.own(b, slice(None)), self.bounce.at[b], self.ls.at[b]).wait()
            pltpu.make_async_copy(self.bounce.at[b], self.full.at[g.f, b], self.ls.at[b]).start()

    def xcopies(self, b, zz, p, j):
        g = self.g
        f = zz * 2 + g.c
        to = (g.s ^ g.order[p][j], g.f)
        out = []
        for m in span(g.order[p][:j]):
            ref = self.full.at[f, b, self.half(p), self.cols(g.s ^ m)]
            out.append(remote(ref, ref, self.xs.at[b, zz, p, j], self.xr.at[b, zz, p, j], to))
        return out

    def xall(self, b, zz, p, j):
        g = self.g
        ref = self.full.at[zz * 2 + g.c, b, self.half(p), pl.ds(0, self.C << j)]
        return remote(ref, ref, self.xs.at[b, zz, p, j], self.xr.at[b, zz, p, j], (g.s ^ g.order[p][j], g.f))

    def item(self, t):
        g = self.g
        h = 1 + t // (2 * self.NB)
        r = lax.rem(t, 2 * self.NB)
        b, below = r // 2, lax.rem(r, 2) == 0
        zz = jnp.where(below, g.z - h, g.z + h)
        ok = (t >= 0) & (t < self.nitems) & (zz >= 0) & (zz < g.Z)
        nxt = jnp.where(below, g.z + 1, g.z - 1)
        more = (nxt >= 0) & (nxt < g.Z)
        way = jnp.where(below, 0, 1)
        return b, zz, ok, nxt, more, way

    def step(self, t):
        g = self.g
        for j in reversed(range(g.nbits + 1)):
            b, zz, ok, nxt, more, way = self.item(t - self.LAG * j)
            @pl.when(ok)
            def _(j=j, b=b, zz=zz, nxt=nxt, more=more, way=way):
                if j == 0:
                    self.zcopy(self.zfull(b, zz), b, zz, 0, g.z).wait_recv()
                    @pl.when(more)
                    def _():
                        self.zcopy(self.zfull(b, zz), b, zz, way, nxt).start()
                else:
                    for p in range(2):
                        self.xall(b, zz, p, j - 1).wait_recv()
                if j < g.nbits:
                    for p in range(2):
                        for cp in self.xcopies(b, zz, p, j):
                            cp.start()
                else:
                    self.mate_copy(self.full.at[zz * 2 + g.c, b], b, zz, g.c).start()

    def run(self, lo, hi):
        @pl.loop(lo, hi)
        def _(t):
            self.step(t)

    def finish(self):
        g = self.g
        @pl.loop(0, self.NB)
        def _(b):
            blk = self.full.at[g.f, b]
            pltpu.make_async_copy(self.bounce.at[b], blk, self.ls.at[b]).wait()
            cp = self.mate_copy(blk, b, g.z, 1 - g.c)
            cp.wait_send()
            cp.wait_recv()
            @pl.when(g.z < g.Z - 1)
            def _():
                self.zcopy(self.zfull(b, g.z), b, g.z, 0, g.z + 1).wait_send()
            @pl.when(g.z > 0)
            def _():
                self.zcopy(self.zfull(b, g.z), b, g.z, 1, g.z - 1).wait_send()
        @pl.loop(0, self.nitems)
        def _(t):
            b, zz, ok, nxt, more, way = self.item(t)
            @pl.when(ok)
            def _():
                @pl.when(more)
                def _():
                    self.zcopy(self.zfull(b, zz), b, zz, way, nxt).wait_send()
                for p in range(2):
                    for j in range(g.nbits):
                        self.xall(b, zz, p, j).wait_send()
                cp = self.mate_copy(self.full.at[zz * 2 + g.c, b], b, zz, 1 - g.c)
                cp.wait_send()
                cp.wait_recv()


class Scatter:
    LAG = 4

    def __init__(self, g, NB, part, out, bufs, sems):
        self.g, self.NB, self.part, self.out = g, NB, part, out
        self.cs_buf, self.r0, self.xb, self.zb, self.fq = bufs
        self.own, self.c_s, self.c_r, self.x_s, self.x_r, self.z_s, self.z_r, self.a_s, self.a_r, self.o = sems
        self.R, self.D = part.shape[2:]
        self.C = self.D // g.S
        self.nitems = NB * g.Z
        self.tail = g.nbits * self.LAG
        self.steps = self.nitems + self.tail + 1 + (g.nbits + 2) * self.LAG * 2

    @staticmethod
    def scratch(S, F, NB, R, D, dtype=jnp.bfloat16):
        Z, nb = F // 2, S.bit_length() - 1
        C = D // S
        n = NB * Z
        return [
            pltpu.VMEM((n, R, D), dtype), pltpu.VMEM((n, R, D), dtype), pltpu.VMEM((n, 2, R // 2, D - C), dtype),
            pltpu.VMEM((NB, Z, R, C), dtype), pltpu.VMEM((NB, R, C), dtype),
            DMA((n,)), DMA((n,)), DMA((n,)), DMA((n, 2, nb)), DMA((n, 2, nb)),
            DMA((NB, Z)), DMA((NB, Z)), DMA((NB, 2, nb)), DMA((NB, 2, nb)), DMA((NB,)),
        ]

    def where(self, t):
        g = self.g
        b, r = t // g.Z, lax.rem(t, g.Z)
        zz = jnp.where(lax.rem(r, 2) == 0, r // 2, g.Z - 1 - r // 2)
        return b, zz

    def cols(self, q):
        return ds(q * self.C, self.C)

    def half(self, p):
        return pl.ds(p * (self.R // 2), self.R // 2)

    def load(self, t):
        b, zz = self.where(t)
        return pltpu.make_async_copy(self.part.at[zz * 2 + self.g.c, b], self.cs_buf.at[t], self.own.at[t])

    def swap(self, t):
        b, zz = self.where(t)
        return remote(self.part.at[zz * 2 + 1 - self.g.c, b], self.r0.at[t], self.c_s.at[t], self.c_r.at[t], self.g.mate)

    def offset(self, j):
        D, C, S = self.D, self.C, self.g.S
        return sum((S >> (i + 1)) * C for i in range(j))

    def halving(self, t, p, j):
        g = self.g
        order = g.order[p]
        mask = sum(order[: j + 1])
        base = (g.s ^ order[j]) & mask
        to = (g.s ^ order[j], g.f)
        out = []
        for i, m in enumerate(span(order[j + 1 :])):
            src = self.cs_buf.at[t, self.half(p), self.cols(base | m)]
            dst = self.xb.at[t, p, :, pl.ds(self.offset(j) + i * self.C, self.C)]
            out.append(remote(src, dst, self.x_s.at[t, p, j], self.x_r.at[t, p, j], to))
        return out

    def halved(self, t, p, j):
        g = self.g
        width = (g.S >> (j + 1)) * self.C
        ref = self.xb.at[t, p, :, pl.ds(self.offset(j), width)]
        return remote(ref, ref, self.x_s.at[t, p, j], self.x_r.at[t, p, j], (g.s ^ g.order[p][j], g.f))

    def add_halves(self, t, p, j):
        g = self.g
        order = g.order[p]
        mask = sum(order[: j + 1])
        base = g.s & mask
        for i, m in enumerate(span(order[j + 1 :])):
            q = self.cols(base | m)
            got = self.xb[t, p, :, pl.ds(self.offset(j) + i * self.C, self.C)]
            self.cs_buf[t, self.half(p), q] = self.cs_buf[t, self.half(p), q] + got

    def piece(self, t, b, zz):
        g = self.g
        return remote(self.cs_buf.at[t, :, self.cols(g.s)], self.zb.at[b, g.z], self.z_s.at[b, zz], self.z_r.at[b, g.z], g.at(zz))

    def arrived(self, b, zz):
        g = self.g
        return remote(self.zb.at[b, zz], self.zb.at[b, zz], self.z_s.at[b, zz], self.z_r.at[b, zz], g.at(zz))

    def doubling(self, b, p, j):
        g = self.g
        to = (g.s ^ g.order[p][j], g.f)
        out = []
        for m in span(g.order[p][:j]):
            dst = self.out.at[b, self.half(p), self.cols(g.s ^ m)]
            src = self.fq.at[b, self.half(p)] if m == 0 else dst
            out.append(remote(src, dst, self.a_s.at[b, p, j], self.a_r.at[b, p, j], to))
        return out

    def doubled(self, b, p, j):
        g = self.g
        ref = self.out.at[b, self.half(p), pl.ds(0, self.C << j)]
        return remote(ref, ref, self.a_s.at[b, p, j], self.a_r.at[b, p, j], (g.s ^ g.order[p][j], g.f))

    def start(self):
        @pl.loop(0, self.nitems)
        def _(t):
            self.swap(t).start()
            self.load(t).start()

    def step(self, t):
        g = self.g
        last = g.Z - 1
        for j in reversed(range(g.nbits + 1)):
            u = t - self.tail - self.LAG * 2 * (1 + j) - last
            @pl.when((u >= 0) & (u < self.nitems) & (lax.rem(u, g.Z) == 0))
            def _(j=j, u=u):
                b = u // g.Z
                if j == 0:
                    r = jnp.where(g.z < (g.Z + 1) // 2, 2 * g.z, 2 * (g.Z - 1 - g.z) + 1)
                    total = self.cs_buf[b * g.Z + r, :, self.cols(g.s)].astype(jnp.float32)
                    for k in range(1, g.Z):
                        zz = lax.rem(g.z + k, g.Z)
                        self.arrived(b, zz).wait_recv()
                        total = total + self.zb[b, zz].astype(jnp.float32)
                    self.fq[b] = total.astype(self.fq.dtype)
                    pltpu.make_async_copy(self.fq.at[b], self.out.at[b, :, self.cols(g.s)], self.o.at[b]).start()
                else:
                    for p in range(2):
                        self.doubled(b, p, j - 1).wait_recv()
                if j < g.nbits:
                    for p in range(2):
                        for cp in self.doubling(b, p, j):
                            cp.start()
        for j in reversed(range(g.nbits + 1)):
            u = t - self.LAG * j
            @pl.when((u >= 0) & (u < self.nitems))
            def _(j=j, u=u):
                b, zz = self.where(u)
                if j == 0:
                    self.load(u).wait()
                    self.swap(u).wait_recv()
                    self.cs_buf[u] = self.cs_buf[u] + self.r0[u]
                else:
                    for p in range(2):
                        self.halved(u, p, j - 1).wait_recv()
                        self.add_halves(u, p, j - 1)
                if j < g.nbits:
                    for p in range(2):
                        for cp in self.halving(u, p, j):
                            cp.start()
                else:
                    @pl.when(zz != g.z)
                    def _():
                        self.piece(u, b, zz).start()

    def run(self, lo, hi):
        @pl.loop(lo, hi)
        def _(t):
            self.step(t)

    def finish(self):
        g = self.g
        @pl.loop(0, self.nitems)
        def _(t):
            b, zz = self.where(t)
            self.swap(t).wait_send()
            for p in range(2):
                for j in range(g.nbits):
                    self.halved(t, p, j).wait_send()
            @pl.when(zz != g.z)
            def _():
                self.piece(t, b, zz).wait_send()
        @pl.loop(0, self.NB)
        def _(b):
            pltpu.make_async_copy(self.fq.at[b], self.out.at[b, :, self.cols(g.s)], self.o.at[b]).wait()
            for p in range(2):
                for j in range(g.nbits):
                    self.doubled(b, p, j).wait_send()


class VecGather:
    def __init__(self, g, vec, out, sems):
        self.g, self.vec, self.out = g, vec, out
        self.vs, self.vr, self.vl = sems

    @staticmethod
    def scratch(F):
        return [DMA((F - 1,)), DMA((F - 1,)), DMA((1,))]

    def copy(self, k):
        g = self.g
        return remote(self.vec, self.out.at[g.f], self.vs.at[k - 1], self.vr.at[k - 1], (g.s, lax.rem(g.f + k, g.F)))

    def start(self):
        for k in range(1, self.g.F):
            self.copy(k).start()
        pltpu.make_async_copy(self.vec, self.out.at[self.g.f], self.vl.at[0]).start()

    def finish(self):
        g = self.g
        pltpu.make_async_copy(self.vec, self.out.at[g.f], self.vl.at[0]).wait()
        for k in range(1, g.F):
            self.copy(k).wait_send()
            src = lax.rem(g.f + g.F - k, g.F)
            remote(self.vec, self.out.at[src], self.vs.at[k - 1], self.vr.at[k - 1], (g.s, src)).wait_recv()


class VecSum:
    def __init__(self, g, vec, out, bufs, sems):
        self.g, self.vec, self.out = g, vec, out
        self.fb, self.mid, self.sb = bufs
        self.vs, self.vr, self.ws, self.wr = sems

    @staticmethod
    def scratch(S, F, N, L):
        return [pltpu.VMEM((F, N, L), jnp.float32), pltpu.VMEM((N, L), jnp.float32), pltpu.VMEM((S, N, L), jnp.float32),
                DMA((F - 1,)), DMA((F - 1,)), DMA((S - 1,)), DMA((S - 1,))]

    def one(self, k):
        g = self.g
        to = lax.rem(g.f + k, g.F)
        return remote(self.vec.at[to], self.fb.at[g.f], self.vs.at[k - 1], self.vr.at[k - 1], (g.s, to))

    def two(self, k):
        g = self.g
        return remote(self.mid, self.sb.at[g.s], self.ws.at[k - 1], self.wr.at[k - 1], (g.s ^ k, g.f))

    def start(self):
        for k in range(1, self.g.F):
            self.one(k).start()

    def middle(self):
        g = self.g
        total = self.vec[g.f]
        for k in range(1, g.F):
            src = lax.rem(g.f + g.F - k, g.F)
            remote(self.fb.at[src], self.fb.at[src], self.vs.at[k - 1], self.vr.at[k - 1], (g.s, src)).wait_recv()
            total = total + self.fb[src]
        self.mid[...] = total
        for k in range(1, g.S):
            self.two(k).start()

    def finish(self):
        g = self.g
        total = self.mid[...]
        for k in range(1, g.S):
            src = g.s ^ k
            remote(self.mid, self.sb.at[src], self.ws.at[k - 1], self.wr.at[k - 1], (src, g.f)).wait_recv()
            total = total + self.sb[src]
        self.out[...] = total
        for k in range(1, g.F):
            self.one(k).wait_send()
        for k in range(1, g.S):
            self.two(k).wait_send()


PARAMS = dict(has_side_effects=True, vmem_limit_bytes=60 * 2**20)


def gather_call(S, F, cid, D, shards, vec, blocks):
    NB = len(blocks)
    R = shards[0].shape[0]

    def kernel(*refs):
        ins, vec_in = refs[: len(shards)], refs[len(shards)]
        full, vec_out = refs[len(shards) + 1 : len(shards) + 3]
        rest = refs[len(shards) + 3 :]
        g = Place(S, F)

        def own(b, cols):
            w, r0, c0 = blocks[b]
            if isinstance(cols, slice):
                return ins[w].at[pl.ds(r0, R), pl.ds(c0, D)]
            return ins[w].at[pl.ds(r0, R), pl.ds(pl.multiple_of(c0 + cols.start, cols.size), cols.size)]

        g.meet()
        vg = VecGather(g, vec_in, vec_out, rest[:3])
        ga = Gather(g, NB, own, full, rest[3], rest[4:])
        vg.start()
        ga.start()
        ga.run(0, ga.steps)
        ga.finish()
        vg.finish()

    return pl.pallas_call(
        kernel,
        out_shape=[jax.ShapeDtypeStruct((F, NB, R, D), jnp.bfloat16), jax.ShapeDtypeStruct((F,) + vec.shape, vec.dtype)],
        in_specs=[ANY] * (len(shards) + 1),
        out_specs=[ANY] * 2,
        scratch_shapes=VecGather.scratch(F) + Gather.scratch(S, F, NB, R, D),
        compiler_params=pltpu.CompilerParams(collective_id=cid, **PARAMS),
        name="weights_in",
    )(*shards, vec)


def scatter_call(S, F, cid, part, vec):
    _, NB, R, D = part.shape
    N, L = vec.shape[1:]

    def kernel(part, vec, out, vec_out, *rest):
        g = Place(S, F)
        g.meet()
        vsum = VecSum(g, vec, vec_out, rest[:3], rest[3:7])
        sc = Scatter(g, NB, part, out, rest[7:12], rest[12:])
        vsum.start()
        sc.start()
        vsum.middle()
        sc.run(0, sc.steps)
        sc.finish()
        vsum.finish()

    return pl.pallas_call(
        kernel,
        out_shape=[jax.ShapeDtypeStruct((NB, R, D), jnp.bfloat16), jax.ShapeDtypeStruct((N, L), jnp.float32)],
        in_specs=[ANY, VM],
        out_specs=[ANY, VM],
        scratch_shapes=VecSum.scratch(S, F, N, L) + Scatter.scratch(S, F, NB, R, D),
        compiler_params=pltpu.CompilerParams(collective_id=cid, **PARAMS),
        name="gradients_out",
    )(part, vec)


def fp32(x):
    return x.astype(jnp.float32)


def dot(a, b, dims=((1,), (0,))):
    return lax.dot_general(a, b, (dims, ((), ())), preferred_element_type=jnp.float32)


NT = ((1,), (1,))
TN = ((0,), (0,))


def mean_rows(x):
    return jnp.mean(x, axis=-1, keepdims=True)


def qkv_kernel(S, F, img, par, eb, wts, x1, heads, wv, stage, wsem, ssem, rsem):
    g = Place(S, F)
    g.meet(fsdp=False)
    slots, T, D = img.shape
    W = D // S
    loads = [pltpu.make_async_copy(wts.at[:, j], wv.at[j], wsem.at[j]) for j in range(3)]
    for cp in loads:
        cp.start()
    gain, shift = par[0:1], par[1:2]
    rows = min(128, T)

    @pl.loop(0, slots * T // rows)
    def _(r):
        i, t = r // (T // rows), lax.rem(r, T // rows)
        x = fp32(img[i, pl.ds(t * rows, rows)])
        x = x - mean_rows(x)
        inv = lax.rsqrt(mean_rows(x * x) + EPSILON)
        x1[ds(r * rows, rows)] = (x * inv * gain + shift).astype(x1.dtype)

    for cp in loads:
        cp.wait()

    def copy(k, j):
        src = stage.at[k, j]
        dst = heads.at[j, :, ds(g.s * T, T)]
        return remote(src, dst, ssem.at[k, j], rsem.at[k, j], (g.s ^ k, g.f))

    def local(j):
        return pltpu.make_async_copy(stage.at[0, j], heads.at[j, :, ds(g.s * T, T)], ssem.at[0, j])

    @pl.loop(0, S * 3)
    def _(n):
        k = lax.rem(1 + n // 3, S)
        j = lax.rem(n, 3)
        cols = ds((g.s ^ k) * W, W)
        w = wv[j, :, :, cols].reshape(D, W)
        out = dot(x1[...], w) + eb[j, :, cols]
        stage[k, j] = out.astype(stage.dtype).reshape(slots, T, W)

        @pl.when(k != 0)
        def _():
            copy(k, j).start()

        @pl.when(k == 0)
        def _():
            local(j).start()

    for j in range(3):
        local(j).wait()
        for k in range(1, S):
            cp = copy(k, j)
            cp.wait_send()
            remote(stage.at[k, j], heads.at[j, :, ds((g.s ^ k) * T, T)], ssem.at[k, j], rsem.at[k, j], (g.s ^ k, g.f)).wait_recv()


def qkv_call(S, F, cid, img, par, eb, wts):
    slots, T, D = img.shape
    _, _, R, _ = wts.shape
    W = D // S
    bf = jnp.bfloat16
    return pl.pallas_call(
        functools.partial(qkv_kernel, S, F),
        out_shape=[jax.ShapeDtypeStruct((slots * T, D), bf), jax.ShapeDtypeStruct((3, slots, S * T, W), bf)],
        in_specs=[VM, VM, VM, ANY],
        out_specs=[VM, ANY],
        scratch_shapes=[pltpu.VMEM((3, F, R, D), bf), pltpu.VMEM((S, 3, slots, T, W), bf), DMA((3,)), DMA((S, 3)), DMA((S, 3))],
        compiler_params=pltpu.CompilerParams(collective_id=cid, **PARAMS),
        name="project",
    )(img, par, eb, wts)


def head_lanes(rows, hh):
    lane = lax.broadcasted_iota(jnp.int32, (rows, 128), 1)
    mine = (lane >= hh * HEAD_DIM) & (lane < (hh + 1) * HEAD_DIM)
    spare = lane == (1 - hh) * HEAD_DIM
    return mine, spare


def masked_keys(k, length, hh):
    N = k.shape[0]
    mine, spare = head_lanes(N, hh)
    late = lax.broadcasted_iota(jnp.int32, (N, 128), 0) >= length
    return jnp.where(mine, fp32(k), jnp.where(spare & late, NEG_LARGE, 0.0)).astype(jnp.bfloat16)


def scaled_queries(q, hh):
    mine, spare = head_lanes(q.shape[0], hh)
    return jnp.where(mine, fp32(q) * HEAD_DIM ** (-0.5), jnp.where(spare, 1.0, 0.0)).astype(jnp.bfloat16)


def attend_kernel(S, F, QB, lengths, q, k, v, out_t, lse, att, kh, vt, o_t, o_buf, ssem, rsem):
    g = Place(S, F)
    i, hp = pl.program_id(0), pl.program_id(1)
    slots, pairs = pl.num_programs(0), pl.num_programs(1)
    N = q.shape[2]
    T = N // S
    W = att.shape[2] // S
    e = i * pairs + hp

    @pl.when(e == 0)
    def _():
        g.meet(fsdp=False)

    length = lengths[i]
    vt[...] = v[0, 0].T
    for hh in range(2):
        kh[hh] = masked_keys(k[0, 0], length, hh)

    @pl.loop(0, N // QB)
    def _(b):
        cols = ds(b * QB, QB)
        qb = q[0, 0, cols]
        for hh in range(2):
            sc = dot(kh[hh], scaled_queries(qb, hh), NT)
            top = jnp.max(sc, axis=0, keepdims=True)
            ex = jnp.exp(sc - top)
            total = jnp.sum(ex, axis=0, keepdims=True)
            w = (ex * (1.0 / total)).astype(jnp.bfloat16)
            o = dot(vt[hh * HEAD_DIM : (hh + 1) * HEAD_DIM], w).astype(jnp.bfloat16)
            o_t[hh * HEAD_DIM : (hh + 1) * HEAD_DIM, cols] = o
            lse[0, 0, hh : hh + 1, cols] = top + jnp.log(total)

    out_t[0] = o_t[...]
    o_buf[e] = o_t[...].T

    def copy(e, i, hp, kk):
        dst = att.at[i, :, pl.ds(pl.multiple_of(g.s * W + hp * 128, 128), 128)]
        return remote(o_buf.at[e, ds((g.s ^ kk) * T, T)], dst, ssem.at[e, kk], rsem.at[e, kk], (g.s ^ kk, g.f))

    def local(e, i, hp):
        dst = att.at[i, :, pl.ds(pl.multiple_of(g.s * W + hp * 128, 128), 128)]
        return pltpu.make_async_copy(o_buf.at[e, ds(g.s * T, T)], dst, ssem.at[e, 0])

    for kk in range(1, S):
        copy(e, i, hp, kk).start()
    local(e, i, hp).start()

    @pl.when(e == slots * pairs - 1)
    def _():
        @pl.loop(0, slots * pairs)
        def _(e):
            i, hp = e // pairs, lax.rem(e, pairs)
            local(e, i, hp).wait()
            for kk in range(1, S):
                cp = copy(e, i, hp, kk)
                cp.wait_send()
                cp.wait_recv()


def attend_call(S, F, cid, lengths, heads):
    _, slots, N, W = heads.shape
    pairs, T, D = W // 128, N // S, W * S
    bf = jnp.bfloat16
    QB = min(256, N)
    part = lambda j: pl.BlockSpec((1, 1, N, 128), lambda i, h: (j, i, 0, h))
    return pl.pallas_call(
        functools.partial(attend_kernel, S, F, QB),
        grid=(slots, pairs),
        out_shape=[
            jax.ShapeDtypeStruct((slots, W, N), bf),
            jax.ShapeDtypeStruct((slots, pairs, 8, N), jnp.float32),
            jax.ShapeDtypeStruct((slots, T, D), bf),
        ],
        in_specs=[pl.BlockSpec(memory_space=pltpu.SMEM), part(0), part(1), part(2)],
        out_specs=[
            pl.BlockSpec((1, 128, N), lambda i, h: (i, h, 0)),
            pl.BlockSpec((1, 1, 8, N), lambda i, h: (i, h, 0, 0)),
            ANY,
        ],
        scratch_shapes=[
            pltpu.VMEM((2, N, 128), bf), pltpu.VMEM((128, N), bf), pltpu.VMEM((128, N), bf),
            pltpu.VMEM((slots * pairs, N, 128), bf), DMA((slots * pairs, S)), DMA((slots * pairs, S)),
        ],
        compiler_params=pltpu.CompilerParams(collective_id=cid, dimension_semantics=("arbitrary",) * 2, **PARAMS),
        name="attend",
    )(lengths, heads, heads, heads)


def middle_kernel(S, F, lengths, held, img, cot, att, par, ub, wx, wu, wd,
                  layer, rescot, vecs, ubg, part, cots,
                  mixed, normed, inv2, x2, x2t, dcot, down, cot2, dwu, dwd, dwx, stage, ssem, rsem, psem):
    g = Place(S, F)
    j = pl.program_id(0)
    slots, T, D = img.shape
    M = slots * T
    W = D // S
    R = wx.shape[2]
    H = wu.shape[3]
    rows = min(128, T)
    nrows = M // rows
    exit_bias, scale1, gain2, shift2 = par[4:5], par[5:6], par[6:7], par[7:8]
    down_bias, scale2 = par[12:13], par[13:14]
    per_block = D // H

    def place(r):
        return r // (T // rows), lax.rem(r, T // rows) * rows

    def mask(r):
        i, t = place(r)
        limit = jnp.where(i < held[g.f], lengths[i], 0)
        pos = lax.broadcasted_iota(jnp.int32, (rows, 1), 0) + (g.s * T + t)
        return jnp.where(pos < limit, 1.0, 0.0)

    def residual(r, sl):
        i, t = place(r)
        return fp32(img[i, pl.ds(t, rows)]) + scale1 * mixed[sl]

    def upstream(r):
        i, t = place(r)
        return mask(r) * fp32(cot[i, pl.ds(t, rows)])

    @pl.when(j == 0)
    def _():
        g.meet(fsdp=False)
        w = wx[...].reshape(D, D)
        mixed[...] = dot(att[...], w) + exit_bias

        @pl.loop(0, nrows)
        def _(r):
            sl = ds(r * rows, rows)
            res = residual(r, sl)
            res = res - mean_rows(res)
            inv = lax.rsqrt(mean_rows(res * res) + EPSILON)
            n = res * inv
            normed[sl] = n
            inv2[sl] = jnp.broadcast_to(inv, (rows, 128))
            x2[sl] = (n * gain2 + shift2).astype(x2.dtype)
            dcot[sl] = (upstream(r) * scale2).astype(dcot.dtype)

        x2t[...] = x2[...].T

    wu_j = wu[...].reshape(D, H)
    wd_j = wd[...].reshape(H, D)
    pre = dot(x2[...], wu_j) + ub[...]
    cumul = 0.5 * (1.0 + lax.erf(pre * (1.0 / math.sqrt(2.0))))
    density = jnp.exp(-0.5 * pre * pre) * (1.0 / math.sqrt(2.0 * math.pi))
    act = (pre * cumul).astype(jnp.bfloat16)
    slope = cumul + pre * density
    pre_cot = dot(dcot[...], wd_j, NT) * slope
    ubg[...] = jnp.sum(pre_cot, axis=0, keepdims=True)
    low = pre_cot.astype(jnp.bfloat16)
    slot = lax.rem(j, 2)

    def put_up(jj, sl):
        cols = pl.ds(pl.multiple_of(lax.rem(jj, per_block) * H, H), H)
        return pltpu.make_async_copy(dwu.at[sl], part.at[:, 4 + jj // per_block, :, cols], psem.at[sl])

    def put_down(jj, sl):
        return pltpu.make_async_copy(dwd.at[sl], part.at[jj, pl.ds(0, 4)], psem.at[2 + sl])

    @pl.when(j >= 2)
    def _():
        put_up(j - 2, slot).wait()
        put_down(j - 2, slot).wait()

    dwu[slot] = dot(x2t[...], low).astype(jnp.bfloat16).reshape(F, R, H)
    dwd[slot] = dot(act, dcot[...], TN).astype(jnp.bfloat16).reshape(4, R, D)
    put_up(j, slot).start()
    put_down(j, slot).start()
    dd = dot(act, wd_j)
    dc = dot(low, wu_j, NT)

    @pl.when(j == 0)
    def _():
        down[...] = dd
        cot2[...] = dc

    @pl.when(j > 0)
    def _():
        down[...] += dd
        cot2[...] += dc

    @pl.when(j == F - 1)
    def _():
        vecs[...] = jnp.zeros_like(vecs)

        @pl.loop(0, nrows)
        def _(r):
            sl = ds(r * rows, rows)
            m = mask(r)
            up = upstream(r)
            out = down[sl] + down_bias
            layer[sl] = (m * (residual(r, sl) + scale2 * out)).astype(layer.dtype)
            n = normed[sl]
            inv = inv2[sl][:, 0:1]
            c2 = cot2[sl]
            c = c2 * gain2
            rc = up + inv * (c - mean_rows(c) - n * mean_rows(c * n))
            rescot[sl] = rc
            mc = rc * scale1
            x2[sl] = mc.astype(x2.dtype)
            total = lambda v: jnp.sum(v, axis=0, keepdims=True)
            vecs[0:1] += total(up * out)
            vecs[1:2] += total(up * scale2)
            vecs[2:3] += total(c2 * n)
            vecs[3:4] += total(c2)
            vecs[4:5] += total(rc * mixed[sl])
            vecs[5:6] += total(mc)

        for k in list(range(1, S)) + [0]:
            peer = g.s ^ k
            stage[k] = dot(x2[...], wx_rows(wx, peer, W), NT).astype(jnp.bfloat16).reshape(slots, T, W)
            dst = cots.at[:, ds(g.s * T, T)]
            if k:
                remote(stage.at[k], dst, ssem.at[k], rsem.at[k], (peer, g.f)).start()
            else:
                pltpu.make_async_copy(stage.at[0], dst, ssem.at[0]).start()
        dwx[...] = dot(att[...], x2[...], TN).astype(jnp.bfloat16).reshape(F, R, D)
        put_x = pltpu.make_async_copy(dwx, part.at[:, 8], psem.at[4])
        put_x.start()
        for jj in (F - 2, F - 1):
            put_up(jj, jj % 2).wait()
            put_down(jj, jj % 2).wait()
        put_x.wait()
        pltpu.make_async_copy(stage.at[0], cots.at[:, ds(g.s * T, T)], ssem.at[0]).wait()
        for k in range(1, S):
            cp = remote(stage.at[k], cots.at[:, ds((g.s ^ k) * T, T)], ssem.at[k], rsem.at[k], (g.s ^ k, g.f))
            cp.wait_send()
            cp.wait_recv()


def wx_rows(wx, peer, W):
    F, _, R, D = wx.shape
    n = W // R
    return wx[pl.ds(peer * n, n), 0].reshape(W, D)


def middle_call(S, F, cid, lengths, held, img, cot, att, par, ub, wts):
    slots, T, D = img.shape
    M = slots * T
    _, NB, R, _ = wts.shape
    FF = ub.shape[1]
    H = FF // F
    W = D // S
    per = D // H
    bf, fl = jnp.bfloat16, jnp.float32
    SM = pl.BlockSpec(memory_space=pltpu.SMEM)
    return pl.pallas_call(
        functools.partial(middle_kernel, S, F),
        grid=(F,),
        out_shape=[
            jax.ShapeDtypeStruct((M, D), bf), jax.ShapeDtypeStruct((M, D), fl), jax.ShapeDtypeStruct((8, D), fl),
            jax.ShapeDtypeStruct((1, FF), fl), jax.ShapeDtypeStruct((F, NB, R, D), bf),
            jax.ShapeDtypeStruct((slots, S * T, W), bf),
        ],
        in_specs=[SM, SM, VM, VM, VM, VM, pl.BlockSpec((1, H), lambda j: (0, j)),
                  pl.BlockSpec((F, 1, R, D), lambda j: (0, 8, 0, 0)),
                  pl.BlockSpec((F, 1, R, H), lambda j: (0, 4 + j // per, 0, lax.rem(j, per))),
                  pl.BlockSpec((1, 4, R, D), lambda j: (j, 0, 0, 0))],
        out_specs=[VM, VM, VM, pl.BlockSpec((1, H), lambda j: (0, j)), ANY, ANY],
        scratch_shapes=[
            pltpu.VMEM((M, D), fl), pltpu.VMEM((M, D), fl), pltpu.VMEM((M, 128), fl), pltpu.VMEM((M, D), bf),
            pltpu.VMEM((D, M), bf), pltpu.VMEM((M, D), bf), pltpu.VMEM((M, D), fl), pltpu.VMEM((M, D), fl),
            pltpu.VMEM((2, F, R, H), bf), pltpu.VMEM((2, 4, R, D), bf), pltpu.VMEM((F, R, D), bf),
            pltpu.VMEM((S, slots, T, W), bf), DMA((S,)), DMA((S,)), DMA((5,)),
        ],
        compiler_params=pltpu.CompilerParams(collective_id=cid, dimension_semantics=("arbitrary",), **PARAMS),
        name="feed_forward",
    )(lengths, held, img, cot, att, par, ub, wts, wts, wts)


def back_kernel(S, F, QB, lengths, q, k, v, out_t, lse, cot, back,
                kh, vh, kt, cot_t, delta, dq_t, dk, dv, stage, ssem, rsem):
    g = Place(S, F)
    i, hp = pl.program_id(0), pl.program_id(1)
    slots, pairs = pl.num_programs(0), pl.num_programs(1)
    N = q.shape[2]
    T = N // S
    D = back.shape[2] // 3
    W = D // S
    e = i * pairs + hp

    @pl.when(e == 0)
    def _():
        g.meet(fsdp=False)

    length = lengths[i]
    kt[...] = k[0, 0].T
    cot_t[...] = cot[0].T
    prod = fp32(cot_t[...]) * fp32(out_t[0])
    for hh in range(2):
        hs = slice(hh * HEAD_DIM, (hh + 1) * HEAD_DIM)
        delta[hh : hh + 1] = jnp.sum(prod[hs], axis=0, keepdims=True)
        kh[hh] = masked_keys(k[0, 0], length, hh)
        mine, _ = head_lanes(N, hh)
        vh[hh] = jnp.where(mine, fp32(v[0, 0]), 0.0).astype(jnp.bfloat16)
    dk[...] = jnp.zeros_like(dk)
    dv[...] = jnp.zeros_like(dv)

    @pl.loop(0, N // QB)
    def _(b):
        cols = ds(b * QB, QB)
        qb, cb = q[0, 0, cols], cot[0, cols]
        mines = [head_lanes(QB, hh)[0] for hh in range(2)]
        for hh in range(2):
            hs = slice(hh * HEAD_DIM, (hh + 1) * HEAD_DIM)
            qs = scaled_queries(qb, hh)
            prob = jnp.exp(dot(kh[hh], qs, NT) - lse[0, 0, hh : hh + 1, cols])
            sg = dot(vh[hh], cb, NT)
            sc = (prob * (sg - delta[hh : hh + 1, cols])).astype(jnp.bfloat16)
            w = prob.astype(jnp.bfloat16)
            dv[...] += dot(w, jnp.where(mines[hh], fp32(cb), 0.0).astype(jnp.bfloat16))
            dk[...] += dot(sc, jnp.where(mines[hh], fp32(qs), 0.0).astype(jnp.bfloat16))
            dq_t[hs, cols] = (dot(kt[hs], sc) * HEAD_DIM ** (-0.5)).astype(jnp.bfloat16)

    stage[e, 0] = dq_t[...].T
    stage[e, 1] = dk[...].astype(jnp.bfloat16)
    stage[e, 2] = dv[...].astype(jnp.bfloat16)

    def dst(i, hp, j):
        return back.at[i, :, pl.ds(pl.multiple_of(j * D + g.s * W + hp * 128, 128), 128)]

    def copy(e, i, hp, j, kk):
        return remote(stage.at[e, j, ds((g.s ^ kk) * T, T)], dst(i, hp, j), ssem.at[e, j, kk], rsem.at[e, j, kk], (g.s ^ kk, g.f))

    def local(e, i, hp, j):
        return pltpu.make_async_copy(stage.at[e, j, ds(g.s * T, T)], dst(i, hp, j), ssem.at[e, j, 0])

    for j in range(3):
        for kk in range(1, S):
            copy(e, i, hp, j, kk).start()
        local(e, i, hp, j).start()

    @pl.when(e == slots * pairs - 1)
    def _():
        @pl.loop(0, slots * pairs)
        def _(e):
            i, hp = e // pairs, lax.rem(e, pairs)
            for j in range(3):
                local(e, i, hp, j).wait()
                for kk in range(1, S):
                    cp = copy(e, i, hp, j, kk)
                    cp.wait_send()
                    cp.wait_recv()


def back_call(S, F, cid, lengths, heads, out_t, lse, cots):
    _, slots, N, W = heads.shape
    pairs, T, D = W // 128, N // S, W * S
    bf, fl = jnp.bfloat16, jnp.float32
    QB = min(256, N)
    part = lambda j: pl.BlockSpec((1, 1, N, 128), lambda i, h: (j, i, 0, h))
    return pl.pallas_call(
        functools.partial(back_kernel, S, F, QB),
        grid=(slots, pairs),
        out_shape=jax.ShapeDtypeStruct((slots, T, 3 * D), bf),
        in_specs=[pl.BlockSpec(memory_space=pltpu.SMEM), part(0), part(1), part(2),
                  pl.BlockSpec((1, 128, N), lambda i, h: (i, h, 0)),
                  pl.BlockSpec((1, 1, 8, N), lambda i, h: (i, h, 0, 0)),
                  pl.BlockSpec((1, N, 128), lambda i, h: (i, 0, h))],
        out_specs=ANY,
        scratch_shapes=[
            pltpu.VMEM((2, N, 128), bf), pltpu.VMEM((2, N, 128), bf), pltpu.VMEM((128, N), bf), pltpu.VMEM((128, N), bf),
            pltpu.VMEM((8, N), fl), pltpu.VMEM((128, N), bf), pltpu.VMEM((N, 128), fl), pltpu.VMEM((N, 128), fl),
            pltpu.VMEM((slots * pairs, 3, N, 128), bf), DMA((slots * pairs, 3, S)), DMA((slots * pairs, 3, S)),
        ],
        compiler_params=pltpu.CompilerParams(collective_id=cid, dimension_semantics=("arbitrary",) * 2, **PARAMS),
        name="attend_back",
    )(lengths, heads, heads, heads, out_t, lse, cots)


def entry_back_kernel(img, x1, e, rescot, par, w, dx, dw, vecs, acc):
    j = pl.program_id(0)
    slots, T, D = img.shape
    M = slots * T
    rows = min(128, T)
    gain = par[0:1]
    ej = e[...]
    d = dot(ej, w[...].reshape(D, D), NT)
    dw[...] = dot(x1[...], ej, TN).astype(dw.dtype).reshape(dw.shape)
    esum = jnp.sum(fp32(ej), axis=0, keepdims=True)

    @pl.when(j == 0)
    def _():
        acc[...] = d
        vecs[...] = jnp.zeros_like(vecs)
        vecs[2:3] = esum

    @pl.when(j > 0)
    def _():
        acc[...] += d

    @pl.when(j == 2)
    def _():
        vecs[3:4] = esum

        @pl.loop(0, M // rows)
        def _(r):
            sl = ds(r * rows, rows)
            i, t = r // (T // rows), lax.rem(r, T // rows) * rows
            x = fp32(img[i, pl.ds(t, rows)])
            x = x - mean_rows(x)
            inv = lax.rsqrt(mean_rows(x * x) + EPSILON)
            n = x * inv
            d1 = acc[sl]
            c = d1 * gain
            dx[sl] = rescot[sl] + inv * (c - mean_rows(c) - n * mean_rows(c * n))
            vecs[0:1] += jnp.sum(d1 * n, axis=0, keepdims=True)
            vecs[1:2] += jnp.sum(d1, axis=0, keepdims=True)


def entry_back_call(F, img, x1, e, rescot, par, wts):
    slots, T, D = img.shape
    M = slots * T
    R = wts.shape[2]
    fl = jnp.float32
    return pl.pallas_call(
        entry_back_kernel,
        grid=(3,),
        out_shape=[jax.ShapeDtypeStruct((M, D), fl), jax.ShapeDtypeStruct((F, 3, R, D), jnp.bfloat16), jax.ShapeDtypeStruct((8, D), fl)],
        in_specs=[VM, VM, pl.BlockSpec((M, D), lambda j: (0, j)), VM, VM, pl.BlockSpec((F, 1, R, D), lambda j: (0, j, 0, 0))],
        out_specs=[VM, pl.BlockSpec((F, 1, R, D), lambda j: (0, j, 0, 0)), VM],
        scratch_shapes=[pltpu.VMEM((M, D), fl)],
        compiler_params=pltpu.CompilerParams(dimension_semantics=("arbitrary",), vmem_limit_bytes=60 * 2**20),
        name="entry_back",
    )(img, x1, e, rescot, par, wts)


def body(S, F, images, out_grad, lengths, images_held, first_gain, first_shift, entry_weight, entry_bias, exit_weight,
         exit_bias, first_scale, second_gain, second_shift, up_weight, up_bias, down_weight, down_bias, second_scale):
    slots, T, D = images.shape
    M = slots * T
    R = entry_weight.shape[0]
    FF = up_weight.shape[1]
    fl = jnp.float32
    V = R
    rows = [first_gain, first_shift, entry_bias, exit_bias, first_scale, second_gain, second_shift, up_bias, down_bias, second_scale]
    own_vec = jnp.concatenate(rows).reshape(-1, V)
    own_vec = jnp.pad(own_vec, ((0, 16 - own_vec.shape[0]), (0, 128 - V)))
    first, vec = gather_call(S, F, 0, D, [entry_weight], own_vec, [(0, 0, j * D) for j in range(3)])
    other_blocks = [(2, j * R, 0) for j in range(4)] + [(1, 0, j * D) for j in range(4)] + [(0, 0, 0)]
    rest, _ = gather_call(S, F, 1, D, [exit_weight, up_weight, down_weight], own_vec, other_blocks)
    vec = vec[:, :, :V].astype(fl)
    par = vec.transpose(1, 0, 2).reshape(16, D)
    eb = vec[:, 2:4].reshape(2, D)
    eb = jnp.stack([eb[0], jnp.zeros_like(eb[0]), eb[1]]).reshape(3, 1, D)
    ub = vec[:, 8:12].reshape(1, FF)

    x1, heads = qkv_call(S, F, 2, images, par, eb, first)
    out_t, lse, att = attend_call(S, F, 3, lengths, heads)
    layer, rescot, vmid, ubg, part, cots = middle_call(
        S, F, 4, lengths, images_held, images, out_grad, att.reshape(M, D), par, ub, rest
    )
    back = back_call(S, F, 5, lengths, heads, out_t, lse, cots)
    dx, dw, vlast = entry_back_call(F, images, x1, back.reshape(M, 3 * D), rescot, par, first)

    eg = vlast[2:4].reshape(F, 2, V)
    ug = ubg.reshape(F, 4, V)
    one = lambda v: v.reshape(F, 1, V)
    slab = jnp.concatenate(
        [one(vlast[0]), one(vlast[1]), eg, one(vmid[5]), one(vmid[4]), one(vmid[2]), one(vmid[3]), ug, one(vmid[1]), one(vmid[0])], axis=1
    )
    slab = jnp.pad(slab, ((0, 0), (0, 2), (0, 128 - V)))
    none = jnp.zeros((F, 8, 128), fl)
    g_rest, _ = scatter_call(S, F, 6, part, none)
    g_first, small = scatter_call(S, F, 7, dw, slab)
    small = small[:, :V]
    row = lambda n, m=1: small[n : n + m].reshape(m * V)
    g_first, g_rest = g_first.astype(fl), g_rest.astype(fl)
    return (
        layer.reshape(slots, T, D),
        dx.reshape(slots, T, D),
        row(0),
        row(1),
        g_first.transpose(1, 0, 2).reshape(R, 3 * D),
        row(2, 2),
        g_rest[8],
        row(4),
        row(5),
        row(6),
        row(7),
        g_rest[4:8].transpose(1, 0, 2).reshape(R, 4 * D),
        row(8, 4),
        g_rest[0:4].reshape(4 * R, D),
        row(12),
        row(13),
    )


def solution(mesh):
    S, F = mesh.shape["seq"], mesh.shape["fsdp"]
    vector, matrix, tokens = P("fsdp"), P("fsdp", None), P("fsdp", "seq", None)
    return jax.shard_map(
        functools.partial(body, S, F),
        mesh=mesh,
        in_specs=(tokens, tokens, vector, P(), vector, vector, matrix, vector, matrix, vector, vector, vector, vector,
                  matrix, vector, matrix, vector, vector),
        out_specs=(tokens, tokens, vector, vector, matrix, vector, matrix, vector, vector, vector, vector, matrix, vector,
                   matrix, vector, vector),
        check_vma=False,
    )
```

time: 1090 us -> 507 us (0.47)
  waiting for transfers between devices: 547 us -> 0 us
  Pallas kernels: 0 us -> 471 us
  matrix products: 196 us -> 0 us
  blocking collectives: 139 us -> 0 us
  other arithmetic: 86.6 us -> 4.94 us
  local copies, waits for them, and re-layouts: 65.6 us -> 29.4 us
  starting transfers between devices: 33.5 us -> 0 us
  between operations: 16.3 us -> 0.83 us
    pallas_call x0 -> x9, Pallas kernels: none -> 471 us  [the longest x2 160 us: scatter_call(): pl.pallas_call(kernel, out_shape=[jax.ShapeDtypeStruct((NB, R, D), jnp.bf...]
    reduce_scatter x4 -> x0, waiting for transfers between devices: 258 us -> none  [the longest x1 90.3 us: body(): lax.psum_scatter(weight_cotangent_bundle[11].astype(jnp.bfloat16), 'fsdp'...]
    dot_general x36 -> x0, matrix products: 196 us -> none  [the longest x2 24.6 us: one_image(): jnp.dot(later_standardize_source.T, before_gelu_narrowed, preferred_eleme...]
    all_gather x4 -> x0, waiting for transfers between devices: 156 us -> none  [the longest x1 82.1 us: body(): lax.all_gather(down_weight, 'fsdp', axis=0, tiled=True)]
    all_gather x10 -> x0, blocking collectives: 103 us -> none  [the longest x1 14.4 us: body(): lax.all_gather(up_bias, 'fsdp', axis=0, tiled=True)]
    all_to_all x8 -> x0, waiting for transfers between devices: 85.4 us -> none  [the longest x2 47.2 us: one_image(): lax.all_to_all(jnp.stack([queries, key_rows, value_rows]), 'seq', split_a...]
    convert_element_type x40 -> x1, other arithmetic: 55 us -> 2.17 us  [body(): g_first, g_rest = (g_first.astype(fl), g_rest.astype(fl))]
    psum x1 -> x0, waiting for transfers between devices: 44.6 us -> none  [body(): lax.psum(shards[2].astype(jnp.bfloat16), 'seq').astype(jnp.float32)]
  transfers between devices with their start and end apart: 17 -> 0, of which waited for: 13 -> 0; matrix products, arithmetic and copies ran while one was open for 9% -> 0% of each run, Pallas kernels for 0% -> 0%
where the time goes in v1:
time: 507 us; the launch traced here: 506 us
  Pallas kernels  471 us (93%)
  local copies, waits for them, and re-layouts  29.4 us (6%)
    pallas_call x2, Pallas kernels, scatter_call(): pl.pallas_call(kernel, out_shape=[jax.ShapeDtypeStruct((NB, R, D), jnp.bf...  160 us
    pallas_call x2, Pallas kernels, gather_call(): pl.pallas_call(kernel, out_shape=[jax.ShapeDtypeStruct((F, NB, R, D), jnp...  108 us
    pallas_call x1, Pallas kernels, middle_call(): pl.pallas_call(functools.partial(middle_kernel, S, F), grid=(F,), out_sha...  60.2 us
    pallas_call x1, Pallas kernels, qkv_call(): pl.pallas_call(functools.partial(qkv_kernel, S, F), out_shape=[jax.ShapeD...  44.8 us
    pallas_call x1, Pallas kernels, back_call(): pl.pallas_call(functools.partial(back_kernel, S, F, QB), grid=(slots, pai...  44.6 us
    pallas_call x1, Pallas kernels, attend_call(): pl.pallas_call(functools.partial(attend_kernel, S, F, QB), grid=(slots, p...  38.1 us
    unnamed x26, local copies, waits for them, and re-layouts  15.3 us
    pallas_call x1, Pallas kernels, entry_back_call(): pl.pallas_call(entry_back_kernel, grid=(3,), out_shape=[jax.ShapeDtypeStr...  15 us

profile of v1, /device:TPU:0, one launch (start us, length us, event | category | flops | bytes accessed | tf_op | source)
XLA Modules:
  0.0 506.0 jit_solution(8380158595080604452)
XLA Ops:
  0.7 0.9 dynamic-update-slice
  1.5 0.8 dynamic-update-slice.1
  2.3 0.8 dynamic-update-slice.2
  3.2 0.8 dynamic-update-slice.3
  4.0 0.8 dynamic-update-slice.4
  4.8 0.8 dynamic-update-slice.5
  5.7 0.8 dynamic-update-slice.6
  6.5 0.9 dynamic-update-slice.7
  7.4 0.8 dynamic-update-slice.8
  8.2 0.8 dynamic-update-slice.9
  9.0 0.6 pad.8.refs_1_.refs_3_
  9.6 35.6 %weights_in.2 = (bf16[8,3,128,1024]{3,2,1,0:T(8,128)(2,1)}, bf16[8,16,128]{2,1,0:T(8,128)(2,1)}) custom-call(bf16[128,3072]{1,0:T(8,128)(2,1)} %refs_0_.2, bf16[16,128]{1,0:T(8,128)(2,1)} %pad.8.refs_1_.refs_3_), custom_call_target="tpu_custom_call" | custom-call | tf_op jit(solution)/shard_map/weights_in/pallas_call | solution.py:483
  45.3 0.7 fusion
  46.0 0.1 pad.11.clone
  46.0 0.1 pad_maximum_fusion
  46.1 0.6 reshape.109.eb
  46.7 1.4 copy_bitcast_fusion.par
  48.1 44.8 %project.1 = (bf16[512,1024]{1,0:T(8,128)(2,1)}, bf16[3,2,1024,256]{3,2,1,0:T(8,128)(2,1)}) custom-call(bf16[2,256,1024]{2,1,0:T(8,128)(2,1)} %img.5, f32[16,1024]{1,0:T(8,128)} %copy_bitcast_fusion.par, f32[3,1,1024]{2,1,0:T(1,128)} %reshape.109.eb, bf16[8,3,128,1024]{3,2,1,0:T(8,128)(2,1)} %get-tuple-element.37.wts.w), custom_call_target="tpu_custom_call" | custom-call | tf_op jit(solution)/shard_map/project/pallas_call | solution.py:597
  93.0 0.0 copy-start.3
  93.0 38.1 %attend.1 = (bf16[2,256,1024]{2,1,0:T(8,128)(2,1)}, f32[2,2,8,1024]{3,2,1,0:T(8,128)}, bf16[2,256,1024]{2,1,0:T(8,128)(2,1)}) custom-call(s32[2]{0:T(128)} %lengths.5, bf16[3,2,1024,256]{3,2,1,0:T(8,128)(2,1)} %get-tuple-element.38.q.k.v, bf16[3,2,1024,256]{3,2,1,0:T(8,128)(2,1)} %get-tuple-element.38.q.k.v, bf16[3,2,1024,256]{3,2,1,0:T(8,128)(2,1)} %get-tuple-element.38.q.k.v), custom_call_target="tpu_custom_call" | custom-call | tf_op jit(solution)/shard_map/attend/pallas_call | solution.py:692
  131.1 0.0 copy-done.3
  131.1 0.6 slice.113
  131.7 72.8 %weights_in.3 = (bf16[8,9,128,1024]{3,2,1,0:T(8,128)(2,1)}, bf16[8,16,128]{2,1,0:T(8,128)(2,1)}) custom-call(bf16[128,1024]{1,0:T(8,128)(2,1)} %refs_0_.3, bf16[128,4096]{1,0:T(8,128)(2,1)} %refs_1_.1, bf16[512,1024]{1,0:T(8,128)(2,1)} %refs_2_.1, bf16[16,128]{1,0:T(8,128)(2,1)} %pad.8.refs_1_.refs_3_), custom_call_target="tpu_custom_call" | custom-call | tf_op jit(solution)/shard_map/weights_in/pallas_call | solution.py:483
  204.6 60.2 %feed_forward.1 = (bf16[512,1024]{1,0:T(8,128)(2,1)}, f32[512,1024]{1,0:T(8,128)}, f32[8,1024]{1,0:T(8,128)}, f32[1,4096]{1,0:T(1,128)}, bf16[8,9,128,1024]{3,2,...) custom-call(s32[2]{0:T(128)} %lengths.5, s32[8]{0:T(128)} %held.1, bf16[2,256,1024]{2,1,0:T(8,128)(2,1)} %img.5, ...), custom_call_target="tpu_custom_call" | custom-call | tf_op jit(solution)/shard_map/feed_forward/pallas_call | solution.py:874
  264.8 44.6 %attend_back.1 = bf16[2,256,3072]{2,1,0:T(8,128)(2,1)} custom-call(s32[2]{0:T(128)} %lengths.5, bf16[3,2,1024,256]{3,2,1,0:T(8,128)(2,1)} %get-tuple-element.38.q.k.v, bf16[3,2,1024,256]{3,2,1,0:T(8,128)(2,1)} %get-tuple-element.38.q.k.v, bf16[3,2,1024,256]{3,2,1,0:T(8,128)(2,1)} %get-tuple-element.38.q.k.v, bf16[2,256,1024]{2,1,0:T(8,128)(2,1)} %get-tuple-element.43.out_t, ...), custom_call_target="tpu_custom_call" | custom-call | tf_op jit(solution)/shard_map/attend_back/pallas_call | solution.py:979
  309.4 0.0 copy-start.4
  309.4 0.0 copy-start.5
  309.4 15.0 %entry_back.1 = (f32[512,1024]{1,0:T(8,128)}, bf16[8,3,128,1024]{3,2,1,0:T(8,128)(2,1)}, f32[8,1024]{1,0:T(8,128)}) custom-call(bf16[2,256,1024]{2,1,0:T(8,128)(2,1)} %img.5, bf16[512,1024]{1,0:T(8,128)(2,1)} %get-tuple-element.42.x1, bf16[512,3072]{1,0:T(8,128)(2,1)} %bitcast.61, f32[512,1024]{1,0:T(8,128)} %get-tuple-element.46.rescot, ...), custom_call_target="tpu_custom_call" | custom-call | tf_op jit(solution)/shard_map/entry_back/pallas_call | solution.py:1043
  324.4 0.0 copy-done.4
  324.4 0.9 slice_bitcast_fusion.2
  325.2 0.8 slice.91
  326.0 0.0 copy-done.5
  326.0 0.1 concatenate.7
  326.1 0.6 pad.9.vec
  326.8 48.5 %gradients_out.2 = (bf16[3,128,1024]{2,1,0:T(8,128)(2,1)}, f32[16,128]{1,0:T(8,128)}) custom-call(bf16[8,3,128,1024]{3,2,1,0:T(8,128)(2,1)} %get-tuple-element.48.part, f32[8,16,128]{2,1,0:T(8,128)} %pad.9.vec), custom_call_target="tpu_custom_call" | custom-call | tf_op jit(solution)/shard_map/gradients_out/pallas_call | solution.py:510
  375.2 1.3 convert_bitcast_fusion
  376.6 0.5 copy.36
  377.0 0.0 copy-start.6
  377.0 1.6 copy.38
  378.7 0.0 copy-done.6
  378.7 0.5 slice_bitcast_fusion.12
  379.2 0.6 slice_bitcast_fusion.10
  379.8 0.6 slice_bitcast_fusion.11
  380.3 0.6 broadcast_in_dim.3.vec
  381.0 111.2 %gradients_out.3 = (bf16[9,128,1024]{2,1,0:T(8,128)(2,1)}, f32[8,128]{1,0:T(8,128)}) custom-call(bf16[8,9,128,1024]{3,2,1,0:T(8,128)(2,1)} %get-tuple-element.54.part, f32[8,8,128]{2,1,0:T(8,128)} %broadcast_in_dim.3.vec), custom_call_target="tpu_custom_call" | custom-call | tf_op jit(solution)/shard_map/gradients_out/pallas_call | solution.py:510
  492.2 2.2 convert_element_type.12
  494.4 0.0 copy-start
  494.4 2.1 copy-done
  496.5 0.2 slice_bitcast_fusion
  496.8 1.8 copy.37
  498.6 0.0 copy-start.1
  498.6 3.0 copy.39
  501.6 1.9 slice_bitcast_fusion.1
  503.5 0.0 copy-done.1
  503.5 0.0 copy-start.2
  503.5 1.6 slice.116
  505.1 0.0 copy-done.2
  505.1 1.0 copy.53
  (2 shorter events, 0.0 us)
Async XLA Ops:
  93.0 38.2 %copy-start.3 = (bf16[8,16,128]{2,1,0:T(8,128)(2,1)S(1)}, bf16[8,16,128]{2,1,0:T(8,128)(2,1)}, u32[]{:S(2)}) copy-start(bf16[8,16,128]{2,1,0:T(8,128)(2,1)} %get-tuple-element.36) | copy-start | bytes 98308
  309.4 15.0 %copy-start.4 = (f32[8,1024]{1,0:T(8,128)S(1)}, f32[8,1024]{1,0:T(8,128)}, u32[]{:S(2)}) copy-start(f32[8,1024]{1,0:T(8,128)} %get-tuple-element.50) | copy-start | bytes 98308
  309.4 16.7 %copy-start.5 = (f32[1,4096]{1,0:T(1,128)S(1)}, f32[1,4096]{1,0:T(1,128)}, u32[]{:S(2)}) copy-start(f32[1,4096]{1,0:T(1,128)} %get-tuple-element.51) | copy-start | bytes 49156
  377.0 1.6 copy-start.6
  494.4 2.1 copy-start
  498.6 4.9 copy-start.1
  503.5 1.6 copy-start.2

commit v2 on v1

--- a/solution.py
+++ b/solution.py
@@ -64,21 +64,21 @@
 
 
 class Gather:
-    LAG = 8
-
-    def __init__(self, g, NB, own, full, bounce, sems):
-        self.g, self.NB, self.own, self.full, self.bounce = g, NB, own, full, bounce
-        self.zs, self.zr, self.xs, self.xr, self.cs, self.cr, self.ls = sems
+    def __init__(self, g, NB, b0, own, full, refs, wide=False, lag=8):
+        self.g, self.NB, self.b0, self.own, self.full, self.lag = g, NB, b0, own, full, lag
+        self.bounce, self.zs, self.zr, self.xs, self.xr, self.ms, self.ls = refs
         self.R, self.D = full.shape[2:]
-        self.C = self.D // g.S
+        self.C = self.D if wide else self.D // g.S
+        self.nbits = 0 if wide else g.nbits
+        self.mine = 0 if wide else g.s
         self.nitems = (g.Z - 1) * NB * 2
-        self.steps = self.nitems + self.LAG * g.nbits
+        self.steps = self.nitems + lag * self.nbits
 
     @staticmethod
-    def scratch(S, F, NB, R, D, dtype=jnp.bfloat16):
+    def scratch(S, F, NB, R, D, bounce=True):
         Z, nb = F // 2, S.bit_length() - 1
-        return [pltpu.VMEM((NB, R, D), dtype), DMA((2, NB, Z)), DMA((NB, Z)), DMA((NB, Z, 2, nb)), DMA((NB, Z, 2, nb)),
-                DMA((NB, Z)), DMA((NB, Z)), DMA((NB,))]
+        return [pltpu.VMEM((NB if bounce else 1, R, D), jnp.bfloat16), DMA((2,)), DMA((NB, Z)), DMA((nb,)),
+                DMA((NB, Z, nb)), DMA((2,)), DMA((1,))]
 
     def cols(self, q):
         return ds(q * self.C, self.C)
@@ -86,48 +86,63 @@
     def half(self, p):
         return pl.ds(p * (self.R // 2), self.R // 2)
 
+    def block(self, f, b):
+        return self.full.at[f, self.b0 + b]
+
+    def zfull(self, b, zz):
+        return self.full.at[zz * 2 + self.g.c, self.b0 + b, :, self.cols(self.mine)]
+
     def zcopy(self, src, b, zz, way, to):
-        g = self.g
-        return remote(src, self.full.at[zz * 2 + g.c, b, :, self.cols(g.s)], self.zs.at[way, b, zz], self.zr.at[b, zz], g.at(to))
-
-    def zfull(self, b, zz):
-        return self.full.at[zz * 2 + self.g.c, b, :, self.cols(self.g.s)]
-
-    def mate_copy(self, src, b, zz, core):
-        return remote(src, self.full.at[zz * 2 + core, b], self.cs.at[b, zz], self.cr.at[b, zz], self.g.mate)
+        return remote(src, self.zfull(b, zz), self.zs.at[way], self.zr.at[b, zz], self.g.at(to))
+
+    def mate_copy(self, src, b, zz):
+        return remote(src, self.block(zz * 2 + self.g.c, b), self.ms.at[0], self.ms.at[1], self.g.mate)
+
+    def keeps(self):
+        direct = self.bounce.shape[0] < self.NB
+        for b in range(self.NB):
+            dst = self.block(self.g.f, b) if direct else self.bounce.at[b]
+            yield pltpu.make_async_copy(self.own(b, slice(None)), dst, self.ls.at[0])
+
+    def stored(self):
+        return pltpu.make_async_copy(self.bounce, self.full.at[self.g.f, pl.ds(self.b0, self.NB)], self.ls.at[0])
 
     def start(self):
         g = self.g
         for b in range(self.NB):
-            piece = self.own(b, self.cols(g.s))
+            piece = self.own(b, self.cols(self.mine))
+
             @pl.when(g.z < g.Z - 1)
             def _():
                 self.zcopy(piece, b, g.z, 0, g.z + 1).start()
+
             @pl.when(g.z > 0)
             def _():
                 self.zcopy(piece, b, g.z, 1, g.z - 1).start()
+
+        for cp in self.keeps():
+            cp.start()
         for b in range(self.NB):
-            pltpu.make_async_copy(self.own(b, slice(None)), self.bounce.at[b], self.ls.at[b]).start()
-        for b in range(self.NB):
-            self.mate_copy(self.own(b, slice(None)), b, g.z, g.c).start()
-        for b in range(self.NB):
-            pltpu.make_async_copy(self.own(b, slice(None)), self.bounce.at[b], self.ls.at[b]).wait()
-            pltpu.make_async_copy(self.bounce.at[b], self.full.at[g.f, b], self.ls.at[b]).start()
+            self.mate_copy(self.own(b, slice(None)), b, g.z).start()
+
+    def kept(self):
+        blocks = self.full.at[self.g.f, pl.ds(self.b0, self.NB)]
+        pltpu.make_async_copy(blocks, blocks, self.ls.at[0]).wait()
+        if self.bounce.shape[0] == self.NB:
+            self.stored().start()
 
     def xcopies(self, b, zz, p, j):
         g = self.g
-        f = zz * 2 + g.c
         to = (g.s ^ g.order[p][j], g.f)
         out = []
         for m in span(g.order[p][:j]):
-            ref = self.full.at[f, b, self.half(p), self.cols(g.s ^ m)]
-            out.append(remote(ref, ref, self.xs.at[b, zz, p, j], self.xr.at[b, zz, p, j], to))
+            ref = self.full.at[zz * 2 + g.c, self.b0 + b, self.half(p), self.cols(g.s ^ m)]
+            out.append(remote(ref, ref, self.xs.at[j], self.xr.at[b, zz, j], to))
         return out
 
-    def xall(self, b, zz, p, j):
-        g = self.g
-        ref = self.full.at[zz * 2 + g.c, b, self.half(p), pl.ds(0, self.C << j)]
-        return remote(ref, ref, self.xs.at[b, zz, p, j], self.xr.at[b, zz, p, j], (g.s ^ g.order[p][j], g.f))
+    def doubled(self, b, zz, j):
+        ref = self.full.at[zz * 2 + self.g.c, self.b0 + b, :, pl.ds(0, self.C << j)]
+        return remote(ref, ref, self.xs.at[j], self.xr.at[b, zz, j], self.g.mate)
 
     def item(self, t):
         g = self.g
@@ -143,59 +158,57 @@
 
     def step(self, t):
         g = self.g
-        for j in reversed(range(g.nbits + 1)):
-            b, zz, ok, nxt, more, way = self.item(t - self.LAG * j)
+        for j in reversed(range(self.nbits + 1)):
+            b, zz, ok, nxt, more, way = self.item(t - self.lag * j)
+
             @pl.when(ok)
             def _(j=j, b=b, zz=zz, nxt=nxt, more=more, way=way):
                 if j == 0:
-                    self.zcopy(self.zfull(b, zz), b, zz, 0, g.z).wait_recv()
+                    piece = self.zfull(b, zz)
+                    self.zcopy(piece, b, zz, 0, g.z).wait_recv()
+
                     @pl.when(more)
                     def _():
-                        self.zcopy(self.zfull(b, zz), b, zz, way, nxt).start()
+                        self.zcopy(piece, b, zz, way, nxt).start()
                 else:
-                    for p in range(2):
-                        self.xall(b, zz, p, j - 1).wait_recv()
-                if j < g.nbits:
+                    self.doubled(b, zz, j - 1).wait_recv()
+                if j < self.nbits:
                     for p in range(2):
                         for cp in self.xcopies(b, zz, p, j):
                             cp.start()
                 else:
-                    self.mate_copy(self.full.at[zz * 2 + g.c, b], b, zz, g.c).start()
+                    self.mate_copy(self.block(zz * 2 + g.c, b), b, zz).start()
 
     def run(self, lo, hi):
         @pl.loop(lo, hi)
         def _(t):
             self.step(t)
 
-    def finish(self):
-        g = self.g
-        @pl.loop(0, self.NB)
-        def _(b):
-            blk = self.full.at[g.f, b]
-            pltpu.make_async_copy(self.bounce.at[b], blk, self.ls.at[b]).wait()
-            cp = self.mate_copy(blk, b, g.z, 1 - g.c)
-            cp.wait_send()
-            cp.wait_recv()
-            @pl.when(g.z < g.Z - 1)
-            def _():
-                self.zcopy(self.zfull(b, g.z), b, g.z, 0, g.z + 1).wait_send()
-            @pl.when(g.z > 0)
-            def _():
-                self.zcopy(self.zfull(b, g.z), b, g.z, 1, g.z - 1).wait_send()
-        @pl.loop(0, self.nitems)
-        def _(t):
-            b, zz, ok, nxt, more, way = self.item(t)
-            @pl.when(ok)
-            def _():
-                @pl.when(more)
-                def _():
-                    self.zcopy(self.zfull(b, zz), b, zz, way, nxt).wait_send()
-                for p in range(2):
-                    for j in range(g.nbits):
-                        self.xall(b, zz, p, j).wait_send()
-                cp = self.mate_copy(self.full.at[zz * 2 + g.c, b], b, zz, 1 - g.c)
-                cp.wait_send()
-                cp.wait_recv()
+    def part(self, chips, cols):
+        ref = self.full.at[pl.ds(0, chips), pl.ds(self.b0, self.NB), :, pl.ds(0, cols)]
+        return ref
+
+    def finish_recv(self):
+        if self.bounce.shape[0] == self.NB:
+            self.stored().wait()
+        ref = self.part(self.g.Z, self.D)
+        remote(ref, ref, self.ms.at[0], self.ms.at[1], self.g.mate).wait_recv()
+
+    def finish_send(self):
+        g = self.g
+        ref = self.part(g.Z, self.D)
+        remote(ref, ref, self.ms.at[0], self.ms.at[1], g.mate).wait_send()
+        for j in range(self.nbits):
+            ref = self.part(g.Z - 1, self.C << j)
+            remote(ref, ref, self.xs.at[j], self.xr.at[0, 0, j], g.mate).wait_send()
+        for zz in range(g.Z):
+
+            @pl.when(g.z == zz)
+            def _(zz=zz):
+                for way, n in ((0, zz + 1 if zz < g.Z - 1 else 0), (1, g.Z - zz if zz > 0 else 0)):
+                    if n:
+                        ref = self.part(n, self.C)
+                        remote(ref, ref, self.zs.at[way], self.zr.at[0, 0], g.mate).wait_send()
 
 
 class Scatter:
@@ -219,8 +232,8 @@
         return [
             pltpu.VMEM((n, R, D), dtype), pltpu.VMEM((n, R, D), dtype), pltpu.VMEM((n, 2, R // 2, D - C), dtype),
             pltpu.VMEM((NB, Z, R, C), dtype), pltpu.VMEM((NB, R, C), dtype),
-            DMA((n,)), DMA((n,)), DMA((n,)), DMA((n, 2, nb)), DMA((n, 2, nb)),
-            DMA((NB, Z)), DMA((NB, Z)), DMA((NB, 2, nb)), DMA((NB, 2, nb)), DMA((NB,)),
+            DMA((n,)), DMA((1,)), DMA((n,)), DMA((nb,)), DMA((n, nb)),
+            DMA((1,)), DMA((NB,)), DMA((nb,)), DMA((NB, nb)), DMA((1,)),
         ]
 
     def where(self, t):
@@ -241,7 +254,7 @@
 
     def swap(self, t):
         b, zz = self.where(t)
-        return remote(self.part.at[zz * 2 + 1 - self.g.c, b], self.r0.at[t], self.c_s.at[t], self.c_r.at[t], self.g.mate)
+        return remote(self.part.at[zz * 2 + 1 - self.g.c, b], self.r0.at[t], self.c_s.at[0], self.c_r.at[t], self.g.mate)
 
     def offset(self, j):
         D, C, S = self.D, self.C, self.g.S
@@ -257,14 +270,12 @@
         for i, m in enumerate(span(order[j + 1 :])):
             src = self.cs_buf.at[t, self.half(p), self.cols(base | m)]
             dst = self.xb.at[t, p, :, pl.ds(self.offset(j) + i * self.C, self.C)]
-            out.append(remote(src, dst, self.x_s.at[t, p, j], self.x_r.at[t, p, j], to))
+            out.append(remote(src, dst, self.x_s.at[j], self.x_r.at[t, j], to))
         return out
 
-    def halved(self, t, p, j):
-        g = self.g
-        width = (g.S >> (j + 1)) * self.C
-        ref = self.xb.at[t, p, :, pl.ds(self.offset(j), width)]
-        return remote(ref, ref, self.x_s.at[t, p, j], self.x_r.at[t, p, j], (g.s ^ g.order[p][j], g.f))
+    def halved(self, t, j):
+        ref = self.xb.at[t, :, :, pl.ds(self.offset(j), (self.g.S >> (j + 1)) * self.C)]
+        return remote(ref, ref, self.x_s.at[j], self.x_r.at[t, j], self.g.mate)
 
     def add_halves(self, t, p, j):
         g = self.g
@@ -278,11 +289,11 @@
 
     def piece(self, t, b, zz):
         g = self.g
-        return remote(self.cs_buf.at[t, :, self.cols(g.s)], self.zb.at[b, g.z], self.z_s.at[b, zz], self.z_r.at[b, g.z], g.at(zz))
-
-    def arrived(self, b, zz):
-        g = self.g
-        return remote(self.zb.at[b, zz], self.zb.at[b, zz], self.z_s.at[b, zz], self.z_r.at[b, zz], g.at(zz))
+        return remote(self.cs_buf.at[t, :, self.cols(g.s)], self.zb.at[b, g.z], self.z_s.at[0], self.z_r.at[b], g.at(zz))
+
+    def arrived(self, b):
+        ref = self.zb.at[b, pl.ds(0, self.g.Z - 1)]
+        return remote(ref, ref, self.z_s.at[0], self.z_r.at[b], self.g.mate)
 
     def doubling(self, b, p, j):
         g = self.g
@@ -291,13 +302,15 @@
         for m in span(g.order[p][:j]):
             dst = self.out.at[b, self.half(p), self.cols(g.s ^ m)]
             src = self.fq.at[b, self.half(p)] if m == 0 else dst
-            out.append(remote(src, dst, self.a_s.at[b, p, j], self.a_r.at[b, p, j], to))
+            out.append(remote(src, dst, self.a_s.at[j], self.a_r.at[b, j], to))
         return out
 
-    def doubled(self, b, p, j):
-        g = self.g
-        ref = self.out.at[b, self.half(p), pl.ds(0, self.C << j)]
-        return remote(ref, ref, self.a_s.at[b, p, j], self.a_r.at[b, p, j], (g.s ^ g.order[p][j], g.f))
+    def doubled(self, b, j):
+        ref = self.out.at[b, :, pl.ds(0, self.C << j)]
+        return remote(ref, ref, self.a_s.at[j], self.a_r.at[b, j], self.g.mate)
+
+    def stored(self, b):
+        return pltpu.make_async_copy(self.fq.at[b], self.out.at[b, :, self.cols(self.g.s)], self.o.at[0])
 
     def start(self):
         @pl.loop(0, self.nitems)
@@ -316,15 +329,13 @@
                 if j == 0:
                     r = jnp.where(g.z < (g.Z + 1) // 2, 2 * g.z, 2 * (g.Z - 1 - g.z) + 1)
                     total = self.cs_buf[b * g.Z + r, :, self.cols(g.s)].astype(jnp.float32)
+                    self.arrived(b).wait_recv()
                     for k in range(1, g.Z):
-                        zz = lax.rem(g.z + k, g.Z)
-                        self.arrived(b, zz).wait_recv()
-                        total = total + self.zb[b, zz].astype(jnp.float32)
+                        total = total + self.zb[b, lax.rem(g.z + k, g.Z)].astype(jnp.float32)
                     self.fq[b] = total.astype(self.fq.dtype)
-                    pltpu.make_async_copy(self.fq.at[b], self.out.at[b, :, self.cols(g.s)], self.o.at[b]).start()
+                    self.stored(b).start()
                 else:
-                    for p in range(2):
-                        self.doubled(b, p, j - 1).wait_recv()
+                    self.doubled(b, j - 1).wait_recv()
                 if j < g.nbits:
                     for p in range(2):
                         for cp in self.doubling(b, p, j):
@@ -339,8 +350,8 @@
                     self.swap(u).wait_recv()
                     self.cs_buf[u] = self.cs_buf[u] + self.r0[u]
                 else:
+                    self.halved(u, j - 1).wait_recv()
                     for p in range(2):
-                        self.halved(u, p, j - 1).wait_recv()
                         self.add_halves(u, p, j - 1)
                 if j < g.nbits:
                     for p in range(2):
@@ -358,137 +369,82 @@
 
     def finish(self):
         g = self.g
-        @pl.loop(0, self.nitems)
-        def _(t):
-            b, zz = self.where(t)
-            self.swap(t).wait_send()
-            for p in range(2):
-                for j in range(g.nbits):
-                    self.halved(t, p, j).wait_send()
-            @pl.when(zz != g.z)
-            def _():
-                self.piece(t, b, zz).wait_send()
-        @pl.loop(0, self.NB)
-        def _(b):
-            pltpu.make_async_copy(self.fq.at[b], self.out.at[b, :, self.cols(g.s)], self.o.at[b]).wait()
-            for p in range(2):
-                for j in range(g.nbits):
-                    self.doubled(b, p, j).wait_send()
+        NB, Z, n = self.NB, g.Z, self.nitems
+        done = lambda ref, sem: remote(ref, ref, sem, self.z_r.at[0], g.mate).wait_send()
+        done(self.r0, self.c_s.at[0])
+        done(self.zb.at[:, pl.ds(0, Z - 1)], self.z_s.at[0])
+        for j in range(g.nbits):
+            done(self.xb.at[:, :, :, pl.ds(self.offset(j), (g.S >> (j + 1)) * self.C)], self.x_s.at[j])
+            done(self.out.at[:, :, pl.ds(0, self.C << j)], self.a_s.at[j])
+        ref = self.out.at[:, :, pl.ds(0, self.C)]
+        pltpu.make_async_copy(ref, ref, self.o.at[0]).wait()
 
 
 class VecGather:
     def __init__(self, g, vec, out, sems):
-        self.g, self.vec, self.out = g, vec, out
-        self.vs, self.vr, self.vl = sems
+        self.g, self.vec, self.out, self.sems = g, vec, out, sems
 
     @staticmethod
     def scratch(F):
-        return [DMA((F - 1,)), DMA((F - 1,)), DMA((1,))]
-
-    def copy(self, k):
-        g = self.g
-        return remote(self.vec, self.out.at[g.f], self.vs.at[k - 1], self.vr.at[k - 1], (g.s, lax.rem(g.f + k, g.F)))
+        return [DMA((3,))]
 
     def start(self):
-        for k in range(1, self.g.F):
-            self.copy(k).start()
-        pltpu.make_async_copy(self.vec, self.out.at[self.g.f], self.vl.at[0]).start()
+        g, sems = self.g, self.sems
+        pltpu.make_async_copy(self.vec, self.out.at[g.f], sems.at[2]).start()
+        for k in range(1, g.F):
+            remote(self.vec, self.out.at[g.f], sems.at[0], sems.at[1], (g.s, lax.rem(g.f + k, g.F))).start()
 
     def finish(self):
-        g = self.g
-        pltpu.make_async_copy(self.vec, self.out.at[g.f], self.vl.at[0]).wait()
-        for k in range(1, g.F):
-            self.copy(k).wait_send()
-            src = lax.rem(g.f + g.F - k, g.F)
-            remote(self.vec, self.out.at[src], self.vs.at[k - 1], self.vr.at[k - 1], (g.s, src)).wait_recv()
+        g, sems = self.g, self.sems
+        pltpu.make_async_copy(self.vec, self.out.at[g.f], sems.at[2]).wait()
+        ref = self.out.at[pl.ds(0, g.F - 1)]
+        cp = remote(ref, ref, sems.at[0], sems.at[1], g.mate)
+        cp.wait_send()
+        cp.wait_recv()
 
 
 class VecSum:
-    def __init__(self, g, vec, out, bufs, sems):
+    def __init__(self, g, vec, out, refs):
         self.g, self.vec, self.out = g, vec, out
-        self.fb, self.mid, self.sb = bufs
-        self.vs, self.vr, self.ws, self.wr = sems
+        self.fb, self.mid, self.sb, self.sems = refs
 
     @staticmethod
     def scratch(S, F, N, L):
-        return [pltpu.VMEM((F, N, L), jnp.float32), pltpu.VMEM((N, L), jnp.float32), pltpu.VMEM((S, N, L), jnp.float32),
-                DMA((F - 1,)), DMA((F - 1,)), DMA((S - 1,)), DMA((S - 1,))]
-
-    def one(self, k):
-        g = self.g
-        to = lax.rem(g.f + k, g.F)
-        return remote(self.vec.at[to], self.fb.at[g.f], self.vs.at[k - 1], self.vr.at[k - 1], (g.s, to))
-
-    def two(self, k):
-        g = self.g
-        return remote(self.mid, self.sb.at[g.s], self.ws.at[k - 1], self.wr.at[k - 1], (g.s ^ k, g.f))
+        fl = jnp.float32
+        return [pltpu.VMEM((F, N, L), fl), pltpu.VMEM((N, L), fl), pltpu.VMEM((S, N, L), fl), DMA((4,))]
 
     def start(self):
-        for k in range(1, self.g.F):
-            self.one(k).start()
+        g = self.g
+        for k in range(1, g.F):
+            to = lax.rem(g.f + k, g.F)
+            remote(self.vec.at[to], self.fb.at[g.f], self.sems.at[0], self.sems.at[1], (g.s, to)).start()
 
     def middle(self):
         g = self.g
+        ref = self.fb.at[pl.ds(0, g.F - 1)]
+        cp = remote(ref, ref, self.sems.at[0], self.sems.at[1], g.mate)
+        cp.wait_recv()
         total = self.vec[g.f]
         for k in range(1, g.F):
-            src = lax.rem(g.f + g.F - k, g.F)
-            remote(self.fb.at[src], self.fb.at[src], self.vs.at[k - 1], self.vr.at[k - 1], (g.s, src)).wait_recv()
-            total = total + self.fb[src]
+            total = total + self.fb[lax.rem(g.f + k, g.F)]
         self.mid[...] = total
         for k in range(1, g.S):
-            self.two(k).start()
+            remote(self.mid, self.sb.at[g.s], self.sems.at[2], self.sems.at[3], (g.s ^ k, g.f)).start()
+        cp.wait_send()
 
     def finish(self):
         g = self.g
+        ref = self.sb.at[pl.ds(0, g.S - 1)]
+        cp = remote(ref, ref, self.sems.at[2], self.sems.at[3], g.mate)
+        cp.wait_recv()
         total = self.mid[...]
         for k in range(1, g.S):
-            src = g.s ^ k
-            remote(self.mid, self.sb.at[src], self.ws.at[k - 1], self.wr.at[k - 1], (src, g.f)).wait_recv()
-            total = total + self.sb[src]
+            total = total + self.sb[g.s ^ k]
         self.out[...] = total
-        for k in range(1, g.F):
-            self.one(k).wait_send()
-        for k in range(1, g.S):
-            self.two(k).wait_send()
+        cp.wait_send()
 
 
 PARAMS = dict(has_side_effects=True, vmem_limit_bytes=60 * 2**20)
-
-
-def gather_call(S, F, cid, D, shards, vec, blocks):
-    NB = len(blocks)
-    R = shards[0].shape[0]
-
-    def kernel(*refs):
-        ins, vec_in = refs[: len(shards)], refs[len(shards)]
-        full, vec_out = refs[len(shards) + 1 : len(shards) + 3]
-        rest = refs[len(shards) + 3 :]
-        g = Place(S, F)
-
-        def own(b, cols):
-            w, r0, c0 = blocks[b]
-            if isinstance(cols, slice):
-                return ins[w].at[pl.ds(r0, R), pl.ds(c0, D)]
-            return ins[w].at[pl.ds(r0, R), pl.ds(pl.multiple_of(c0 + cols.start, cols.size), cols.size)]
-
-        g.meet()
-        vg = VecGather(g, vec_in, vec_out, rest[:3])
-        ga = Gather(g, NB, own, full, rest[3], rest[4:])
-        vg.start()
-        ga.start()
-        ga.run(0, ga.steps)
-        ga.finish()
-        vg.finish()
-
-    return pl.pallas_call(
-        kernel,
-        out_shape=[jax.ShapeDtypeStruct((F, NB, R, D), jnp.bfloat16), jax.ShapeDtypeStruct((F,) + vec.shape, vec.dtype)],
-        in_specs=[ANY] * (len(shards) + 1),
-        out_specs=[ANY] * 2,
-        scratch_shapes=VecGather.scratch(F) + Gather.scratch(S, F, NB, R, D),
-        compiler_params=pltpu.CompilerParams(collective_id=cid, **PARAMS),
-        name="weights_in",
-    )(*shards, vec)
 
 
 def scatter_call(S, F, cid, part, vec):
@@ -498,8 +454,8 @@
     def kernel(part, vec, out, vec_out, *rest):
         g = Place(S, F)
         g.meet()
-        vsum = VecSum(g, vec, vec_out, rest[:3], rest[3:7])
-        sc = Scatter(g, NB, part, out, rest[7:12], rest[12:])
+        vsum = VecSum(g, vec, vec_out, rest[:4])
+        sc = Scatter(g, NB, part, out, rest[4:9], rest[9:])
         vsum.start()
         sc.start()
         vsum.middle()
@@ -534,15 +490,59 @@
     return jnp.mean(x, axis=-1, keepdims=True)
 
 
-def qkv_kernel(S, F, img, par, eb, wts, x1, heads, wv, stage, wsem, ssem, rsem):
+def head_lanes(rows, hh):
+    lane = lax.broadcasted_iota(jnp.int32, (rows, 128), 1)
+    mine = (lane >= hh * HEAD_DIM) & (lane < (hh + 1) * HEAD_DIM)
+    spare = lane == (1 - hh) * HEAD_DIM
+    return mine, spare
+
+
+def masked_keys(k, length, hh):
+    N = k.shape[0]
+    mine, spare = head_lanes(N, hh)
+    late = lax.broadcasted_iota(jnp.int32, (N, 128), 0) >= length
+    return jnp.where(mine, fp32(k), jnp.where(spare & late, NEG_LARGE, 0.0)).astype(jnp.bfloat16)
+
+
+def scaled_queries(q, hh):
+    mine, spare = head_lanes(q.shape[0], hh)
+    return jnp.where(mine, fp32(q) * HEAD_DIM ** (-0.5), jnp.where(spare, 1.0, 0.0)).astype(jnp.bfloat16)
+
+
+def front_kernel(S, F, nwide, QB, lengths, img, vec, wq, wx, wu, wd,
+                 first, rest, par, ub, x1, heads_out, out_t, lse, att,
+                 vec_full, norm, eb, stage, heads, kh, vt, o_buf, asem, hsem, ssem, rsem, osem, *refs):
     g = Place(S, F)
-    g.meet(fsdp=False)
     slots, T, D = img.shape
+    R = first.shape[2]
+    V = R
     W = D // S
-    loads = [pltpu.make_async_copy(wts.at[:, j], wv.at[j], wsem.at[j]) for j in range(3)]
-    for cp in loads:
-        cp.start()
-    gain, shift = par[0:1], par[1:2]
+    N = S * T
+    pairs = W // 128
+    vg = VecGather(g, vec, vec_full, refs[0])
+
+    def own_first(b, cols):
+        if isinstance(cols, slice):
+            return wq.at[:, pl.ds(b * D, D)]
+        return wq.at[:, pl.ds(pl.multiple_of(b * D + cols.start, 128), cols.size)]
+
+    def own_rest(b0):
+        def own(b, cols):
+            b = b + b0
+            ref, r0, c0 = (wd, b * R, 0) if b < 4 else (wu, 0, (b - 4) * D) if b < 8 else (wx, 0, 0)
+            if isinstance(cols, slice):
+                return ref.at[pl.ds(r0, R), pl.ds(c0, D)]
+            return ref.at[pl.ds(r0, R), pl.ds(pl.multiple_of(c0 + cols.start, 128), cols.size)]
+
+        return own
+
+    entry = Gather(g, 3, 0, own_first, first, refs[1:8], lag=ENTRY_LAG)
+    thin = Gather(g, 9 - nwide, nwide, own_rest(nwide), rest, refs[8:15])
+    wide = Gather(g, nwide, 0, own_rest(0), rest, refs[15:22], wide=True)
+
+    g.meet()
+    vg.start()
+    entry.start()
     rows = min(128, T)
 
     @pl.loop(0, slots * T // rows)
@@ -550,166 +550,175 @@
         i, t = r // (T // rows), lax.rem(r, T // rows)
         x = fp32(img[i, pl.ds(t * rows, rows)])
         x = x - mean_rows(x)
-        inv = lax.rsqrt(mean_rows(x * x) + EPSILON)
-        x1[ds(r * rows, rows)] = (x * inv * gain + shift).astype(x1.dtype)
-
-    for cp in loads:
-        cp.wait()
-
-    def copy(k, j):
-        src = stage.at[k, j]
-        dst = heads.at[j, :, ds(g.s * T, T)]
-        return remote(src, dst, ssem.at[k, j], rsem.at[k, j], (g.s ^ k, g.f))
-
-    def local(j):
-        return pltpu.make_async_copy(stage.at[0, j], heads.at[j, :, ds(g.s * T, T)], ssem.at[0, j])
-
-    @pl.loop(0, S * 3)
-    def _(n):
-        k = lax.rem(1 + n // 3, S)
-        j = lax.rem(n, 3)
-        cols = ds((g.s ^ k) * W, W)
-        w = wv[j, :, :, cols].reshape(D, W)
-        out = dot(x1[...], w) + eb[j, :, cols]
-        stage[k, j] = out.astype(stage.dtype).reshape(slots, T, W)
-
-        @pl.when(k != 0)
+        norm[ds(r * rows, rows)] = x * lax.rsqrt(mean_rows(x * x) + EPSILON)
+
+    entry.kept()
+    entry.run(0, entry.nitems)
+    vg.finish()
+    thin.start()
+    wide.start()
+    for f in range(F):
+        v = fp32(vec_full[f])[:, :V]
+        par[:, f * V : (f + 1) * V] = v
+        for r in range(2):
+            at = (f * 2 + r) * V
+            eb[2 * (at // D), :, at % D : at % D + V] = v[2 + r : 3 + r]
+        for r in range(4):
+            at = (f * 4 + r) * V
+            ub[:, at : at + V] = v[8 + r : 9 + r]
+    eb[1] = jnp.zeros((1, D), jnp.float32)
+    gain, shift = par[0:1], par[1:2]
+
+    @pl.loop(0, slots * T // rows)
+    def _(r):
+        x1[ds(r * rows, rows)] = (norm[ds(r * rows, rows)] * gain + shift).astype(x1.dtype)
+
+    entry.run(entry.nitems, entry.steps)
+    thin.kept()
+    wide.kept()
+    entry.finish_recv()
+
+    def copy(i, k, j):
+        src = stage.at[i, k, j]
+        dst = heads.at[j, i, ds(g.s * T, T)]
+        return remote(src, dst, ssem.at[i, k, j], rsem.at[i, k, j], (g.s ^ k, g.f))
+
+    def local(i, j):
+        return pltpu.make_async_copy(stage.at[i, 0, j], heads.at[j, i, ds(g.s * T, T)], ssem.at[i, 0, j])
+
+    def project(i):
+        @pl.loop(0, S * 3)
+        def _(n):
+            k = lax.rem(1 + n // 3, S)
+            j = lax.rem(n, 3)
+            cols = ds((g.s ^ k) * W, W)
+            w = first[:, j, :, cols].reshape(D, W)
+            out = dot(x1[i * T : (i + 1) * T], w) + eb[j, :, cols]
+            stage[i, k, j] = out.astype(stage.dtype)
+
+            @pl.when(k != 0)
+            def _():
+                copy(i, k, j).start()
+
+            @pl.when(k == 0)
+            def _():
+                local(i, j).start()
+
+    def projected(i):
+        for j in range(3):
+            local(i, j).wait()
+            for k in range(1, S):
+                copy(i, k, j).wait_send()
+                dst = heads.at[j, i, ds((g.s ^ k) * T, T)]
+                remote(dst, dst, ssem.at[i, k, j], rsem.at[i, k, j], (g.s ^ k, g.f)).wait_recv()
+        keep_heads(i).start()
+
+    def keep_heads(i):
+        return pltpu.make_async_copy(heads.at[:, i], heads_out.at[:, i], hsem.at[i])
+
+    def out_copy(i, hp, kk):
+        e = i * pairs + hp
+        dst = att.at[i, :, pl.ds(pl.multiple_of(g.s * W + hp * 128, 128), 128)]
+        if kk == 0:
+            return pltpu.make_async_copy(o_buf.at[e, ds(g.s * T, T)], dst, osem.at[0, e, 0])
+        return remote(o_buf.at[e, ds((g.s ^ kk) * T, T)], dst, osem.at[0, e, kk], osem.at[1, e, kk], (g.s ^ kk, g.f))
+
+    def attend(i, hp):
+        e = i * pairs + hp
+        lanes = slice(hp * 128, (hp + 1) * 128)
+        vt[...] = heads[2, i, :, lanes].T
+        for hh in range(2):
+            kh[hh] = masked_keys(heads[1, i, :, lanes], lengths[i], hh)
+
+        @pl.loop(0, N // QB)
+        def _(b):
+            cols = ds(b * QB, QB)
+            qb = heads[0, i, cols, lanes]
+            for hh in range(2):
+                sc = dot(kh[hh], scaled_queries(qb, hh), NT)
+                top = jnp.max(sc, axis=0, keepdims=True)
+                ex = jnp.exp(sc - top)
+                total = jnp.sum(ex, axis=0, keepdims=True)
+                w = (ex * (1.0 / total)).astype(jnp.bfloat16)
+                o = dot(vt[hh * HEAD_DIM : (hh + 1) * HEAD_DIM], w).astype(jnp.bfloat16)
+                at = hp * 128 + hh * HEAD_DIM
+                out_t[i, at : at + HEAD_DIM, cols] = o
+                lse[i, hp, hh : hh + 1, cols] = top + jnp.log(total)
+            background(e * (N // QB) + b)
+
+        o_buf[e] = out_t[i, lanes].T
+        for kk in list(range(1, S)) + [0]:
+            out_copy(i, hp, kk).start()
+
+    units = [(i, hp) for i in range(slots) for hp in range(pairs)]
+    early = thin.steps // EARLY
+    per_unit = -(-(thin.steps - early) // (len(units) * (N // QB)))
+
+    def background(n):
+        @pl.when(n < wide.steps)
         def _():
-            copy(k, j).start()
-
-        @pl.when(k == 0)
-        def _():
-            local(j).start()
-
-    for j in range(3):
-        local(j).wait()
-        for k in range(1, S):
-            cp = copy(k, j)
-            cp.wait_send()
-            remote(stage.at[k, j], heads.at[j, :, ds((g.s ^ k) * T, T)], ssem.at[k, j], rsem.at[k, j], (g.s ^ k, g.f)).wait_recv()
-
-
-def qkv_call(S, F, cid, img, par, eb, wts):
-    slots, T, D = img.shape
-    _, _, R, _ = wts.shape
-    W = D // S
-    bf = jnp.bfloat16
-    return pl.pallas_call(
-        functools.partial(qkv_kernel, S, F),
-        out_shape=[jax.ShapeDtypeStruct((slots * T, D), bf), jax.ShapeDtypeStruct((3, slots, S * T, W), bf)],
-        in_specs=[VM, VM, VM, ANY],
-        out_specs=[VM, ANY],
-        scratch_shapes=[pltpu.VMEM((3, F, R, D), bf), pltpu.VMEM((S, 3, slots, T, W), bf), DMA((3,)), DMA((S, 3)), DMA((S, 3))],
-        compiler_params=pltpu.CompilerParams(collective_id=cid, **PARAMS),
-        name="project",
-    )(img, par, eb, wts)
-
-
-def head_lanes(rows, hh):
-    lane = lax.broadcasted_iota(jnp.int32, (rows, 128), 1)
-    mine = (lane >= hh * HEAD_DIM) & (lane < (hh + 1) * HEAD_DIM)
-    spare = lane == (1 - hh) * HEAD_DIM
-    return mine, spare
-
-
-def masked_keys(k, length, hh):
-    N = k.shape[0]
-    mine, spare = head_lanes(N, hh)
-    late = lax.broadcasted_iota(jnp.int32, (N, 128), 0) >= length
-    return jnp.where(mine, fp32(k), jnp.where(spare & late, NEG_LARGE, 0.0)).astype(jnp.bfloat16)
-
-
-def scaled_queries(q, hh):
-    mine, spare = head_lanes(q.shape[0], hh)
-    return jnp.where(mine, fp32(q) * HEAD_DIM ** (-0.5), jnp.where(spare, 1.0, 0.0)).astype(jnp.bfloat16)
-
-
-def attend_kernel(S, F, QB, lengths, q, k, v, out_t, lse, att, kh, vt, o_t, o_buf, ssem, rsem):
-    g = Place(S, F)
-    i, hp = pl.program_id(0), pl.program_id(1)
-    slots, pairs = pl.num_programs(0), pl.num_programs(1)
-    N = q.shape[2]
-    T = N // S
-    W = att.shape[2] // S
-    e = i * pairs + hp
-
-    @pl.when(e == 0)
-    def _():
-        g.meet(fsdp=False)
-
-    length = lengths[i]
-    vt[...] = v[0, 0].T
-    for hh in range(2):
-        kh[hh] = masked_keys(k[0, 0], length, hh)
-
-    @pl.loop(0, N // QB)
-    def _(b):
-        cols = ds(b * QB, QB)
-        qb = q[0, 0, cols]
-        for hh in range(2):
-            sc = dot(kh[hh], scaled_queries(qb, hh), NT)
-            top = jnp.max(sc, axis=0, keepdims=True)
-            ex = jnp.exp(sc - top)
-            total = jnp.sum(ex, axis=0, keepdims=True)
-            w = (ex * (1.0 / total)).astype(jnp.bfloat16)
-            o = dot(vt[hh * HEAD_DIM : (hh + 1) * HEAD_DIM], w).astype(jnp.bfloat16)
-            o_t[hh * HEAD_DIM : (hh + 1) * HEAD_DIM, cols] = o
-            lse[0, 0, hh : hh + 1, cols] = top + jnp.log(total)
-
-    out_t[0] = o_t[...]
-    o_buf[e] = o_t[...].T
-
-    def copy(e, i, hp, kk):
-        dst = att.at[i, :, pl.ds(pl.multiple_of(g.s * W + hp * 128, 128), 128)]
-        return remote(o_buf.at[e, ds((g.s ^ kk) * T, T)], dst, ssem.at[e, kk], rsem.at[e, kk], (g.s ^ kk, g.f))
-
-    def local(e, i, hp):
-        dst = att.at[i, :, pl.ds(pl.multiple_of(g.s * W + hp * 128, 128), 128)]
-        return pltpu.make_async_copy(o_buf.at[e, ds(g.s * T, T)], dst, ssem.at[e, 0])
-
-    for kk in range(1, S):
-        copy(e, i, hp, kk).start()
-    local(e, i, hp).start()
-
-    @pl.when(e == slots * pairs - 1)
-    def _():
-        @pl.loop(0, slots * pairs)
-        def _(e):
-            i, hp = e // pairs, lax.rem(e, pairs)
-            local(e, i, hp).wait()
-            for kk in range(1, S):
-                cp = copy(e, i, hp, kk)
+            wide.step(n)
+
+        for m in range(per_unit):
+            thin.step(early + n * per_unit + m)
+
+    for i in range(slots):
+        project(i)
+    thin.run(0, early)
+    entry.finish_send()
+    for n, (i, hp) in enumerate(units):
+        if hp == 0:
+            projected(i)
+        attend(i, hp)
+    wide.run(len(units) * (N // QB), wide.steps)
+    for gather in (thin, wide):
+        gather.finish_recv()
+        gather.finish_send()
+    for i, hp in units:
+        for kk in range(S):
+            cp = out_copy(i, hp, kk)
+            if kk == 0:
+                cp.wait()
+            else:
                 cp.wait_send()
                 cp.wait_recv()
-
-
-def attend_call(S, F, cid, lengths, heads):
-    _, slots, N, W = heads.shape
-    pairs, T, D = W // 128, N // S, W * S
-    bf = jnp.bfloat16
-    QB = min(256, N)
-    part = lambda j: pl.BlockSpec((1, 1, N, 128), lambda i, h: (j, i, 0, h))
+    for i in range(slots):
+        keep_heads(i).wait()
+
+
+ENTRY_LAG = 6
+WIDE = 3
+EARLY = 10
+
+
+def front_call(S, F, cid, lengths, img, vec, wq, wx, wu, wd):
+    slots, T, D = img.shape
+    R, FF = wq.shape[0], wu.shape[1]
+    W, N = D // S, S * T
+    pairs = W // 128
+    bf, fl = jnp.bfloat16, jnp.float32
+    out = jax.ShapeDtypeStruct
     return pl.pallas_call(
-        functools.partial(attend_kernel, S, F, QB),
-        grid=(slots, pairs),
+        functools.partial(front_kernel, S, F, WIDE, min(256, N)),
         out_shape=[
-            jax.ShapeDtypeStruct((slots, W, N), bf),
-            jax.ShapeDtypeStruct((slots, pairs, 8, N), jnp.float32),
-            jax.ShapeDtypeStruct((slots, T, D), bf),
+            out((F, 3, R, D), bf), out((F, 9, R, D), bf), out((16, D), fl), out((1, FF), fl), out((slots * T, D), bf),
+            out((3, slots, N, W), bf), out((slots, W, N), bf), out((slots, pairs, 8, N), fl), out((slots, T, D), bf),
         ],
-        in_specs=[pl.BlockSpec(memory_space=pltpu.SMEM), part(0), part(1), part(2)],
-        out_specs=[
-            pl.BlockSpec((1, 128, N), lambda i, h: (i, h, 0)),
-            pl.BlockSpec((1, 1, 8, N), lambda i, h: (i, h, 0, 0)),
-            ANY,
-        ],
+        in_specs=[pl.BlockSpec(memory_space=pltpu.SMEM), VM, ANY, ANY, ANY, ANY, ANY],
+        out_specs=[VM, ANY, VM, VM, VM, ANY, VM, VM, ANY],
         scratch_shapes=[
-            pltpu.VMEM((2, N, 128), bf), pltpu.VMEM((128, N), bf), pltpu.VMEM((128, N), bf),
-            pltpu.VMEM((slots * pairs, N, 128), bf), DMA((slots * pairs, S)), DMA((slots * pairs, S)),
-        ],
-        compiler_params=pltpu.CompilerParams(collective_id=cid, dimension_semantics=("arbitrary",) * 2, **PARAMS),
-        name="attend",
-    )(lengths, heads, heads, heads)
+            pltpu.VMEM((F, 16, 128), bf), pltpu.VMEM((slots * T, D), fl), pltpu.VMEM((3, 1, D), fl), pltpu.VMEM((slots, S, 3, T, W), bf),
+            pltpu.VMEM((3, slots, N, W), bf), pltpu.VMEM((2, N, 128), bf), pltpu.VMEM((128, N), bf),
+            pltpu.VMEM((slots * pairs, N, 128), bf), DMA((1,)), DMA((slots,)), DMA((slots, S, 3)), DMA((slots, S, 3)),
+            DMA((2, slots * pairs, S)),
+        ]
+        + VecGather.scratch(F)
+        + Gather.scratch(S, F, 3, R, D, bounce=False)
+        + Gather.scratch(S, F, 9 - WIDE, R, D)
+        + Gather.scratch(S, F, WIDE, R, D),
+        compiler_params=pltpu.CompilerParams(collective_id=cid, **PARAMS),
+        name="front",
+    )(lengths, img, vec, wq, wx, wu, wd)
 
 
 def middle_kernel(S, F, lengths, held, img, cot, att, par, ub, wx, wu, wd,
@@ -1061,19 +1070,14 @@
     fl = jnp.float32
     V = R
     rows = [first_gain, first_shift, entry_bias, exit_bias, first_scale, second_gain, second_shift, up_bias, down_bias, second_scale]
-    own_vec = jnp.concatenate(rows).reshape(-1, V)
-    own_vec = jnp.pad(own_vec, ((0, 16 - own_vec.shape[0]), (0, 128 - V)))
-    first, vec = gather_call(S, F, 0, D, [entry_weight], own_vec, [(0, 0, j * D) for j in range(3)])
-    other_blocks = [(2, j * R, 0) for j in range(4)] + [(1, 0, j * D) for j in range(4)] + [(0, 0, 0)]
-    rest, _ = gather_call(S, F, 1, D, [exit_weight, up_weight, down_weight], own_vec, other_blocks)
-    vec = vec[:, :, :V].astype(fl)
-    par = vec.transpose(1, 0, 2).reshape(16, D)
-    eb = vec[:, 2:4].reshape(2, D)
-    eb = jnp.stack([eb[0], jnp.zeros_like(eb[0]), eb[1]]).reshape(3, 1, D)
-    ub = vec[:, 8:12].reshape(1, FF)
-
-    x1, heads = qkv_call(S, F, 2, images, par, eb, first)
-    out_t, lse, att = attend_call(S, F, 3, lengths, heads)
+    own_vec, at = jnp.zeros((16, 128), jnp.bfloat16), 0
+    for v in rows:
+        n = v.shape[0] // V
+        own_vec = own_vec + jnp.pad(v.reshape(n, V), ((at, 16 - at - n), (0, 128 - V)))
+        at += n
+    first, rest, par, ub, x1, heads, out_t, lse, att = front_call(
+        S, F, 0, lengths, images, own_vec, entry_weight, exit_weight, up_weight, down_weight
+    )
     layer, rescot, vmid, ubg, part, cots = middle_call(
         S, F, 4, lengths, images_held, images, out_grad, att.reshape(M, D), par, ub, rest
     )

time: 507 us -> 433 us (0.85)
  Pallas kernels: 471 us -> 409 us
  local copies, waits for them, and re-layouts: 29.4 us -> 18.4 us
    pallas_call x4 -> x1, Pallas kernels: 191 us -> 129 us  [front_call(): pl.pallas_call(functools.partial(front_kernel, S, F, WIDE, min(256, N)),...]
    unnamed x26 -> x15, local copies, waits for them, and re-layouts: 15.3 us -> 7.76 us
where the time goes in v2:
time: 433 us
  Pallas kernels  409 us (94%)
  local copies, waits for them, and re-layouts  18.4 us (4%)
  other arithmetic  4.87 us (1%)
    pallas_call x2, Pallas kernels, scatter_call(): pl.pallas_call(kernel, out_shape=[jax.ShapeDtypeStruct((NB, R, D), jnp.bf...  159 us
    pallas_call x1, Pallas kernels, front_call(): pl.pallas_call(functools.partial(front_kernel, S, F, WIDE, min(256, N)),...  129 us
    pallas_call x1, Pallas kernels, middle_call(): pl.pallas_call(functools.partial(middle_kernel, S, F), grid=(F,), out_sha...  59.8 us
    pallas_call x1, Pallas kernels, back_call(): pl.pallas_call(functools.partial(back_kernel, S, F, QB), grid=(slots, pai...  45.4 us
    pallas_call x1, Pallas kernels, entry_back_call(): pl.pallas_call(entry_back_kernel, grid=(3,), out_shape=[jax.ShapeDtypeStr...  15.1 us

profile of v2, /device:TPU:0, one launch (start us, length us, event | category | flops | bytes accessed | tf_op | source)
XLA Modules:
  0.0 432.6 jit_solution(8429163109785054607)
XLA Ops:
  0.6 1.4 pad_add_fusion.vec
  2.1 129.3 %front.1 = (bf16[8,3,128,1024]{3,2,1,0:T(8,128)(2,1)}, bf16[8,9,128,1024]{3,2,1,0:T(8,128)(2,1)}, f32[16,1024]{1,0:T(8,128)}, f32[1,4096]{1,0:T(1,128)}, bf16[51...) custom-call(s32[2]{0:T(128)} %lengths.5, ...), custom_call_target="tpu_custom_call" | custom-call | tf_op jit(solution)/shard_map/front/pallas_call | solution.py:701
  131.4 59.8 %feed_forward.1 = (bf16[512,1024]{1,0:T(8,128)(2,1)}, f32[512,1024]{1,0:T(8,128)}, f32[8,1024]{1,0:T(8,128)}, f32[1,4096]{1,0:T(1,128)}, bf16[8,9,128,1024]{3,2,...) custom-call(s32[2]{0:T(128)} %lengths.5, s32[8]{0:T(128)} %held.1, bf16[2,256,1024]{2,1,0:T(8,128)(2,1)} %img.5, ...), custom_call_target="tpu_custom_call" | custom-call | tf_op jit(solution)/shard_map/feed_forward/pallas_call | solution.py:883
  191.2 45.4 %attend_back.1 = bf16[2,256,3072]{2,1,0:T(8,128)(2,1)} custom-call(s32[2]{0:T(128)} %lengths.5, bf16[3,2,1024,256]{3,2,1,0:T(8,128)(2,1)} %get-tuple-element.43.q.k.v, bf16[3,2,1024,256]{3,2,1,0:T(8,128)(2,1)} %get-tuple-element.43.q.k.v, bf16[3,2,1024,256]{3,2,1,0:T(8,128)(2,1)} %get-tuple-element.43.q.k.v, bf16[2,256,1024]{2,1,0:T(8,128)(2,1)} %get-tuple-element.44.out_t, ...), custom_call_target="tpu_custom_call" | custom-call | tf_op jit(solution)/shard_map/attend_back/pallas_call | solution.py:988
  236.6 0.0 copy-start.3
  236.6 0.0 copy-start.4
  236.6 15.1 %entry_back.1 = (f32[512,1024]{1,0:T(8,128)}, bf16[8,3,128,1024]{3,2,1,0:T(8,128)(2,1)}, f32[8,1024]{1,0:T(8,128)}) custom-call(bf16[2,256,1024]{2,1,0:T(8,128)(2,1)} %img.5, bf16[512,1024]{1,0:T(8,128)(2,1)} %get-tuple-element.42.x1, bf16[512,3072]{1,0:T(8,128)(2,1)} %bitcast.60, f32[512,1024]{1,0:T(8,128)} %get-tuple-element.47.rescot, ...), custom_call_target="tpu_custom_call" | custom-call | tf_op jit(solution)/shard_map/entry_back/pallas_call | solution.py:1052
  251.6 0.0 copy-done.3
  251.7 0.9 slice_bitcast_fusion.2
  252.5 0.8 slice.68
  253.3 0.0 copy-done.4
  253.3 0.1 concatenate.3
  253.4 0.6 pad.54.vec
  254.0 51.9 %gradients_out.2 = (bf16[3,128,1024]{2,1,0:T(8,128)(2,1)}, f32[16,128]{1,0:T(8,128)}) custom-call(bf16[8,3,128,1024]{3,2,1,0:T(8,128)(2,1)} %get-tuple-element.50.part, f32[8,16,128]{2,1,0:T(8,128)} %pad.54.vec), custom_call_target="tpu_custom_call" | custom-call | tf_op jit(solution)/shard_map/gradients_out/pallas_call | solution.py:466
  305.9 1.3 convert_bitcast_fusion
  307.2 0.5 copy.34
  307.7 0.0 copy-start.5
  307.7 1.6 copy.36
  309.3 0.0 copy-done.5
  309.3 0.5 slice_bitcast_fusion.12
  309.9 0.6 slice_bitcast_fusion.10
  310.4 0.6 slice_bitcast_fusion.11
  311.0 0.6 broadcast_in_dim.3.vec
  311.6 107.2 %gradients_out.3 = (bf16[9,128,1024]{2,1,0:T(8,128)(2,1)}, f32[8,128]{1,0:T(8,128)}) custom-call(bf16[8,9,128,1024]{3,2,1,0:T(8,128)(2,1)} %get-tuple-element.56.part, f32[8,8,128]{2,1,0:T(8,128)} %broadcast_in_dim.3.vec), custom_call_target="tpu_custom_call" | custom-call | tf_op jit(solution)/shard_map/gradients_out/pallas_call | solution.py:466
  418.8 2.2 convert_element_type.26
  421.0 0.0 copy-start
  421.0 2.1 copy-done
  423.1 0.2 slice_bitcast_fusion
  423.4 1.8 copy.35
  425.2 0.0 copy-start.1
  425.2 3.0 copy.37
  428.2 1.9 slice_bitcast_fusion.1
  430.1 0.0 copy-done.1
  430.1 0.0 copy-start.2
  430.1 1.6 slice.90
  431.7 0.0 copy-done.2
  431.7 1.0 copy.39
  (1 shorter events, 0.0 us)
Async XLA Ops:
  236.6 15.1 %copy-start.3 = (f32[8,1024]{1,0:T(8,128)S(1)}, f32[8,1024]{1,0:T(8,128)}, u32[]{:S(2)}) copy-start(f32[8,1024]{1,0:T(8,128)} %get-tuple-element.52) | copy-start | bytes 98308
  236.6 16.7 %copy-start.4 = (f32[1,4096]{1,0:T(1,128)S(1)}, f32[1,4096]{1,0:T(1,128)}, u32[]{:S(2)}) copy-start(f32[1,4096]{1,0:T(1,128)} %get-tuple-element.53) | copy-start | bytes 49156
  307.7 1.6 copy-start.5
  421.0 2.1 copy-start
  425.2 4.9 %copy-start.1 = (bf16[9,128,1024]{2,1,0:T(8,128)(2,1)S(1)}, bf16[9,128,1024]{2,1,0:T(8,128)(2,1)}, u32[]{:S(2)}) copy-start(bf16[9,128,1024]{2,1,0:T(8,128)(2,1)} %get-tuple-element.57) | copy-start | bytes 7077892
  430.1 1.6 copy-start.2

commit v3 on v2

v3 whole, which is shorter than its diff:
```python
import functools
import math

import jax
import jax.numpy as jnp
from jax import lax
from jax.experimental import pallas as pl
from jax.experimental.pallas import tpu as pltpu
from jax.sharding import PartitionSpec as P

HEAD_DIM = 64
EPSILON = 1e-06
NEG_LARGE = -1e30

MESH = pl.DeviceIdType.MESH
DMA = pltpu.SemaphoreType.DMA
ANY = pl.BlockSpec(memory_space=pl.ANY)
VM = pl.BlockSpec(memory_space=pltpu.VMEM)


def remote(src, dst, ssem, rsem, dev):
    return pltpu.make_async_remote_copy(
        src_ref=src, dst_ref=dst, send_sem=ssem, recv_sem=rsem, device_id=dev, device_id_type=MESH
    )


class Place:
    def __init__(self, S, F):
        self.S, self.F, self.Z = S, F, F // 2
        self.bits = [1 << b for b in range(S.bit_length() - 1)]
        self.nbits = len(self.bits)
        self.order = [self.bits, self.bits[1:] + self.bits[:1]]
        self.s = lax.axis_index("seq")
        self.f = lax.axis_index("fsdp")
        self.z, self.c = self.f // 2, lax.rem(self.f, 2)
        self.mate = (self.s, self.f ^ 1)

    def at(self, zz):
        return (self.s, zz * 2 + self.c)

    def greet(self):
        bar = pltpu.get_barrier_semaphore()
        for k in range(1, self.F):
            pl.semaphore_signal(bar, inc=1, device_id=(self.s, lax.rem(self.f + k, self.F)), device_id_type=MESH)
        for k in range(1, self.S):
            pl.semaphore_signal(bar, inc=1, device_id=(self.s ^ k, self.f), device_id_type=MESH)
        return lambda: pl.semaphore_wait(bar, self.F + self.S - 2)

    def meet(self):
        self.greet()()


def span(bits):
    out = [0]
    for b in bits:
        out = out + [m | b for m in out]
    return out


def ds(start, size):
    return pl.ds(pl.multiple_of(start, size), size)


class Gather:
    def __init__(self, g, NB, b0, own, full, refs, wide=False, lag=8):
        self.g, self.NB, self.b0, self.own, self.full, self.lag = g, NB, b0, own, full, lag
        self.bounce, self.zs, self.zr, self.xs, self.xr, self.ms, self.ls = refs
        self.R, self.D = full.shape[2:]
        self.C = self.D if wide else self.D // g.S
        self.nbits = 0 if wide else g.nbits
        self.mine = 0 if wide else g.s
        self.nitems = (g.Z - 1) * NB * 2
        self.steps = self.nitems + lag * self.nbits

    @staticmethod
    def scratch(S, F, NB, R, D, bounce=True):
        Z, nb = F // 2, S.bit_length() - 1
        return [pltpu.VMEM((NB if bounce else 1, R, D), jnp.bfloat16), DMA((2,)), DMA((NB, Z)), DMA((nb,)),
                DMA((NB, Z, nb)), DMA((2,)), DMA((1,))]

    def cols(self, q):
        return ds(q * self.C, self.C)

    def half(self, p):
        return pl.ds(p * (self.R // 2), self.R // 2)

    def block(self, f, b):
        return self.full.at[f, self.b0 + b]

    def zfull(self, b, zz):
        return self.full.at[zz * 2 + self.g.c, self.b0 + b, :, self.cols(self.mine)]

    def zcopy(self, src, b, zz, way, to):
        return remote(src, self.zfull(b, zz), self.zs.at[way], self.zr.at[b, zz], self.g.at(to))

    def mate_copy(self, src, b, zz):
        return remote(src, self.block(zz * 2 + self.g.c, b), self.ms.at[0], self.ms.at[1], self.g.mate)

    def keeps(self):
        direct = self.bounce.shape[0] < self.NB
        for b in range(self.NB):
            dst = self.block(self.g.f, b) if direct else self.bounce.at[b]
            yield pltpu.make_async_copy(self.own(b, slice(None)), dst, self.ls.at[0])

    def stored(self):
        return pltpu.make_async_copy(self.bounce, self.full.at[self.g.f, pl.ds(self.b0, self.NB)], self.ls.at[0])

    def start(self):
        g = self.g
        for b in range(self.NB):
            piece = self.own(b, self.cols(self.mine))

            @pl.when(g.z < g.Z - 1)
            def _():
                self.zcopy(piece, b, g.z, 0, g.z + 1).start()

            @pl.when(g.z > 0)
            def _():
                self.zcopy(piece, b, g.z, 1, g.z - 1).start()

        for cp in self.keeps():
            cp.start()
        for b in range(self.NB):
            self.mate_copy(self.own(b, slice(None)), b, g.z).start()

    def kept(self):
        blocks = self.full.at[self.g.f, pl.ds(self.b0, self.NB)]
        pltpu.make_async_copy(blocks, blocks, self.ls.at[0]).wait()
        if self.bounce.shape[0] == self.NB:
            self.stored().start()

    def xcopies(self, b, zz, p, j):
        g = self.g
        to = (g.s ^ g.order[p][j], g.f)
        out = []
        for m in span(g.order[p][:j]):
            ref = self.full.at[zz * 2 + g.c, self.b0 + b, self.half(p), self.cols(g.s ^ m)]
            out.append(remote(ref, ref, self.xs.at[j], self.xr.at[b, zz, j], to))
        return out

    def doubled(self, b, zz, j):
        ref = self.full.at[zz * 2 + self.g.c, self.b0 + b, :, pl.ds(0, self.C << j)]
        return remote(ref, ref, self.xs.at[j], self.xr.at[b, zz, j], self.g.mate)

    def item(self, t):
        g = self.g
        h = 1 + t // (2 * self.NB)
        r = lax.rem(t, 2 * self.NB)
        b, below = r // 2, lax.rem(r, 2) == 0
        zz = jnp.where(below, g.z - h, g.z + h)
        ok = (t >= 0) & (t < self.nitems) & (zz >= 0) & (zz < g.Z)
        nxt = jnp.where(below, g.z + 1, g.z - 1)
        more = (nxt >= 0) & (nxt < g.Z)
        way = jnp.where(below, 0, 1)
        return b, zz, ok, nxt, more, way

    def step(self, t):
        g = self.g
        for j in reversed(range(self.nbits + 1)):
            b, zz, ok, nxt, more, way = self.item(t - self.lag * j)

            @pl.when(ok)
            def _(j=j, b=b, zz=zz, nxt=nxt, more=more, way=way):
                if j == 0:
                    piece = self.zfull(b, zz)
                    self.zcopy(piece, b, zz, 0, g.z).wait_recv()

                    @pl.when(more)
                    def _():
                        self.zcopy(piece, b, zz, way, nxt).start()
                else:
                    self.doubled(b, zz, j - 1).wait_recv()
                if j < self.nbits:
                    for p in range(2):
                        for cp in self.xcopies(b, zz, p, j):
                            cp.start()
                else:
                    self.mate_copy(self.block(zz * 2 + g.c, b), b, zz).start()

    def run(self, lo, hi):
        @pl.loop(lo, hi)
        def _(t):
            self.step(t)

    def part(self, chips, cols):
        ref = self.full.at[pl.ds(0, chips), pl.ds(self.b0, self.NB), :, pl.ds(0, cols)]
        return ref

    def finish_recv(self):
        if self.bounce.shape[0] == self.NB:
            self.stored().wait()
        ref = self.part(self.g.Z, self.D)
        remote(ref, ref, self.ms.at[0], self.ms.at[1], self.g.mate).wait_recv()

    def finish_send(self):
        g = self.g
        ref = self.part(g.Z, self.D)
        remote(ref, ref, self.ms.at[0], self.ms.at[1], g.mate).wait_send()
        for j in range(self.nbits):
            ref = self.part(g.Z - 1, self.C << j)
            remote(ref, ref, self.xs.at[j], self.xr.at[0, 0, j], g.mate).wait_send()
        for zz in range(g.Z):

            @pl.when(g.z == zz)
            def _(zz=zz):
                for way, n in ((0, zz + 1 if zz < g.Z - 1 else 0), (1, g.Z - zz if zz > 0 else 0)):
                    if n:
                        ref = self.part(n, self.C)
                        remote(ref, ref, self.zs.at[way], self.zr.at[0, 0], g.mate).wait_send()


class Scatter:
    def __init__(self, g, part, out, refs, per=0, wide=False, lag=4, tail=0, above=False):
        self.g, self.part, self.out, self.per, self.wide, self.lag, self.above = g, part, out, per, wide, lag, above
        self.core, self.ring, self.xb, self.zb, self.fq = refs[:5]
        self.own, self.c_s, self.c_r, self.x_s, self.x_r, self.z_s, self.z_r, self.a_s, self.a_r, self.o, self.free = refs[5:]
        _, self.NB, self.R, self.D = part.shape
        self.C = self.D // g.S
        self.n = self.NB * g.Z
        self.K = self.ring.shape[0]
        self.tail = tail or (lag if wide else g.nbits * lag + 2 * lag)
        self.after = g.nbits if wide else 0
        self.steps = self.n + self.per + self.tail + lag * (self.after + g.nbits + 1) + 1

    @staticmethod
    def scratch(S, F, NB, R, D, wide=False, K=0):
        Z, nb = F // 2, S.bit_length() - 1
        K = K or NB * Z
        C, n, bf = D // S, NB * Z, jnp.bfloat16
        nx = NB if wide else n
        return [
            pltpu.VMEM((n, R, D), bf), pltpu.VMEM((K, R, D), bf), pltpu.VMEM((nx, 2, R // 2, D - C), bf),
            pltpu.VMEM((NB, Z - 1, R, D if wide else C), bf), pltpu.VMEM((NB, R, D if wide else C), bf),
            DMA((n,)), DMA((1,)), DMA((K,)), DMA((nb,)), DMA((nx, nb)), DMA((1,)), DMA((NB,)),
            DMA((nb,)), DMA((NB, nb)), DMA((1,)), pltpu.SemaphoreType.REGULAR,
        ]

    def fold(self, zz):
        Z = self.g.Z
        return jnp.where(zz < (Z + 1) // 2, 2 * zz, 2 * (Z - 1 - zz) + 1)

    def unfold(self, r):
        return jnp.where(lax.rem(r, 2) == 0, r // 2, self.g.Z - 1 - r // 2)

    def where(self, t):
        Z, per = self.g.Z, self.per
        b, zz = t // Z, self.unfold(lax.rem(t, Z))
        if per:
            rows = t < per * Z
            b, zz = jnp.where(rows, lax.rem(t, per), b), jnp.where(rows, t // per, zz)
        return b, zz

    def item_of(self, b, zz):
        Z, per = self.g.Z, self.per
        t = b * Z + self.fold(zz)
        return jnp.where(b < per, zz * per + b, t) if per else t

    def due(self, v):
        Z, per = self.g.Z, self.per
        ok = (v >= 0) & (v < self.n) & (lax.rem(v, Z) == Z - 1)
        b = v // Z
        if per:
            first = per * Z
            u = v - first + 1
            early = (u >= 0) & (u < per)
            w = v - per
            late = (w >= first) & (w < self.n) & (lax.rem(w, Z) == Z - 1)
            ok = early | late
            b = jnp.where(early, u, w // Z)
        return b, ok

    def cols(self, q):
        return ds(q * self.C, self.C)

    def half(self, p):
        return pl.ds(p * (self.R // 2), self.R // 2)

    def load(self, t):
        b, zz = self.where(t)
        return pltpu.make_async_copy(self.part.at[zz * 2 + self.g.c, b], self.core.at[t], self.own.at[t])

    def swap(self, t):
        b, zz = self.where(t)
        k = lax.rem(t, self.K)
        return remote(self.part.at[zz * 2 + 1 - self.g.c, b], self.ring.at[k], self.c_s.at[0], self.c_r.at[k], self.g.mate)

    def offset(self, j):
        return sum((self.g.S >> (i + 1)) * self.C for i in range(j))

    def halving(self, src, x, p, j):
        g = self.g
        order = g.order[p]
        base = (g.s ^ order[j]) & sum(order[: j + 1])
        to = (g.s ^ order[j], g.f)
        out = []
        for i, m in enumerate(span(order[j + 1 :])):
            dst = self.xb.at[x, p, :, pl.ds(self.offset(j) + i * self.C, self.C)]
            out.append(remote(src.at[self.half(p), self.cols(base | m)], dst, self.x_s.at[j], self.x_r.at[x, j], to))
        return out

    def halved(self, x, j):
        ref = self.xb.at[x, :, :, pl.ds(self.offset(j), (self.g.S >> (j + 1)) * self.C)]
        return remote(ref, ref, self.x_s.at[j], self.x_r.at[x, j], self.g.mate)

    def add_halves(self, buf, x, j):
        g = self.g
        for p in range(2):
            order = g.order[p]
            base = g.s & sum(order[: j + 1])
            for i, m in enumerate(span(order[j + 1 :])):
                q = self.cols(base | m)
                got = self.xb[x, p, :, pl.ds(self.offset(j) + i * self.C, self.C)]
                buf[self.half(p), q] = buf[self.half(p), q] + got

    def piece(self, t, b, zz):
        g = self.g
        src = self.core.at[t] if self.wide else self.core.at[t, :, self.cols(g.s)]
        slot = lax.rem(g.z - zz - 1 + g.Z, g.Z)
        return remote(src, self.zb.at[b, slot], self.z_s.at[0], self.z_r.at[b], g.at(zz))

    def arrived(self, b):
        ref = self.zb.at[b]
        return remote(ref, ref, self.z_s.at[0], self.z_r.at[b], self.g.mate)

    def final(self, b, rows=slice(None)):
        return self.fq.at[b, rows, self.cols(self.g.s)] if self.wide else self.fq.at[b, rows]

    def result(self, b, q, p=None):
        rows, start = (self.R, 0) if p is None else (self.R // 2, p * (self.R // 2))
        if self.above:
            return self.out.at[ds(b * self.R + start, rows), self.cols(q)]
        return self.out.at[pl.ds(start, rows), ds(b * self.D + q * self.C, self.C)]

    def doubling(self, b, p, j):
        g = self.g
        to = (g.s ^ g.order[p][j], g.f)
        out = []
        for m in span(g.order[p][:j]):
            dst = self.result(b, g.s ^ m, p)
            src = self.final(b, self.half(p)) if m == 0 else dst
            out.append(remote(src, dst, self.a_s.at[j], self.a_r.at[b, j], to))
        return out

    def doubled(self, b, j):
        ref = self.out.at[pl.ds(0, self.R), pl.ds(0, self.C << j)]
        return remote(ref, ref, self.a_s.at[j], self.a_r.at[b, j], self.g.mate)

    def stored(self, b):
        return pltpu.make_async_copy(self.final(b), self.result(b, self.g.s), self.o.at[0])

    def ready(self, lo, hi):
        @pl.loop(lo, hi)
        def _(t):
            self.load(t).start()

            @pl.when(t >= self.K)
            def _():
                pl.semaphore_wait(self.free, 1)

            self.swap(t).start()

    def step(self, t):
        g = self.g
        for j in reversed(range(self.after + g.nbits + 1)):
            b, ok = self.due(t - self.tail - self.lag * j)

            @pl.when(ok)
            def _(j=j, b=b):
                if j == 0:
                    self.arrived(b).wait_recv()
                    mine = self.core[self.item_of(b, g.z)] if self.wide else self.core[self.item_of(b, g.z), :, self.cols(g.s)]
                    total = mine.astype(jnp.float32)
                    for k in range(g.Z - 1):
                        total = total + self.zb[b, k].astype(jnp.float32)
                    self.fq[b] = total.astype(self.fq.dtype)
                elif j <= self.after:
                    self.halved(b, j - 1).wait_recv()
                    self.add_halves(self.fq.at[b], b, j - 1)
                else:
                    self.doubled(b, j - self.after - 1).wait_recv()
                if j < self.after:
                    for p in range(2):
                        for cp in self.halving(self.fq.at[b], b, p, j):
                            cp.start()
                elif j < self.after + g.nbits:
                    if j == self.after:
                        self.stored(b).start()
                    for p in range(2):
                        for cp in self.doubling(b, p, j - self.after):
                            cp.start()

        last = 0 if self.wide else g.nbits
        for j in reversed(range(last + 1)):
            u = t - self.lag * j

            @pl.when((u >= 0) & (u < self.n))
            def _(j=j, u=u):
                b, zz = self.where(u)
                buf = self.core.at[u]
                if j == 0:
                    self.load(u).wait()
                    self.swap(u).wait_recv()
                    buf[...] = buf[...] + self.ring[lax.rem(u, self.K)]

                    @pl.when(u + self.K < self.n)
                    def _():
                        pl.semaphore_signal(self.free, inc=1, device_id=g.mate, device_id_type=MESH)
                else:
                    self.halved(u, j - 1).wait_recv()
                    self.add_halves(buf, u, j - 1)
                if j < last:
                    for p in range(2):
                        for cp in self.halving(buf, u, p, j):
                            cp.start()
                else:

                    @pl.when(zz != g.z)
                    def _():
                        self.piece(u, b, zz).start()

    def run(self, lo, hi):
        @pl.loop(lo, hi)
        def _(t):
            self.step(t)

    def finish(self):
        g = self.g

        def done(ref, sem):
            remote(ref, ref, sem, self.z_r.at[0], g.mate).wait_send()

        done(self.core, self.c_s.at[0])
        done(self.zb, self.z_s.at[0])
        for j in range(g.nbits):
            done(self.xb.at[:, :, :, pl.ds(self.offset(j), (g.S >> (j + 1)) * self.C)], self.x_s.at[j])
            done(self.all_of(self.C << j), self.a_s.at[j])
        ref = self.all_of(self.C)
        pltpu.make_async_copy(ref, ref, self.o.at[0]).wait()

    def all_of(self, width):
        return self.out.at[:, pl.ds(0, width if self.above else width * self.NB)]


class VecGather:
    def __init__(self, g, vec, out, sems):
        self.g, self.vec, self.out, self.sems = g, vec, out, sems

    @staticmethod
    def scratch(F):
        return [DMA((3,))]

    def start(self):
        g, sems = self.g, self.sems
        pltpu.make_async_copy(self.vec, self.out.at[g.f], sems.at[2]).start()
        for k in range(1, g.F):
            remote(self.vec, self.out.at[g.f], sems.at[0], sems.at[1], (g.s, lax.rem(g.f + k, g.F))).start()

    def finish(self):
        g, sems = self.g, self.sems
        pltpu.make_async_copy(self.vec, self.out.at[g.f], sems.at[2]).wait()
        ref = self.out.at[pl.ds(0, g.F - 1)]
        cp = remote(ref, ref, sems.at[0], sems.at[1], g.mate)
        cp.wait_send()
        cp.wait_recv()


class VecSum:
    def __init__(self, g, vec, out, refs):
        self.g, self.vec, self.out = g, vec, out
        self.fb, self.mid, self.sb, self.sems = refs

    @staticmethod
    def scratch(S, F, N, L):
        fl = jnp.float32
        return [pltpu.VMEM((F, N, L), fl), pltpu.VMEM((N, L), fl), pltpu.VMEM((S, N, L), fl), DMA((4,))]

    def start(self):
        g = self.g
        for k in range(1, g.F):
            to = lax.rem(g.f + k, g.F)
            remote(self.vec.at[to], self.fb.at[g.f], self.sems.at[0], self.sems.at[1], (g.s, to)).start()

    def middle(self):
        g = self.g
        ref = self.fb.at[pl.ds(0, g.F - 1)]
        cp = remote(ref, ref, self.sems.at[0], self.sems.at[1], g.mate)
        cp.wait_recv()
        total = self.vec[g.f]
        for k in range(1, g.F):
            total = total + self.fb[lax.rem(g.f + k, g.F)]
        self.mid[...] = total
        for k in range(1, g.S):
            remote(self.mid, self.sb.at[g.s], self.sems.at[2], self.sems.at[3], (g.s ^ k, g.f)).start()
        cp.wait_send()

    def finish(self):
        g = self.g
        ref = self.sb.at[pl.ds(0, g.S - 1)]
        cp = remote(ref, ref, self.sems.at[2], self.sems.at[3], g.mate)
        cp.wait_recv()
        total = self.mid[...]
        for k in range(1, g.S):
            total = total + self.sb[g.s ^ k]
        self.out[...] = total
        cp.wait_send()


PARAMS = dict(has_side_effects=True, vmem_limit_bytes=62 * 2**20)


def fp32(x):
    return x.astype(jnp.float32)


def dot(a, b, dims=((1,), (0,))):
    return lax.dot_general(a, b, (dims, ((), ())), preferred_element_type=jnp.float32)


NT = ((1,), (1,))
TN = ((0,), (0,))


def mean_rows(x):
    return jnp.mean(x, axis=-1, keepdims=True)


def head_lanes(rows, hh):
    lane = lax.broadcasted_iota(jnp.int32, (rows, 128), 1)
    mine = (lane >= hh * HEAD_DIM) & (lane < (hh + 1) * HEAD_DIM)
    spare = lane == (1 - hh) * HEAD_DIM
    return mine, spare


def masked_keys(k, length, hh):
    N = k.shape[0]
    mine, spare = head_lanes(N, hh)
    late = lax.broadcasted_iota(jnp.int32, (N, 128), 0) >= length
    return jnp.where(mine, fp32(k), jnp.where(spare & late, NEG_LARGE, 0.0)).astype(jnp.bfloat16)


def scaled_queries(q, hh):
    mine, spare = head_lanes(q.shape[0], hh)
    return jnp.where(mine, fp32(q) * HEAD_DIM ** (-0.5), jnp.where(spare, 1.0, 0.0)).astype(jnp.bfloat16)


def front_kernel(S, F, nwide, QB, lengths, img, vec, wq, wx, wu, wd,
                 first, rest, par, ub, x1, heads_out, out_t, lse, att,
                 vec_full, norm, eb, stage, heads, kh, vt, o_buf, asem, hsem, ssem, rsem, osem, *refs):
    g = Place(S, F)
    slots, T, D = img.shape
    R = first.shape[2]
    V = R
    W = D // S
    N = S * T
    pairs = W // 128
    vg = VecGather(g, vec, vec_full, refs[0])

    def own_first(b, cols):
        if isinstance(cols, slice):
            return wq.at[:, pl.ds(b * D, D)]
        return wq.at[:, pl.ds(pl.multiple_of(b * D + cols.start, 128), cols.size)]

    def own_rest(b0):
        def own(b, cols):
            b = b + b0
            ref, r0, c0 = (wd, b * R, 0) if b < 4 else (wu, 0, (b - 4) * D) if b < 6 else (wx, 0, 0)
            if isinstance(cols, slice):
                return ref.at[pl.ds(r0, R), pl.ds(c0, D)]
            return ref.at[pl.ds(r0, R), pl.ds(pl.multiple_of(c0 + cols.start, 128), cols.size)]

        return own

    entry = Gather(g, 3, 0, own_first, first, refs[1:8], lag=ENTRY_LAG)
    thin = Gather(g, 7 - nwide, nwide, own_rest(nwide), rest, refs[8:15])
    wide = Gather(g, nwide, 0, own_rest(0), rest, refs[15:22], wide=True)

    g.meet()
    vg.start()
    entry.start()
    rows = min(128, T)

    @pl.loop(0, slots * T // rows)
    def _(r):
        i, t = r // (T // rows), lax.rem(r, T // rows)
        x = fp32(img[i, pl.ds(t * rows, rows)])
        x = x - mean_rows(x)
        norm[ds(r * rows, rows)] = x * lax.rsqrt(mean_rows(x * x) + EPSILON)

    entry.kept()
    entry.run(0, entry.nitems)
    vg.finish()
    thin.start()
    wide.start()
    for f in range(F):
        v = fp32(vec_full[f])[:, :V]
        par[:, f * V : (f + 1) * V] = v
        for r in range(2):
            at = (f * 2 + r) * V
            eb[2 * (at // D), :, at % D : at % D + V] = v[2 + r : 3 + r]
        for r in range(4):
            at = (f * 4 + r) * V
            ub[:, at : at + V] = v[8 + r : 9 + r]
    eb[1] = jnp.zeros((1, D), jnp.float32)
    gain, shift = par[0:1], par[1:2]

    @pl.loop(0, slots * T // rows)
    def _(r):
        x1[ds(r * rows, rows)] = (norm[ds(r * rows, rows)] * gain + shift).astype(x1.dtype)

    entry.run(entry.nitems, entry.steps)
    thin.kept()
    wide.kept()
    entry.finish_recv()

    def copy(i, k, j):
        src = stage.at[i, k, j]
        dst = heads.at[j, i, ds(g.s * T, T)]
        return remote(src, dst, ssem.at[i, k, j], rsem.at[i, k, j], (g.s ^ k, g.f))

    def local(i, j):
        return pltpu.make_async_copy(stage.at[i, 0, j], heads.at[j, i, ds(g.s * T, T)], ssem.at[i, 0, j])

    def project(i):
        @pl.loop(0, S * 3)
        def _(n):
            k = lax.rem(1 + n // 3, S)
            j = lax.rem(n, 3)
            cols = ds((g.s ^ k) * W, W)
            w = first[:, j, :, cols].reshape(D, W)
            out = dot(x1[i * T : (i + 1) * T], w) + eb[j, :, cols]
            stage[i, k, j] = out.astype(stage.dtype)

            @pl.when(k != 0)
            def _():
                copy(i, k, j).start()

            @pl.when(k == 0)
            def _():
                local(i, j).start()

    def projected(i):
        for j in range(3):
            local(i, j).wait()
            for k in range(1, S):
                copy(i, k, j).wait_send()
                dst = heads.at[j, i, ds((g.s ^ k) * T, T)]
                remote(dst, dst, ssem.at[i, k, j], rsem.at[i, k, j], (g.s ^ k, g.f)).wait_recv()
        keep_heads(i).start()

    def keep_heads(i):
        return pltpu.make_async_copy(heads.at[:, i], heads_out.at[:, i], hsem.at[i])

    def out_copy(i, hp, kk):
        e = i * pairs + hp
        dst = att.at[i, :, pl.ds(pl.multiple_of(g.s * W + hp * 128, 128), 128)]
        if kk == 0:
            return pltpu.make_async_copy(o_buf.at[e, ds(g.s * T, T)], dst, osem.at[0, e, 0])
        return remote(o_buf.at[e, ds((g.s ^ kk) * T, T)], dst, osem.at[0, e, kk], osem.at[1, e, kk], (g.s ^ kk, g.f))

    def attend(i, hp):
        e = i * pairs + hp
        lanes = slice(hp * 128, (hp + 1) * 128)
        vt[...] = heads[2, i, :, lanes].T
        for hh in range(2):
            kh[hh] = masked_keys(heads[1, i, :, lanes], lengths[i], hh)

        @pl.loop(0, N // QB)
        def _(b):
            cols = ds(b * QB, QB)
            qb = heads[0, i, cols, lanes]
            for hh in range(2):
                sc = dot(kh[hh], scaled_queries(qb, hh), NT)
                top = jnp.max(sc, axis=0, keepdims=True)
                ex = jnp.exp(sc - top)
                total = jnp.sum(ex, axis=0, keepdims=True)
                w = (ex * (1.0 / total)).astype(jnp.bfloat16)
                o = dot(vt[hh * HEAD_DIM : (hh + 1) * HEAD_DIM], w).astype(jnp.bfloat16)
                at = hp * 128 + hh * HEAD_DIM
                out_t[i, at : at + HEAD_DIM, cols] = o
                lse[i, hp, hh : hh + 1, cols] = top + jnp.log(total)
            background(e * (N // QB) + b)

        o_buf[e] = out_t[i, lanes].T
        for kk in list(range(1, S)) + [0]:
            out_copy(i, hp, kk).start()

    units = [(i, hp) for i in range(slots) for hp in range(pairs)]
    early = thin.steps // EARLY
    per_unit = -(-(thin.steps - early) // (len(units) * (N // QB)))

    def background(n):
        @pl.when(n < wide.steps)
        def _():
            wide.step(n)

        for m in range(per_unit):
            thin.step(early + n * per_unit + m)

    for i in range(slots):
        project(i)
    thin.run(0, early)
    entry.finish_send()
    for n, (i, hp) in enumerate(units):
        if hp == 0:
            projected(i)
        attend(i, hp)
    wide.run(len(units) * (N // QB), wide.steps)
    for gather in (thin, wide):
        gather.finish_recv()
        gather.finish_send()
    for i, hp in units:
        for kk in range(S):
            cp = out_copy(i, hp, kk)
            if kk == 0:
                cp.wait()
            else:
                cp.wait_send()
                cp.wait_recv()
    for i in range(slots):
        keep_heads(i).wait()


ENTRY_LAG = 6
WIDE = 3
EARLY = 10


def front_call(S, F, cid, lengths, img, vec, wq, wx, wu, wd):
    slots, T, D = img.shape
    R, FF = wq.shape[0], wu.shape[1]
    W, N = D // S, S * T
    pairs = W // 128
    bf, fl = jnp.bfloat16, jnp.float32
    out = jax.ShapeDtypeStruct
    return pl.pallas_call(
        functools.partial(front_kernel, S, F, WIDE, min(256, N)),
        out_shape=[
            out((F, 3, R, D), bf), out((F, 7, R, D), bf), out((16, D), fl), out((1, FF), fl), out((slots * T, D), bf),
            out((3, slots, N, W), bf), out((slots, W, N), bf), out((slots, pairs, 8, N), fl), out((slots, T, D), bf),
        ],
        in_specs=[pl.BlockSpec(memory_space=pltpu.SMEM), VM, ANY, ANY, ANY, ANY, ANY],
        out_specs=[VM, ANY, VM, VM, VM, ANY, VM, VM, ANY],
        scratch_shapes=[
            pltpu.VMEM((F, 16, 128), bf), pltpu.VMEM((slots * T, D), fl), pltpu.VMEM((3, 1, D), fl), pltpu.VMEM((slots, S, 3, T, W), bf),
            pltpu.VMEM((3, slots, N, W), bf), pltpu.VMEM((2, N, 128), bf), pltpu.VMEM((128, N), bf),
            pltpu.VMEM((slots * pairs, N, 128), bf), DMA((1,)), DMA((slots,)), DMA((slots, S, 3)), DMA((slots, S, 3)),
            DMA((2, slots * pairs, S)),
        ]
        + VecGather.scratch(F)
        + Gather.scratch(S, F, 3, R, D, bounce=False)
        + Gather.scratch(S, F, 7 - WIDE, R, D)
        + Gather.scratch(S, F, WIDE, R, D),
        compiler_params=pltpu.CompilerParams(collective_id=cid, **PARAMS),
        name="front",
    )(lengths, img, vec, wq, wx, wu, wd)


def rear_kernel(S, F, QB, lengths, held, img, cot, att, par, ub, wu_own, wts, heads, out_t, lse, x1, first,
                layer, dx, small, part_down, part_up, g_down, g_up, g_first, back, late,
                cots, vecs, ubg, slab, csem, esem, wsem, psem, hsem, *refs):
    g = Place(S, F)
    slots, T, D = img.shape
    M = slots * T
    W = D // S
    N = S * T
    pairs = W // 128
    R = wts.shape[2]
    H = ub.shape[2]
    rows = min(128, T)
    nrows = M // rows
    exit_bias, scale1, gain2, shift2 = par[4:5], par[5:6], par[6:7], par[7:8]
    down_bias, scale2 = par[12:13], par[13:14]
    per_block = D // H
    bf, fl = jnp.bfloat16, jnp.float32
    down_sum = Scatter(g, part_down, g_down, refs[:16], per=4, lag=LAG, above=True)
    up_sum = Scatter(g, part_up, g_up, refs[16:32], wide=True, lag=4, tail=UP_TAIL)
    vsum = VecSum(g, slab, small, refs[48:52])

    def own_late(b, cols):
        if isinstance(cols, slice):
            return wu_own.at[:, pl.ds((2 + b) * D, D)]
        return wu_own.at[:, pl.ds(pl.multiple_of((2 + b) * D + cols.start, 128), cols.size)]

    more = Gather(g, 2, 0, own_late, late, refs[52:59])
    units = slots * pairs
    chunks = F // 4
    done = (F - chunks - 2) * g.Z // chunks

    def place(r):
        return r // (T // rows), lax.rem(r, T // rows) * rows

    def mask(r):
        i, t = place(r)
        limit = jnp.where(i < held[g.f], lengths[i], 0)
        pos = lax.broadcasted_iota(jnp.int32, (rows, 1), 0) + (g.s * T + t)
        return jnp.where(pos < limit, 1.0, 0.0)

    def upstream(r):
        i, t = place(r)
        return mask(r) * fp32(cot[i, pl.ds(t, rows)])

    def cot_copies(stage, k):
        for i in range(slots):
            src, dst = stage.at[pl.ds(i * T, T), pl.ds(k * W, W)], cots.at[i, ds(g.s * T, T)]
            if k == 0:
                yield pltpu.make_async_copy(src, dst, csem.at[0, 0])
            else:
                yield remote(src, dst, csem.at[0, k], csem.at[1, k], (g.s ^ k, g.f))

    def feed_forward(mixed, x2, x2t, dcot, down, cot2, wu, wd, wx, dwu, dwd):
        def up_load(j):
            cols = pl.ds(pl.multiple_of(lax.rem(j, per_block) * H, H), H)
            slot = lax.rem(j, 2)
            block = j // per_block
            soon = pltpu.make_async_copy(wts.at[:, 4 + jnp.minimum(block, 1), :, cols], wu.at[slot], wsem.at[0, slot])
            return soon, pltpu.make_async_copy(late.at[:, jnp.maximum(block - 2, 0), :, cols], wu.at[slot], wsem.at[0, slot])

        def start_up(j):
            soon, later = up_load(j)

            @pl.when(j < F // 2)
            def _():
                soon.start()

            @pl.when(j >= F // 2)
            def _():
                later.start()

        def down_load(j):
            return pltpu.make_async_copy(wts.at[j, pl.ds(0, 4)], wd.at[lax.rem(j, 2)], wsem.at[1, lax.rem(j, 2)])

        def put_up(j):
            cols = pl.ds(pl.multiple_of(lax.rem(j, per_block) * H, H), H)
            return pltpu.make_async_copy(dwu, part_up.at[:, j // per_block, :, cols], psem.at[0])

        def put_down(j):
            return pltpu.make_async_copy(dwd, part_down.at[j, pl.ds(0, 4)], psem.at[1])

        x_load = pltpu.make_async_copy(wts.at[:, 6], wx, wsem.at[2, 0])
        x_load.start()
        start_up(0)
        down_load(0).start()
        more.kept()
        x_load.wait()
        mixed[...] = dot(att[...], wx[...].reshape(D, D)) + exit_bias

        def residual(r, sl):
            i, t = place(r)
            return fp32(img[i, pl.ds(t, rows)]) + scale1 * mixed[sl]

        def norm(res):
            res = res - mean_rows(res)
            inv = lax.rsqrt(mean_rows(res * res) + EPSILON)
            return res * inv, inv

        @pl.loop(0, nrows)
        def _(r):
            sl = ds(r * rows, rows)
            n, _ = norm(residual(r, sl))
            x2[sl] = (n * gain2 + shift2).astype(bf)
            dcot[sl] = (upstream(r) * scale2).astype(bf)

        x2t[...] = x2[...].T
        down[...] = jnp.zeros_like(down)
        cot2[...] = jnp.zeros_like(cot2)

        @pl.loop(0, F)
        def _(j):
            slot = lax.rem(j, 2)
            every = -(-more.steps // (F // 2 - 1))

            @pl.when(j < F // 2 - 1)
            def _():
                more.run(j * every, (j + 1) * every)

            @pl.when(j == F // 2 - 1)
            def _():
                more.finish_recv()

            @pl.when(j + 1 < F)
            def _():
                start_up(j + 1)
                down_load(j + 1).start()

            up_load(j)[0].wait()
            down_load(j).wait()
            wu_j = wu[slot].reshape(D, H)
            wd_j = wd[slot].reshape(H, D)
            pre = dot(x2[...], wu_j) + ub[j]
            cumul = 0.5 * (1.0 + lax.erf(pre * (1.0 / math.sqrt(2.0))))
            density = jnp.exp(-0.5 * pre * pre) * (1.0 / math.sqrt(2.0 * math.pi))
            act = (pre * cumul).astype(bf)
            slope = cumul + pre * density
            pre_cot = dot(dcot[...], wd_j, NT) * slope
            ubg[j] = jnp.sum(pre_cot, axis=0, keepdims=True)
            low = pre_cot.astype(bf)
            @pl.when(j > 0)
            def _():
                put_up(j - 1).wait()
                put_down(j - 1).wait()

            @pl.when((j > 0) & (lax.rem(j, chunks) == 0))
            def _():
                n = (j // chunks - 1) * g.Z
                up_sum.ready(n, n + g.Z)
                down_sum.ready(n, n + g.Z)

            dwu[...] = dot(x2t[...], low).astype(bf).reshape(F, R, H)
            dwd[...] = dot(act, dcot[...], TN).astype(bf).reshape(4, R, D)
            put_up(j).start()
            put_down(j).start()
            down[...] += dot(act, wd_j)
            cot2[...] += dot(low, wu_j, NT)

            @pl.when((j > chunks) & (j < F - 1))
            def _():
                first = (j - chunks - 1) * g.Z // chunks
                up_sum.run(first, first + g.Z // chunks)
                down_sum.run(first, first + g.Z // chunks)

        put_up(F - 1).wait()
        put_down(F - 1).wait()
        n = 3 * g.Z
        up_sum.ready(n, n + g.Z)
        down_sum.ready(n, n + g.Z)
        vecs[...] = jnp.zeros_like(vecs)

        @pl.loop(0, nrows)
        def _(r):
            sl = ds(r * rows, rows)
            m = mask(r)
            up = upstream(r)
            out = down[sl] + down_bias
            res = residual(r, sl)
            layer[sl] = (m * (res + scale2 * out)).astype(bf)
            n, inv = norm(res)
            c2 = cot2[sl]
            c = c2 * gain2
            rc = up + inv * (c - mean_rows(c) - n * mean_rows(c * n))
            dx[sl] = rc
            mc = rc * scale1
            x2[sl] = mc.astype(bf)
            total = lambda v: jnp.sum(v, axis=0, keepdims=True)
            vecs[0:1] += total(up * out)
            vecs[1:2] += total(up * scale2)
            vecs[2:3] += total(c2 * n)
            vecs[3:4] += total(c2)
            vecs[4:5] += total(rc * mixed[sl])
            vecs[5:6] += total(mc)

        for k in list(range(1, S)) + [0]:
            dcot[:, k * W : (k + 1) * W] = dot(x2[...], wx_rows(wx, g.s ^ k, W), NT).astype(bf)
            for cp in cot_copies(dcot, k):
                cp.start()
        for n in range(F // 4):
            at = n * 4 * R
            dwd[...] = dot(att[:, at : at + 4 * R], x2[...], TN).astype(bf).reshape(4, R, D)
            put_x = pltpu.make_async_copy(dwd, part_down.at[pl.ds(n * 4, 4), 4], psem.at[2])
            put_x.start()
            put_x.wait()
        up_sum.run(done, 3 * g.Z)
        down_sum.run(done, 3 * g.Z)
        down_sum.ready(4 * g.Z, 5 * g.Z)
        for k in range(S):
            for cp in cot_copies(dcot, k):
                if k == 0:
                    cp.wait()
        ref = dcot.at[:, pl.ds(0, W)]
        for k in range(1, S):
            remote(ref, ref, csem.at[0, k], csem.at[1, k], g.mate).wait_send()

    polls = units * (N // QB)

    def background(n):
        @pl.when(3 * g.Z + n < up_sum.steps)
        def _():
            up_sum.step(3 * g.Z + n)

        down_sum.step(3 * g.Z + n)

    def attend_back(hd, ot, ls, kh, vh, kt, cot_t, delta, dq_t, dk, dv, stage):
        loads = [pltpu.make_async_copy(a, b, hsem.at[n]) for n, (a, b) in enumerate(((heads, hd), (out_t, ot), (lse, ls)))]
        for cp in loads:
            cp.start()
        for k in range(1, S):
            ref = cots.at[:, ds((g.s ^ k) * T, T)]
            remote(ref, ref, csem.at[0, k], csem.at[1, k], (g.s ^ k, g.f)).wait_recv()
        for cp in loads:
            cp.wait()

        def copy(e, j, kk):
            i, hp = e // pairs, lax.rem(e, pairs)
            dst = back.at[i, :, ds(j * D + g.s * W + hp * 128, 128)]
            src = stage.at[e, j, ds((g.s ^ kk) * T, T)]
            if kk == 0:
                return pltpu.make_async_copy(src, dst, esem.at[2])
            return remote(src, dst, esem.at[0], esem.at[1], (g.s ^ kk, g.f))

        @pl.loop(0, units)
        def _(e):
            i, hp = e // pairs, lax.rem(e, pairs)
            lanes = ds(hp * 128, 128)
            length = lengths[i]
            kt[...] = hd[1, i, :, lanes].T
            cot_t[...] = cots[i, :, lanes].T
            prod = fp32(cot_t[...]) * fp32(ot[i, lanes])
            for hh in range(2):
                hs = slice(hh * HEAD_DIM, (hh + 1) * HEAD_DIM)
                delta[hh : hh + 1] = jnp.sum(prod[hs], axis=0, keepdims=True)
                kh[hh] = masked_keys(hd[1, i, :, lanes], length, hh)
                mine, _ = head_lanes(N, hh)
                vh[hh] = jnp.where(mine, fp32(hd[2, i, :, lanes]), 0.0).astype(bf)
            dk[...] = jnp.zeros_like(dk)
            dv[...] = jnp.zeros_like(dv)

            @pl.loop(0, N // QB)
            def _(b):
                cols = ds(b * QB, QB)
                qb, cb = hd[0, i, cols, lanes], cots[i, cols, lanes]
                for hh in range(2):
                    hs = slice(hh * HEAD_DIM, (hh + 1) * HEAD_DIM)
                    mine, _ = head_lanes(QB, hh)
                    qs = scaled_queries(qb, hh)
                    prob = jnp.exp(dot(kh[hh], qs, NT) - ls[i, hp, hh : hh + 1, cols])
                    sg = dot(vh[hh], cb, NT)
                    sc = (prob * (sg - delta[hh : hh + 1, cols])).astype(bf)
                    w = prob.astype(bf)
                    dv[...] += dot(w, jnp.where(mine, fp32(cb), 0.0).astype(bf))
                    dk[...] += dot(sc, jnp.where(mine, fp32(qs), 0.0).astype(bf))
                    dq_t[hs, cols] = (dot(kt[hs], sc) * HEAD_DIM ** (-0.5)).astype(bf)
                background(e * (N // QB) + b)

            stage[e, 0] = dq_t[...].T
            stage[e, 1] = dk[...].astype(bf)
            stage[e, 2] = dv[...].astype(bf)
            for j in range(3):
                for kk in list(range(1, S)) + [0]:
                    copy(e, j, kk).start()

        ref = stage.at[:, :, pl.ds(0, (S - 1) * T)]
        cp = remote(ref, ref, esem.at[0], esem.at[1], g.mate)
        cp.wait_send()
        cp.wait_recv()
        ref = stage.at[:, :, pl.ds(0, T)]
        pltpu.make_async_copy(ref, ref, esem.at[2]).wait()

    def entry(part, ein, win, x1v, x1t, acc, rows_v):
        entry_sum = Scatter(g, part, g_first, refs[32:48])
        loads = [pltpu.make_async_copy(back.at[:, :, pl.ds(j * D, D)], ein.at[j], hsem.at[j]) for j in range(3)]
        weights = [pltpu.make_async_copy(first.at[:, j], win.at[j % 2], wsem.at[2, j % 2]) for j in range(3)]
        x_load = pltpu.make_async_copy(x1, x1v, wsem.at[0, 0])
        for cp in [x_load] + loads + weights[:2]:
            cp.start()
        x_load.wait()
        x1t[...] = x1v[...].T
        at = 3 * g.Z + polls

        def others(n, k):
            for t in range(at + n, at + n + k):
                up_sum.step(t)
                down_sum.step(t)

        rows_v[...] = jnp.zeros_like(rows_v)
        cot_of = lambda j: ein[j].reshape(M, D)
        for j in range(3):
            loads[j].wait()
            part[:, j] = dot(x1t[...], cot_of(j)).astype(bf).reshape(F, R, D)
            if j:
                entry_sum.run((j - 1) * g.Z, j * g.Z)
            entry_sum.ready(j * g.Z, (j + 1) * g.Z)
            others(2 * j, 2)
        for j in range(3):
            weights[j].wait()
            d = dot(cot_of(j), win[j % 2].reshape(D, D), NT)
            if j == 0:
                weights[2].start()
                acc[...] = d
            else:
                acc[...] += d
            others(6 + 2 * j, 2)
            entry_sum.run(2 * g.Z + j, 2 * g.Z + j + 1)
        rows_v[2:3] = jnp.sum(fp32(cot_of(0)), axis=0, keepdims=True)
        rows_v[3:4] = jnp.sum(fp32(cot_of(2)), axis=0, keepdims=True)
        gain = par[0:1]

        @pl.loop(0, nrows)
        def _(r):
            sl = ds(r * rows, rows)
            i, t = place(r)
            x = fp32(img[i, pl.ds(t, rows)])
            x = x - mean_rows(x)
            inv = lax.rsqrt(mean_rows(x * x) + EPSILON)
            n = x * inv
            d1 = acc[sl]
            c = d1 * gain
            dx[sl] = dx[sl] + inv * (c - mean_rows(c) - n * mean_rows(c * n))
            rows_v[0:1] += jnp.sum(d1 * n, axis=0, keepdims=True)
            rows_v[1:2] += jnp.sum(d1, axis=0, keepdims=True)
            entry_sum.step(2 * g.Z + 3 + r)

        slab[...] = jnp.zeros_like(slab)
        own = [(0, rows_v, 0), (1, rows_v, 1), (4, vecs, 5), (5, vecs, 4), (6, vecs, 2), (7, vecs, 3), (12, vecs, 1), (13, vecs, 0)]
        V = R
        for f in range(F):
            for to, src, r in own:
                slab[f, to : to + 1, :V] = src[r : r + 1, f * V : (f + 1) * V]
            for r in range(2):
                p = (f * 2 + r) * V
                slab[f, 2 + r : 3 + r, :V] = rows_v[2 + p // D : 3 + p // D, p % D : p % D + V]
            for r in range(4):
                slab[f, 8 + r : 9 + r, :V] = ubg[f, :, r * V : (r + 1) * V]
        vsum.start()
        mark = 2 * g.Z + 3 + nrows
        entry_sum.run(mark, mark + 4)
        vsum.middle()
        left = max(down_sum.steps, up_sum.steps) - (at + 12)

        @pl.loop(0, max(left, entry_sum.steps - mark - 4))
        def _(t):
            up_sum.step(at + 12 + t)
            down_sum.step(at + 12 + t)
            entry_sum.step(mark + 4 + t)

        entry_sum.finish()

    g.meet()
    more.start()
    v = pltpu.VMEM
    pl.run_scoped(
        feed_forward, v((M, D), fl), v((M, D), bf), v((D, M), bf), v((M, D), bf), v((M, D), fl), v((M, D), fl),
        v((2, F, R, H), bf), v((2, 4, R, D), bf), v((F, R, D), bf), v((F, R, H), bf), v((4, R, D), bf),
    )
    pl.run_scoped(
        attend_back, v((3, slots, N, W), bf), v((slots, W, N), bf), v((slots, pairs, 8, N), fl), v((2, N, 128), bf),
        v((2, N, 128), bf), v((128, N), bf), v((128, N), bf), v((8, N), fl), v((128, N), bf), v((N, 128), fl),
        v((N, 128), fl), v((units, 3, N, 128), bf),
    )
    pl.run_scoped(
        entry, v((F, 3, R, D), bf), v((3, slots, T, D), bf), v((2, F, R, D), bf), v((M, D), bf), v((D, M), bf),
        v((M, D), fl), v((8, D), fl),
    )
    up_sum.finish()
    down_sum.finish()
    vsum.finish()
    more.finish_send()


def wx_rows(wx, peer, W):
    F, R, D = wx.shape
    n = W // R
    return wx[pl.ds(peer * n, n)].reshape(W, D)


LAG = 4
UP_TAIL = 17


def rear_call(S, F, cid, lengths, held, img, cot, att, par, ub, wu_own, wts, heads, out_t, lse, x1, first):
    slots, T, D = img.shape
    M = slots * T
    R = wts.shape[2]
    FF = ub.shape[1]
    H = FF // F
    W, N = D // S, S * T
    bf, fl = jnp.bfloat16, jnp.float32
    SM = pl.BlockSpec(memory_space=pltpu.SMEM)
    out, v = jax.ShapeDtypeStruct, pltpu.VMEM
    return pl.pallas_call(
        functools.partial(rear_kernel, S, F, min(256, N)),
        out_shape=[
            out((M, D), bf), out((M, D), fl), out((16, 128), fl), out((F, 5, R, D), bf), out((F, 4, R, D), bf),
            out((5 * R, D), bf), out((R, 4 * D), bf), out((R, 3 * D), bf), out((slots, T, 3 * D), bf), out((F, 2, R, D), bf),
        ],
        in_specs=[SM, SM, VM, VM, VM, VM, VM] + [ANY] * 7,
        out_specs=[VM, VM, VM] + [ANY] * 7,
        scratch_shapes=[v((slots, N, W), bf), v((8, D), fl), v((F, 1, H), fl), v((F, 16, 128), fl),
                        DMA((2, S)), DMA((3,)), DMA((3, 2)), DMA((3,)), DMA((3,))]
        + Scatter.scratch(S, F, 5, R, D, K=F)
        + Scatter.scratch(S, F, 4, R, D, wide=True, K=F)
        + Scatter.scratch(S, F, 3, R, D, K=F // 2)
        + VecSum.scratch(S, F, 16, 128)
        + Gather.scratch(S, F, 2, R, D),
        compiler_params=pltpu.CompilerParams(collective_id=cid, **PARAMS),
        name="rear",
    )(lengths, held, img, cot, att, par, ub.reshape(F, 1, H), wu_own, wts, heads, out_t, lse, x1, first)


def body(S, F, images, out_grad, lengths, images_held, first_gain, first_shift, entry_weight, entry_bias, exit_weight,
         exit_bias, first_scale, second_gain, second_shift, up_weight, up_bias, down_weight, down_bias, second_scale):
    slots, T, D = images.shape
    M = slots * T
    R = entry_weight.shape[0]
    FF = up_weight.shape[1]
    fl = jnp.float32
    V = R
    rows = [first_gain, first_shift, entry_bias, exit_bias, first_scale, second_gain, second_shift, up_bias, down_bias, second_scale]
    own_vec, at = jnp.zeros((16, 128), jnp.bfloat16), 0
    for v in rows:
        n = v.shape[0] // V
        own_vec = own_vec + jnp.pad(v.reshape(n, V), ((at, 16 - at - n), (0, 128 - V)))
        at += n
    first, rest, par, ub, x1, heads, out_t, lse, att = front_call(
        S, F, 0, lengths, images, own_vec, entry_weight, exit_weight, up_weight, down_weight
    )
    layer, dx, small, _, _, g_down, g_up, g_first, _, _ = rear_call(
        S, F, 1, lengths, images_held, images, out_grad, att.reshape(M, D), par, ub, up_weight, rest, heads, out_t, lse, x1, first
    )
    small = small[:, :V]
    row = lambda n, m=1: small[n : n + m].reshape(m * V)
    g_first, g_down, g_up = g_first.astype(fl), g_down.astype(fl), g_up.astype(fl)
    return (
        layer.reshape(slots, T, D),
        dx.reshape(slots, T, D),
        row(0),
        row(1),
        g_first,
        row(2, 2),
        g_down[4 * R :],
        row(4),
        row(5),
        row(6),
        row(7),
        g_up,
        row(8, 4),
        g_down[: 4 * R],
        row(12),
        row(13),
    )


def solution(mesh):
    S, F = mesh.shape["seq"], mesh.shape["fsdp"]
    vector, matrix, tokens = P("fsdp"), P("fsdp", None), P("fsdp", "seq", None)
    return jax.shard_map(
        functools.partial(body, S, F),
        mesh=mesh,
        in_specs=(tokens, tokens, vector, P(), vector, vector, matrix, vector, matrix, vector, vector, vector, vector,
                  matrix, vector, matrix, vector, vector),
        out_specs=(tokens, tokens, vector, vector, matrix, vector, matrix, vector, vector, vector, vector, matrix, vector,
                   matrix, vector, vector),
        check_vma=False,
    )
```

time: 433 us -> 350 us (0.81)
  Pallas kernels: 409 us -> 334 us
  local copies, waits for them, and re-layouts: 18.4 us -> 11 us
    pallas_call x5 -> x1, Pallas kernels: 279 us -> 213 us  [rear_call(): pl.pallas_call(functools.partial(rear_kernel, S, F, min(256, N)), out_sha...]
    pallas_call x1, Pallas kernels: 129 us -> 121 us  [front_call(): pl.pallas_call(functools.partial(front_kernel, S, F, WIDE, min(256, N)),...]
    unnamed x15 -> x10, local copies, waits for them, and re-layouts: 7.76 us -> 2.3 us
where the time goes in v3:
time: 350 us
  Pallas kernels  334 us (95%)
  local copies, waits for them, and re-layouts  11 us (3%)
  other arithmetic  4.22 us (1%)
    pallas_call x1, Pallas kernels, rear_call(): pl.pallas_call(functools.partial(rear_kernel, S, F, min(256, N)), out_sha...  213 us
    pallas_call x1, Pallas kernels, front_call(): pl.pallas_call(functools.partial(front_kernel, S, F, WIDE, min(256, N)),...  121 us

profile of v3, /device:TPU:0, one launch (start us, length us, event | category | flops | bytes accessed | tf_op | source)
XLA Modules:
  0.0 349.9 jit_solution(12187058686327979954)
XLA Ops:
  0.6 1.4 pad_add_fusion.vec
  2.1 121.3 %front.1 = (bf16[8,3,128,1024]{3,2,1,0:T(8,128)(2,1)}, bf16[8,7,128,1024]{3,2,1,0:T(8,128)(2,1)}, f32[16,1024]{1,0:T(8,128)}, f32[1,4096]{1,0:T(1,128)}, bf16[51...) custom-call(s32[2]{0:T(128)} %lengths.3, ...), custom_call_target="tpu_custom_call" | custom-call | tf_op jit(solution)/shard_map/front/pallas_call | solution.py:735
  123.4 212.6 %rear.1 = (bf16[512,1024]{1,0:T(8,128)(2,1)}, f32[512,1024]{1,0:T(8,128)}, f32[16,128]{1,0:T(8,128)}, bf16[8,5,128,1024]{3,2,1,0:T(8,128)(2,1)}, bf16[8,4,128,10...) custom-call(s32[2]{0:T(128)} %lengths.3, s32[8]{0:T(128)} %held.1, ...), custom_call_target="tpu_custom_call" | custom-call | tf_op jit(solution)/shard_map/rear/pallas_call | solution.py:1168
  336.0 0.0 copy-start.3
  336.0 1.3 slice_bitcast_fusion.1
  337.4 1.3 slice_bitcast_fusion
  338.6 1.4 slice_bitcast_fusion.2
  340.1 1.8 slice.48
  341.9 0.0 copy-start.1
  341.9 2.9 slice.49
  344.7 0.0 copy-done.3
  344.7 0.0 copy-start.2
  344.7 1.3 convert_element_type.29
  346.0 0.0 copy-done.1
  346.0 0.0 copy-start
  346.0 1.5 convert_element_type.31
  347.6 0.0 copy-done.2
  347.6 1.0 copy.36
  348.5 0.0 copy-done
  348.5 1.3 copy.37
Async XLA Ops:
  336.0 8.7 %copy-start.3 = (bf16[128,3072]{1,0:T(8,128)(2,1)S(1)}, bf16[128,3072]{1,0:T(8,128)(2,1)}, u32[]{:S(2)}) copy-start(bf16[128,3072]{1,0:T(8,128)(2,1)} %get-tuple-element.43) | copy-start | bytes 2359300
  341.9 4.2 %copy-start.1 = (bf16[128,4096]{1,0:T(8,128)(2,1)S(1)}, bf16[128,4096]{1,0:T(8,128)(2,1)}, u32[]{:S(2)}) copy-start(bf16[128,4096]{1,0:T(8,128)(2,1)} %get-tuple-element.45) | copy-start | bytes 3145732
  344.7 2.8 copy-start.2
  346.0 2.5 copy-start

commit v4 on v3

--- a/solution.py
+++ b/solution.py
@@ -25,8 +25,8 @@
 
 
 class Place:
-    def __init__(self, S, F):
-        self.S, self.F, self.Z = S, F, F // 2
+    def __init__(self, S, F, slots):
+        self.S, self.F, self.Z, self.slots = S, F, F // 2, slots
         self.bits = [1 << b for b in range(S.bit_length() - 1)]
         self.nbits = len(self.bits)
         self.order = [self.bits, self.bits[1:] + self.bits[:1]]
@@ -34,20 +34,94 @@
         self.f = lax.axis_index("fsdp")
         self.z, self.c = self.f // 2, lax.rem(self.f, 2)
         self.mate = (self.s, self.f ^ 1)
+        self.regroup = whole_images(S, slots)
+        self.n = 2 if self.regroup else S
+        self.me = self.c if self.regroup else self.s
+        self.images = 1 if self.regroup else slots
 
     def at(self, zz):
         return (self.s, zz * 2 + self.c)
+
+    def peer(self, k):
+        return (self.s, self.f ^ k) if self.regroup else (self.s ^ k, self.f)
+
+    def image(self, i):
+        if self.regroup:
+            return self.z * 2 + self.s // self.slots, lax.rem(self.s, self.slots)
+        return self.f, i
+
+    def goes(self, i):
+        if not self.regroup:
+            return self.mate, i, True
+        to, core = self.c * self.slots + i, self.s // self.slots
+        return (to, self.z * 2 + core), lax.rem(self.s, self.slots), (to == self.s) & (core == self.c)
+
+    def came(self, r):
+        if not self.regroup:
+            return self.mate, r, True
+        of, core = self.c * self.slots + r, self.s // self.slots
+        return (of, self.z * 2 + core), lax.rem(self.s, self.slots), (of == self.s) & (core == self.c)
 
     def greet(self):
         bar = pltpu.get_barrier_semaphore()
         for k in range(1, self.F):
             pl.semaphore_signal(bar, inc=1, device_id=(self.s, lax.rem(self.f + k, self.F)), device_id_type=MESH)
         for k in range(1, self.S):
-            pl.semaphore_signal(bar, inc=1, device_id=(self.s ^ k, self.f), device_id_type=MESH)
-        return lambda: pl.semaphore_wait(bar, self.F + self.S - 2)
+            for core in range(2 if self.regroup else 1):
+                pl.semaphore_signal(bar, inc=1, device_id=(self.s ^ k, self.f ^ core), device_id_type=MESH)
+        return lambda: pl.semaphore_wait(bar, self.F - 1 + (self.S - 1) * (2 if self.regroup else 1))
 
     def meet(self):
         self.greet()()
+
+
+def whole_images(S, slots):
+    return S == 2 * slots
+
+
+class Regroup:
+    def __init__(self, g, src, dst, sems, back=False):
+        self.g, self.src, self.dst, self.sems = g, src, dst, sems
+        self.out, self.into = (g.came, g.goes) if back else (g.goes, g.came)
+
+    @staticmethod
+    def scratch(slots):
+        return [DMA((2, slots))]
+
+    def each(self, way, local, remote_part):
+        for p in range(self.g.slots):
+            device, q, here = way(p)
+            if here is True:
+                local(p, q)
+            else:
+                pl.when(here)(lambda p=p, q=q: local(p, q))
+                pl.when(jnp.logical_not(here))(lambda p=p, q=q, device=device: remote_part(p, q, device))
+
+    def start(self):
+        def local(p, q):
+            pltpu.make_async_copy(self.src(p), self.dst(q), self.sems.at[0, p]).start()
+
+        def away(p, q, device):
+            remote(self.src(p), self.dst(q), self.sems.at[0, p], self.sems.at[1, q], device).start()
+
+        self.each(self.out, local, away)
+
+    def arrived(self):
+        def away(p, q, device):
+            remote(self.dst(p), self.dst(p), self.sems.at[0, p], self.sems.at[1, p], device).wait_recv()
+
+        self.each(self.into, lambda p, q: None, away)
+
+        def local(p, q):
+            pltpu.make_async_copy(self.src(p), self.dst(q), self.sems.at[0, p]).wait()
+
+        self.each(self.out, local, lambda p, q, device: None)
+
+    def sent(self):
+        def away(p, q, device):
+            remote(self.src(p), self.dst(p), self.sems.at[0, p], self.sems.at[1, p], device).wait_send()
+
+        self.each(self.out, lambda p, q: None, away)
 
 
 def span(bits):
@@ -531,10 +605,16 @@
     return mine, spare
 
 
+def length_of(par, group, slot, V):
+    lane = lax.broadcasted_iota(jnp.int32, (1, par.shape[1]), 1)
+    value = par[14:15] * 32.0 + par[15:16]
+    return jnp.sum(jnp.where(lane == group * V + slot, value, 0.0), axis=1, keepdims=True)
+
+
 def masked_keys(k, length, hh):
     N = k.shape[0]
     mine, spare = head_lanes(N, hh)
-    late = lax.broadcasted_iota(jnp.int32, (N, 128), 0) >= length
+    late = fp32(lax.broadcasted_iota(jnp.int32, (N, 128), 0)) >= length
     return jnp.where(mine, fp32(k), jnp.where(spare & late, NEG_LARGE, 0.0)).astype(jnp.bfloat16)
 
 
@@ -543,16 +623,19 @@
     return jnp.where(mine, fp32(q) * HEAD_DIM ** (-0.5), jnp.where(spare, 1.0, 0.0)).astype(jnp.bfloat16)
 
 
-def front_kernel(S, F, nwide, QB, lengths, img, vec, wq, wx, wu, wd,
-                 first, rest, par, ub, x1, heads_out, out_t, lse, att,
-                 vec_full, norm, eb, stage, heads, kh, vt, o_buf, asem, hsem, ssem, rsem, osem, *refs):
-    g = Place(S, F)
-    slots, T, D = img.shape
+def front_kernel(S, F, nwide, QB, img, vec, wq, wx, wu, wd,
+                 first_out, rest, par, ub, x1, heads_out, out_t, lse, att, tok_out,
+                 first, tok, fsem, tsem, vec_full, norm, eb, stage, heads, kh, vt, o_buf, asem, hsem, ssem, rsem, osem, *refs):
+    slots, piece, D = img.shape
+    g = Place(S, F, slots)
+    images = g.images
+    T = slots * piece // images
     R = first.shape[2]
     V = R
-    W = D // S
-    N = S * T
+    W = D // g.n
+    N = g.n * T
     pairs = W // 128
+    tokens = Regroup(g, lambda p: img.at[p], lambda q: tok.at[ds(q * piece, piece)], tsem)
     vg = VecGather(g, vec, vec_full, refs[0])
 
     def own_first(b, cols):
@@ -575,19 +658,22 @@
     wide = Gather(g, nwide, 0, own_rest(0), rest, refs[15:22], wide=True)
 
     g.meet()
+    entry.start()
+    tokens.start()
     vg.start()
-    entry.start()
-    rows = min(128, T)
-
-    @pl.loop(0, slots * T // rows)
+    rows = min(128, piece)
+    entry.kept()
+    entry.run(0, entry.nitems)
+    tokens.arrived()
+    keep_tok = pltpu.make_async_copy(tok, tok_out, fsem.at[1])
+    keep_tok.start()
+
+    @pl.loop(0, slots * piece // rows)
     def _(r):
-        i, t = r // (T // rows), lax.rem(r, T // rows)
-        x = fp32(img[i, pl.ds(t * rows, rows)])
+        x = fp32(tok[ds(r * rows, rows)])
         x = x - mean_rows(x)
         norm[ds(r * rows, rows)] = x * lax.rsqrt(mean_rows(x * x) + EPSILON)
 
-    entry.kept()
-    entry.run(0, entry.nitems)
     vg.finish()
     thin.start()
     wide.start()
@@ -603,7 +689,7 @@
     eb[1] = jnp.zeros((1, D), jnp.float32)
     gain, shift = par[0:1], par[1:2]
 
-    @pl.loop(0, slots * T // rows)
+    @pl.loop(0, slots * piece // rows)
     def _(r):
         x1[ds(r * rows, rows)] = (norm[ds(r * rows, rows)] * gain + shift).astype(x1.dtype)
 
@@ -611,21 +697,23 @@
     thin.kept()
     wide.kept()
     entry.finish_recv()
+    keep_first = pltpu.make_async_copy(first, first_out, fsem.at[0])
+    keep_first.start()
 
     def copy(i, k, j):
         src = stage.at[i, k, j]
-        dst = heads.at[j, i, ds(g.s * T, T)]
-        return remote(src, dst, ssem.at[i, k, j], rsem.at[i, k, j], (g.s ^ k, g.f))
+        dst = heads.at[j, i, ds(g.me * T, T)]
+        return remote(src, dst, ssem.at[i, k, j], rsem.at[i, k, j], g.peer(k))
 
     def local(i, j):
-        return pltpu.make_async_copy(stage.at[i, 0, j], heads.at[j, i, ds(g.s * T, T)], ssem.at[i, 0, j])
+        return pltpu.make_async_copy(stage.at[i, 0, j], heads.at[j, i, ds(g.me * T, T)], ssem.at[i, 0, j])
 
     def project(i):
-        @pl.loop(0, S * 3)
+        @pl.loop(0, g.n * 3)
         def _(n):
-            k = lax.rem(1 + n // 3, S)
+            k = lax.rem(1 + n // 3, g.n)
             j = lax.rem(n, 3)
-            cols = ds((g.s ^ k) * W, W)
+            cols = ds((g.me ^ k) * W, W)
             w = first[:, j, :, cols].reshape(D, W)
             out = dot(x1[i * T : (i + 1) * T], w) + eb[j, :, cols]
             stage[i, k, j] = out.astype(stage.dtype)
@@ -641,10 +729,10 @@
     def projected(i):
         for j in range(3):
             local(i, j).wait()
-            for k in range(1, S):
+            for k in range(1, g.n):
                 copy(i, k, j).wait_send()
-                dst = heads.at[j, i, ds((g.s ^ k) * T, T)]
-                remote(dst, dst, ssem.at[i, k, j], rsem.at[i, k, j], (g.s ^ k, g.f)).wait_recv()
+                dst = heads.at[j, i, ds((g.me ^ k) * T, T)]
+                remote(dst, dst, ssem.at[i, k, j], rsem.at[i, k, j], g.peer(k)).wait_recv()
         keep_heads(i).start()
 
     def keep_heads(i):
@@ -652,17 +740,18 @@
 
     def out_copy(i, hp, kk):
         e = i * pairs + hp
-        dst = att.at[i, :, pl.ds(pl.multiple_of(g.s * W + hp * 128, 128), 128)]
+        dst = att.at[i, :, pl.ds(pl.multiple_of(g.me * W + hp * 128, 128), 128)]
         if kk == 0:
-            return pltpu.make_async_copy(o_buf.at[e, ds(g.s * T, T)], dst, osem.at[0, e, 0])
-        return remote(o_buf.at[e, ds((g.s ^ kk) * T, T)], dst, osem.at[0, e, kk], osem.at[1, e, kk], (g.s ^ kk, g.f))
+            return pltpu.make_async_copy(o_buf.at[e, ds(g.me * T, T)], dst, osem.at[0, e, 0])
+        return remote(o_buf.at[e, ds((g.me ^ kk) * T, T)], dst, osem.at[0, e, kk], osem.at[1, e, kk], g.peer(kk))
 
     def attend(i, hp):
         e = i * pairs + hp
         lanes = slice(hp * 128, (hp + 1) * 128)
         vt[...] = heads[2, i, :, lanes].T
+        length = length_of(par, *g.image(i), V)
         for hh in range(2):
-            kh[hh] = masked_keys(heads[1, i, :, lanes], lengths[i], hh)
+            kh[hh] = masked_keys(heads[1, i, :, lanes], length, hh)
 
         @pl.loop(0, N // QB)
         def _(b):
@@ -681,10 +770,10 @@
             background(e * (N // QB) + b)
 
         o_buf[e] = out_t[i, lanes].T
-        for kk in list(range(1, S)) + [0]:
+        for kk in list(range(1, g.n)) + [0]:
             out_copy(i, hp, kk).start()
 
-    units = [(i, hp) for i in range(slots) for hp in range(pairs)]
+    units = [(i, hp) for i in range(images) for hp in range(pairs)]
     early = thin.steps // EARLY
     per_unit = -(-(thin.steps - early) // (len(units) * (N // QB)))
 
@@ -696,7 +785,7 @@
         for m in range(per_unit):
             thin.step(early + n * per_unit + m)
 
-    for i in range(slots):
+    for i in range(images):
         project(i)
     thin.run(0, early)
     entry.finish_send()
@@ -709,42 +798,49 @@
         gather.finish_recv()
         gather.finish_send()
     for i, hp in units:
-        for kk in range(S):
+        for kk in range(g.n):
             cp = out_copy(i, hp, kk)
             if kk == 0:
                 cp.wait()
             else:
                 cp.wait_send()
                 cp.wait_recv()
-    for i in range(slots):
+    for i in range(images):
         keep_heads(i).wait()
-
-
-ENTRY_LAG = 6
-WIDE = 3
-EARLY = 10
-
-
-def front_call(S, F, cid, lengths, img, vec, wq, wx, wu, wd):
-    slots, T, D = img.shape
+    keep_tok.wait()
+    keep_first.wait()
+    tokens.sent()
+
+
+ENTRY_LAG = 8
+WIDE = 2
+EARLY = 4
+
+
+def front_call(S, F, cid, img, vec, wq, wx, wu, wd):
+    slots, piece, D = img.shape
+    M = slots * piece
+    n, images = (2, 1) if whole_images(S, slots) else (S, slots)
+    T = M // images
     R, FF = wq.shape[0], wu.shape[1]
-    W, N = D // S, S * T
+    W, N = D // n, n * T
     pairs = W // 128
     bf, fl = jnp.bfloat16, jnp.float32
     out = jax.ShapeDtypeStruct
     return pl.pallas_call(
         functools.partial(front_kernel, S, F, WIDE, min(256, N)),
         out_shape=[
-            out((F, 3, R, D), bf), out((F, 7, R, D), bf), out((16, D), fl), out((1, FF), fl), out((slots * T, D), bf),
-            out((3, slots, N, W), bf), out((slots, W, N), bf), out((slots, pairs, 8, N), fl), out((slots, T, D), bf),
+            out((F, 3, R, D), bf), out((F, 7, R, D), bf), out((16, D), fl), out((1, FF), fl), out((M, D), bf),
+            out((3, images, N, W), bf), out((images, W, N), bf), out((images, pairs, 8, N), fl), out((images, T, D), bf), out((M, D), bf),
         ],
-        in_specs=[pl.BlockSpec(memory_space=pltpu.SMEM), VM, ANY, ANY, ANY, ANY, ANY],
-        out_specs=[VM, ANY, VM, VM, VM, ANY, VM, VM, ANY],
+        in_specs=[ANY] * 6,
+        out_specs=[ANY, ANY, VM, VM, VM, ANY, VM, VM, ANY, ANY],
         scratch_shapes=[
-            pltpu.VMEM((F, 16, 128), bf), pltpu.VMEM((slots * T, D), fl), pltpu.VMEM((3, 1, D), fl), pltpu.VMEM((slots, S, 3, T, W), bf),
-            pltpu.VMEM((3, slots, N, W), bf), pltpu.VMEM((2, N, 128), bf), pltpu.VMEM((128, N), bf),
-            pltpu.VMEM((slots * pairs, N, 128), bf), DMA((1,)), DMA((slots,)), DMA((slots, S, 3)), DMA((slots, S, 3)),
-            DMA((2, slots * pairs, S)),
+            pltpu.VMEM((F, 3, R, D), bf), pltpu.VMEM((M, D), bf), DMA((2,)), DMA((2, slots)),
+            pltpu.VMEM((F, 16, 128), bf), pltpu.VMEM((M, D), fl), pltpu.VMEM((3, 1, D), fl), pltpu.VMEM((images, n, 3, T, W), bf),
+            pltpu.VMEM((3, images, N, W), bf), pltpu.VMEM((2, N, 128), bf), pltpu.VMEM((128, N), bf),
+            pltpu.VMEM((images * pairs, N, 128), bf), DMA((1,)), DMA((images,)), DMA((images, n, 3)), DMA((images, n, 3)),
+            DMA((2, images * pairs, n)),
         ]
         + VecGather.scratch(F)
         + Gather.scratch(S, F, 3, R, D, bounce=False)
@@ -752,60 +848,65 @@
         + Gather.scratch(S, F, WIDE, R, D),
         compiler_params=pltpu.CompilerParams(collective_id=cid, **PARAMS),
         name="front",
-    )(lengths, img, vec, wq, wx, wu, wd)
-
-
-def rear_kernel(S, F, QB, lengths, held, img, cot, att, par, ub, wu_own, wts, heads, out_t, lse, x1, first,
-                layer, dx, small, part_down, part_up, g_down, g_up, g_first, back, late,
-                cots, vecs, ubg, slab, csem, esem, wsem, psem, hsem, *refs):
-    g = Place(S, F)
-    slots, T, D = img.shape
-    M = slots * T
-    W = D // S
-    N = S * T
+    )(img, vec, wq, wx, wu, wd)
+
+
+def rear_kernel(S, F, QB, held, tok, att, par, ub, cot_in, wu_own, wts, heads, out_t, lse, x1, first,
+                layer_out, dx_out, small, part_down, part_a, part_b, g_down, g_up, g_first, back, late,
+                cot, layer, dx, msem, cots, vecs, ubg, slab, csem, esem, wsem, psem, hsem, *refs):
+    slots, piece, D = cot_in.shape
+    g = Place(S, F, slots)
+    images = g.images
+    M = slots * piece
+    T = M // images
+    W = D // g.n
+    N = g.n * T
     pairs = W // 128
     R = wts.shape[2]
     H = ub.shape[2]
-    rows = min(128, T)
+    rows = min(128, piece)
     nrows = M // rows
     exit_bias, scale1, gain2, shift2 = par[4:5], par[5:6], par[6:7], par[7:8]
     down_bias, scale2 = par[12:13], par[13:14]
     per_block = D // H
     bf, fl = jnp.bfloat16, jnp.float32
     down_sum = Scatter(g, part_down, g_down, refs[:16], per=4, lag=LAG, above=True)
-    up_sum = Scatter(g, part_up, g_up, refs[16:32], wide=True, lag=4, tail=UP_TAIL)
-    vsum = VecSum(g, slab, small, refs[48:52])
+    up_a = Scatter(g, part_a, g_up.at[:, pl.ds(0, 2 * D)], refs[16:32], wide=True, lag=4, tail=UP_TAIL)
+    up_b = Scatter(g, part_b, g_up.at[:, pl.ds(2 * D, 2 * D)], refs[32:48], lag=LAG)
+    vsum = VecSum(g, slab, small, refs[64:68])
 
     def own_late(b, cols):
         if isinstance(cols, slice):
             return wu_own.at[:, pl.ds((2 + b) * D, D)]
         return wu_own.at[:, pl.ds(pl.multiple_of((2 + b) * D + cols.start, 128), cols.size)]
 
-    more = Gather(g, 2, 0, own_late, late, refs[52:59])
-    units = slots * pairs
+    more = Gather(g, 2, 0, own_late, late, refs[68:75])
+    units = images * pairs
+    part_of = lambda ref: lambda p: ref.at[ds(p * piece, piece)]
+    cots_in = Regroup(g, lambda p: cot_in.at[p], part_of(cot), msem.at[0])
+    layers = Regroup(g, part_of(layer), lambda q: layer_out.at[q], msem.at[1], back=True)
     chunks = F // 4
-    done = (F - chunks - 2) * g.Z // chunks
 
     def place(r):
         return r // (T // rows), lax.rem(r, T // rows) * rows
 
     def mask(r):
         i, t = place(r)
-        limit = jnp.where(i < held[g.f], lengths[i], 0)
-        pos = lax.broadcasted_iota(jnp.int32, (rows, 1), 0) + (g.s * T + t)
-        return jnp.where(pos < limit, 1.0, 0.0)
+        group, slot = g.image(i)
+        limit = jnp.where(slot < held[group], length_of(par, group, slot, R), 0.0)
+        pos = lax.broadcasted_iota(jnp.int32, (rows, 1), 0) + (g.me * T + t)
+        return jnp.where(fp32(pos) < limit, 1.0, 0.0)
 
     def upstream(r):
-        i, t = place(r)
-        return mask(r) * fp32(cot[i, pl.ds(t, rows)])
+        return mask(r) * fp32(cot[ds(r * rows, rows)])
 
     def cot_copies(stage, k):
-        for i in range(slots):
-            src, dst = stage.at[pl.ds(i * T, T), pl.ds(k * W, W)], cots.at[i, ds(g.s * T, T)]
+        for i in range(images):
+            src, dst = stage.at[pl.ds(i * T, T), pl.ds(k * W, W)], cots.at[i, ds(g.me * T, T)]
             if k == 0:
                 yield pltpu.make_async_copy(src, dst, csem.at[0, 0])
             else:
-                yield remote(src, dst, csem.at[0, k], csem.at[1, k], (g.s ^ k, g.f))
+                yield remote(src, dst, csem.at[0, k], csem.at[1, k], g.peer(k))
 
     def feed_forward(mixed, x2, x2t, dcot, down, cot2, wu, wd, wx, dwu, dwd):
         def up_load(j):
@@ -815,8 +916,8 @@
             soon = pltpu.make_async_copy(wts.at[:, 4 + jnp.minimum(block, 1), :, cols], wu.at[slot], wsem.at[0, slot])
             return soon, pltpu.make_async_copy(late.at[:, jnp.maximum(block - 2, 0), :, cols], wu.at[slot], wsem.at[0, slot])
 
-        def start_up(j):
-            soon, later = up_load(j)
+        def start_either(j, copies):
+            soon, later = copies
 
             @pl.when(j < F // 2)
             def _():
@@ -831,22 +932,25 @@
 
         def put_up(j):
             cols = pl.ds(pl.multiple_of(lax.rem(j, per_block) * H, H), H)
-            return pltpu.make_async_copy(dwu, part_up.at[:, j // per_block, :, cols], psem.at[0])
+            block = j // per_block
+            soon = pltpu.make_async_copy(dwu, part_a.at[:, jnp.minimum(block, 1), :, cols], psem.at[0])
+            return soon, pltpu.make_async_copy(dwu, part_b.at[:, jnp.maximum(block - 2, 0), :, cols], psem.at[0])
 
         def put_down(j):
             return pltpu.make_async_copy(dwd, part_down.at[j, pl.ds(0, 4)], psem.at[1])
 
         x_load = pltpu.make_async_copy(wts.at[:, 6], wx, wsem.at[2, 0])
         x_load.start()
-        start_up(0)
+        start_either(0, up_load(0))
         down_load(0).start()
         more.kept()
         x_load.wait()
         mixed[...] = dot(att[...], wx[...].reshape(D, D)) + exit_bias
 
         def residual(r, sl):
-            i, t = place(r)
-            return fp32(img[i, pl.ds(t, rows)]) + scale1 * mixed[sl]
+            return fp32(tok[sl]) + scale1 * mixed[sl]
+
+        cots_in.arrived()
 
         def norm(res):
             res = res - mean_rows(res)
@@ -879,7 +983,7 @@
 
             @pl.when(j + 1 < F)
             def _():
-                start_up(j + 1)
+                start_either(j + 1, up_load(j + 1))
                 down_load(j + 1).start()
 
             up_load(j)[0].wait()
@@ -896,32 +1000,50 @@
             low = pre_cot.astype(bf)
             @pl.when(j > 0)
             def _():
-                put_up(j - 1).wait()
+                put_up(j - 1)[0].wait()
                 put_down(j - 1).wait()
 
             @pl.when((j > 0) & (lax.rem(j, chunks) == 0))
             def _():
                 n = (j // chunks - 1) * g.Z
-                up_sum.ready(n, n + g.Z)
+                @pl.when(j <= 2 * chunks)
+                def _():
+                    up_a.ready(n, n + g.Z)
+
+                @pl.when(j > 2 * chunks)
+                def _():
+                    up_b.ready(n - 2 * g.Z, n - g.Z)
+
                 down_sum.ready(n, n + g.Z)
 
             dwu[...] = dot(x2t[...], low).astype(bf).reshape(F, R, H)
             dwd[...] = dot(act, dcot[...], TN).astype(bf).reshape(4, R, D)
-            put_up(j).start()
+            start_either(j, put_up(j))
             put_down(j).start()
             down[...] += dot(act, wd_j)
             cot2[...] += dot(low, wu_j, NT)
 
-            @pl.when((j > chunks) & (j < F - 1))
+            @pl.when((j > 0) & (lax.rem(j, chunks) == 1))
             def _():
-                first = (j - chunks - 1) * g.Z // chunks
-                up_sum.run(first, first + g.Z // chunks)
-                down_sum.run(first, first + g.Z // chunks)
-
-        put_up(F - 1).wait()
+                first = (j // chunks - 1) * g.Z
+
+                @pl.when(first >= 0)
+                def _():
+                    @pl.when(first < 2 * g.Z)
+                    def _():
+                        up_a.run(first, first + g.Z)
+
+                    @pl.when(first >= 2 * g.Z)
+                    def _():
+                        up_a.run(first, first + g.Z)
+                        up_b.run(first - 2 * g.Z, first - g.Z)
+
+                    down_sum.run(first, first + g.Z)
+
+        put_up(F - 1)[0].wait()
         put_down(F - 1).wait()
         n = 3 * g.Z
-        up_sum.ready(n, n + g.Z)
+        up_b.ready(n - 2 * g.Z, n - g.Z)
         down_sum.ready(n, n + g.Z)
         vecs[...] = jnp.zeros_like(vecs)
 
@@ -948,8 +1070,8 @@
             vecs[4:5] += total(rc * mixed[sl])
             vecs[5:6] += total(mc)
 
-        for k in list(range(1, S)) + [0]:
-            dcot[:, k * W : (k + 1) * W] = dot(x2[...], wx_rows(wx, g.s ^ k, W), NT).astype(bf)
+        for k in list(range(1, g.n)) + [0]:
+            dcot[:, k * W : (k + 1) * W] = dot(x2[...], wx_rows(wx, g.me ^ k, W), NT).astype(bf)
             for cp in cot_copies(dcot, k):
                 cp.start()
         for n in range(F // 4):
@@ -958,49 +1080,51 @@
             put_x = pltpu.make_async_copy(dwd, part_down.at[pl.ds(n * 4, 4), 4], psem.at[2])
             put_x.start()
             put_x.wait()
-        up_sum.run(done, 3 * g.Z)
-        down_sum.run(done, 3 * g.Z)
         down_sum.ready(4 * g.Z, 5 * g.Z)
-        for k in range(S):
-            for cp in cot_copies(dcot, k):
-                if k == 0:
-                    cp.wait()
+        layers.start()
+        for cp in cot_copies(dcot, 0):
+            cp.wait()
         ref = dcot.at[:, pl.ds(0, W)]
-        for k in range(1, S):
+        for k in range(1, g.n):
             remote(ref, ref, csem.at[0, k], csem.at[1, k], g.mate).wait_send()
 
     polls = units * (N // QB)
 
     def background(n):
-        @pl.when(3 * g.Z + n < up_sum.steps)
+        t = 3 * g.Z + n // EVERY
+
+        @pl.when(lax.rem(n, EVERY) == 0)
         def _():
-            up_sum.step(3 * g.Z + n)
-
-        down_sum.step(3 * g.Z + n)
+            step_all(t)
+
+    def step_all(t):
+        up_a.step(t)
+        up_b.step(t - 2 * g.Z)
+        down_sum.step(t)
 
     def attend_back(hd, ot, ls, kh, vh, kt, cot_t, delta, dq_t, dk, dv, stage):
         loads = [pltpu.make_async_copy(a, b, hsem.at[n]) for n, (a, b) in enumerate(((heads, hd), (out_t, ot), (lse, ls)))]
         for cp in loads:
             cp.start()
-        for k in range(1, S):
-            ref = cots.at[:, ds((g.s ^ k) * T, T)]
-            remote(ref, ref, csem.at[0, k], csem.at[1, k], (g.s ^ k, g.f)).wait_recv()
+        for k in range(1, g.n):
+            ref = cots.at[:, ds((g.me ^ k) * T, T)]
+            remote(ref, ref, csem.at[0, k], csem.at[1, k], g.peer(k)).wait_recv()
         for cp in loads:
             cp.wait()
 
         def copy(e, j, kk):
             i, hp = e // pairs, lax.rem(e, pairs)
-            dst = back.at[i, :, ds(j * D + g.s * W + hp * 128, 128)]
-            src = stage.at[e, j, ds((g.s ^ kk) * T, T)]
+            dst = back.at[i, :, ds(j * D + g.me * W + hp * 128, 128)]
+            src = stage.at[e, j, ds((g.me ^ kk) * T, T)]
             if kk == 0:
                 return pltpu.make_async_copy(src, dst, esem.at[2])
-            return remote(src, dst, esem.at[0], esem.at[1], (g.s ^ kk, g.f))
+            return remote(src, dst, esem.at[0], esem.at[1], g.peer(kk))
 
         @pl.loop(0, units)
         def _(e):
             i, hp = e // pairs, lax.rem(e, pairs)
             lanes = ds(hp * 128, 128)
-            length = lengths[i]
+            length = length_of(par, *g.image(i), R)
             kt[...] = hd[1, i, :, lanes].T
             cot_t[...] = cots[i, :, lanes].T
             prod = fp32(cot_t[...]) * fp32(ot[i, lanes])
@@ -1034,18 +1158,19 @@
             stage[e, 1] = dk[...].astype(bf)
             stage[e, 2] = dv[...].astype(bf)
             for j in range(3):
-                for kk in list(range(1, S)) + [0]:
+                for kk in list(range(1, g.n)) + [0]:
                     copy(e, j, kk).start()
 
-        ref = stage.at[:, :, pl.ds(0, (S - 1) * T)]
+        ref = stage.at[:, :, pl.ds(0, (g.n - 1) * T)]
         cp = remote(ref, ref, esem.at[0], esem.at[1], g.mate)
         cp.wait_send()
         cp.wait_recv()
         ref = stage.at[:, :, pl.ds(0, T)]
         pltpu.make_async_copy(ref, ref, esem.at[2]).wait()
 
-    def entry(part, ein, win, x1v, x1t, acc, rows_v):
-        entry_sum = Scatter(g, part, g_first, refs[32:48])
+    def entry(part, ein, win, x1v, x1t, acc, rows_v, dxl):
+        grads = Regroup(g, part_of(dxl), lambda q: dx_out.at[q], msem.at[2], back=True)
+        entry_sum = Scatter(g, part, g_first, refs[48:64])
         loads = [pltpu.make_async_copy(back.at[:, :, pl.ds(j * D, D)], ein.at[j], hsem.at[j]) for j in range(3)]
         weights = [pltpu.make_async_copy(first.at[:, j], win.at[j % 2], wsem.at[2, j % 2]) for j in range(3)]
         x_load = pltpu.make_async_copy(x1, x1v, wsem.at[0, 0])
@@ -1053,12 +1178,11 @@
             cp.start()
         x_load.wait()
         x1t[...] = x1v[...].T
-        at = 3 * g.Z + polls
+        at = 3 * g.Z + polls // EVERY
 
         def others(n, k):
             for t in range(at + n, at + n + k):
-                up_sum.step(t)
-                down_sum.step(t)
+                step_all(t)
 
         rows_v[...] = jnp.zeros_like(rows_v)
         cot_of = lambda j: ein[j].reshape(M, D)
@@ -1086,18 +1210,18 @@
         @pl.loop(0, nrows)
         def _(r):
             sl = ds(r * rows, rows)
-            i, t = place(r)
-            x = fp32(img[i, pl.ds(t, rows)])
+            x = fp32(tok[sl])
             x = x - mean_rows(x)
             inv = lax.rsqrt(mean_rows(x * x) + EPSILON)
             n = x * inv
             d1 = acc[sl]
             c = d1 * gain
-            dx[sl] = dx[sl] + inv * (c - mean_rows(c) - n * mean_rows(c * n))
+            dxl[sl] = (dx[sl] + inv * (c - mean_rows(c) - n * mean_rows(c * n))).astype(bf)
             rows_v[0:1] += jnp.sum(d1 * n, axis=0, keepdims=True)
             rows_v[1:2] += jnp.sum(d1, axis=0, keepdims=True)
             entry_sum.step(2 * g.Z + 3 + r)
 
+        grads.start()
         slab[...] = jnp.zeros_like(slab)
         own = [(0, rows_v, 0), (1, rows_v, 1), (4, vecs, 5), (5, vecs, 4), (6, vecs, 2), (7, vecs, 3), (12, vecs, 1), (13, vecs, 0)]
         V = R
@@ -1113,36 +1237,42 @@
         mark = 2 * g.Z + 3 + nrows
         entry_sum.run(mark, mark + 4)
         vsum.middle()
-        left = max(down_sum.steps, up_sum.steps) - (at + 12)
+        left = max(down_sum.steps, up_a.steps, up_b.steps + 2 * g.Z) - (at + 12)
 
         @pl.loop(0, max(left, entry_sum.steps - mark - 4))
         def _(t):
-            up_sum.step(at + 12 + t)
-            down_sum.step(at + 12 + t)
+            step_all(at + 12 + t)
             entry_sum.step(mark + 4 + t)
 
         entry_sum.finish()
+        grads.arrived()
+        grads.sent()
 
     g.meet()
     more.start()
+    cots_in.start()
     v = pltpu.VMEM
     pl.run_scoped(
         feed_forward, v((M, D), fl), v((M, D), bf), v((D, M), bf), v((M, D), bf), v((M, D), fl), v((M, D), fl),
         v((2, F, R, H), bf), v((2, 4, R, D), bf), v((F, R, D), bf), v((F, R, H), bf), v((4, R, D), bf),
     )
     pl.run_scoped(
-        attend_back, v((3, slots, N, W), bf), v((slots, W, N), bf), v((slots, pairs, 8, N), fl), v((2, N, 128), bf),
+        attend_back, v((3, images, N, W), bf), v((images, W, N), bf), v((images, pairs, 8, N), fl), v((2, N, 128), bf),
         v((2, N, 128), bf), v((128, N), bf), v((128, N), bf), v((8, N), fl), v((128, N), bf), v((N, 128), fl),
         v((N, 128), fl), v((units, 3, N, 128), bf),
     )
     pl.run_scoped(
-        entry, v((F, 3, R, D), bf), v((3, slots, T, D), bf), v((2, F, R, D), bf), v((M, D), bf), v((D, M), bf),
-        v((M, D), fl), v((8, D), fl),
+        entry, v((F, 3, R, D), bf), v((3, images, T, D), bf), v((2, F, R, D), bf), v((M, D), bf), v((D, M), bf),
+        v((M, D), fl), v((8, D), fl), v((M, D), bf),
     )
-    up_sum.finish()
+    up_a.finish()
+    up_b.finish()
     down_sum.finish()
     vsum.finish()
     more.finish_send()
+    cots_in.sent()
+    layers.arrived()
+    layers.sent()
 
 
 def wx_rows(wx, peer, W):
@@ -1152,37 +1282,41 @@
 
 
 LAG = 4
-UP_TAIL = 17
-
-
-def rear_call(S, F, cid, lengths, held, img, cot, att, par, ub, wu_own, wts, heads, out_t, lse, x1, first):
-    slots, T, D = img.shape
-    M = slots * T
+UP_TAIL = 10
+EVERY = 2
+
+
+def rear_call(S, F, cid, held, tok, att, par, ub, cot, wu_own, wts, heads, out_t, lse, x1, first):
+    slots, piece, D = cot.shape
+    M = slots * piece
+    n, images = (2, 1) if whole_images(S, slots) else (S, slots)
+    T = M // images
     R = wts.shape[2]
     FF = ub.shape[1]
     H = FF // F
-    W, N = D // S, S * T
+    W, N = D // n, n * T
     bf, fl = jnp.bfloat16, jnp.float32
     SM = pl.BlockSpec(memory_space=pltpu.SMEM)
     out, v = jax.ShapeDtypeStruct, pltpu.VMEM
     return pl.pallas_call(
         functools.partial(rear_kernel, S, F, min(256, N)),
         out_shape=[
-            out((M, D), bf), out((M, D), fl), out((16, 128), fl), out((F, 5, R, D), bf), out((F, 4, R, D), bf),
-            out((5 * R, D), bf), out((R, 4 * D), bf), out((R, 3 * D), bf), out((slots, T, 3 * D), bf), out((F, 2, R, D), bf),
+            out(cot.shape, bf), out(cot.shape, bf), out((16, 128), fl), out((F, 5, R, D), bf), out((F, 2, R, D), bf), out((F, 2, R, D), bf),
+            out((5 * R, D), bf), out((R, 4 * D), bf), out((R, 3 * D), bf), out((images, T, 3 * D), bf), out((F, 2, R, D), bf),
         ],
-        in_specs=[SM, SM, VM, VM, VM, VM, VM] + [ANY] * 7,
-        out_specs=[VM, VM, VM] + [ANY] * 7,
-        scratch_shapes=[v((slots, N, W), bf), v((8, D), fl), v((F, 1, H), fl), v((F, 16, 128), fl),
-                        DMA((2, S)), DMA((3,)), DMA((3, 2)), DMA((3,)), DMA((3,))]
+        in_specs=[SM, VM, VM, VM, VM] + [ANY] * 8,
+        out_specs=[ANY, ANY, VM] + [ANY] * 8,
+        scratch_shapes=[v((M, D), bf), v((M, D), bf), v((M, D), fl), DMA((3, 2, slots)), v((images, N, W), bf), v((8, D), fl), v((F, 1, H), fl), v((F, 16, 128), fl),
+                        DMA((2, n)), DMA((3,)), DMA((3, 2)), DMA((3,)), DMA((3,))]
         + Scatter.scratch(S, F, 5, R, D, K=F)
-        + Scatter.scratch(S, F, 4, R, D, wide=True, K=F)
+        + Scatter.scratch(S, F, 2, R, D, wide=True, K=F // 2)
+        + Scatter.scratch(S, F, 2, R, D, K=F // 2)
         + Scatter.scratch(S, F, 3, R, D, K=F // 2)
         + VecSum.scratch(S, F, 16, 128)
         + Gather.scratch(S, F, 2, R, D),
         compiler_params=pltpu.CompilerParams(collective_id=cid, **PARAMS),
         name="rear",
-    )(lengths, held, img, cot, att, par, ub.reshape(F, 1, H), wu_own, wts, heads, out_t, lse, x1, first)
+    )(held, tok, att, par, ub.reshape(F, 1, H), cot, wu_own, wts, heads, out_t, lse, x1, first)
 
 
 def body(S, F, images, out_grad, lengths, images_held, first_gain, first_shift, entry_weight, entry_bias, exit_weight,
@@ -1199,18 +1333,21 @@
         n = v.shape[0] // V
         own_vec = own_vec + jnp.pad(v.reshape(n, V), ((at, 16 - at - n), (0, 128 - V)))
         at += n
-    first, rest, par, ub, x1, heads, out_t, lse, att = front_call(
-        S, F, 0, lengths, images, own_vec, entry_weight, exit_weight, up_weight, down_weight
+    for v in (lengths // 32, lengths % 32):
+        own_vec = own_vec + jnp.pad(v.astype(jnp.bfloat16).reshape(1, slots), ((at, 15 - at), (0, 128 - slots)))
+        at += 1
+    first, rest, par, ub, x1, heads, out_t, lse, att, tok = front_call(
+        S, F, 0, images, own_vec, entry_weight, exit_weight, up_weight, down_weight
     )
-    layer, dx, small, _, _, g_down, g_up, g_first, _, _ = rear_call(
-        S, F, 1, lengths, images_held, images, out_grad, att.reshape(M, D), par, ub, up_weight, rest, heads, out_t, lse, x1, first
+    layer, dx, small, _, _, _, g_down, g_up, g_first, _, _ = rear_call(
+        S, F, 1, images_held, tok, att.reshape(M, D), par, ub, out_grad, up_weight, rest, heads, out_t, lse, x1, first
     )
     small = small[:, :V]
     row = lambda n, m=1: small[n : n + m].reshape(m * V)
     g_first, g_down, g_up = g_first.astype(fl), g_down.astype(fl), g_up.astype(fl)
     return (
-        layer.reshape(slots, T, D),
-        dx.reshape(slots, T, D),
+        layer,
+        dx.astype(fl),
         row(0),
         row(1),
         g_first,

time: 350 us -> 315 us (0.900)
  Pallas kernels: 334 us -> 298 us
    pallas_call x1, Pallas kernels: 121 us -> 98.8 us  [front_call(): pl.pallas_call(functools.partial(front_kernel, S, F, WIDE, min(256, N)),...]
    pallas_call x1, Pallas kernels: 213 us -> 199 us  [rear_call(): pl.pallas_call(functools.partial(rear_kernel, S, F, min(256, N)), out_sha...]
where the time goes in v4:
time: 315 us
  Pallas kernels  298 us (95%)
  local copies, waits for them, and re-layouts  9.66 us (3%)
  other arithmetic  6.46 us (2%)
    pallas_call x1, Pallas kernels, rear_call(): pl.pallas_call(functools.partial(rear_kernel, S, F, min(256, N)), out_sha...  199 us
    pallas_call x1, Pallas kernels, front_call(): pl.pallas_call(functools.partial(front_kernel, S, F, WIDE, min(256, N)),...  98.8 us

profile of v4, /device:TPU:0, one launch (start us, length us, event | category | flops | bytes accessed | tf_op | source)
XLA Modules:
  0.0 315.0 jit_solution(11714088815179479938)
XLA Ops:
  0.6 0.7 convert_bitcast_fusion
  1.3 1.4 pad_add_fusion.vec
  2.7 98.8 %front.1 = (bf16[8,3,128,1024]{3,2,1,0:T(8,128)(2,1)}, bf16[8,7,128,1024]{3,2,1,0:T(8,128)(2,1)}, f32[16,1024]{1,0:T(8,128)}, f32[1,4096]{1,0:T(1,128)}, bf16[51...) custom-call(bf16[2,256,1024]{2,1,0:T(8,128)(2,1)} %img.1, ...), custom_call_target="tpu_custom_call" | custom-call | tf_op jit(solution)/shard_map/front/pallas_call | solution.py:830
  101.5 199.3 %rear.1 = (bf16[2,256,1024]{2,1,0:T(8,128)(2,1)}, bf16[2,256,1024]{2,1,0:T(8,128)(2,1)}, f32[16,128]{1,0:T(8,128)}, bf16[8,5,128,1024]{3,2,1,0:T(8,128)(2,1)}, b...) custom-call(s32[8]{0:T(128)} %held.1, ...), custom_call_target="tpu_custom_call" | custom-call | tf_op jit(solution)/shard_map/rear/pallas_call | solution.py:1301
  300.9 0.0 copy-start.3
  300.9 1.3 slice_bitcast_fusion.1
  302.2 1.3 slice_bitcast_fusion
  303.5 1.4 slice_bitcast_fusion.2
  304.9 1.8 slice.48
  306.7 0.0 copy-start.1
  306.7 2.9 slice.49
  309.6 0.0 copy-done.3
  309.6 0.0 copy-start
  309.6 1.3 convert_element_type.45
  310.9 0.0 copy-done.1
  310.9 0.0 copy-start.2
  310.9 1.6 convert_element_type.44
  312.5 0.0 copy-done
  312.5 1.5 convert_element_type.47
  314.0 0.0 copy-done.2
  314.0 1.0 copy.35
Async XLA Ops:
  300.9 8.7 %copy-start.3 = (bf16[128,3072]{1,0:T(8,128)(2,1)S(1)}, bf16[128,3072]{1,0:T(8,128)(2,1)}, u32[]{:S(2)}) copy-start(bf16[128,3072]{1,0:T(8,128)(2,1)} %get-tuple-element.45) | copy-start | bytes 2359300
  306.7 4.2 %copy-start.1 = (bf16[2,256,1024]{2,1,0:T(8,128)(2,1)S(1)}, bf16[2,256,1024]{2,1,0:T(8,128)(2,1)}, u32[]{:S(2)}) copy-start(bf16[2,256,1024]{2,1,0:T(8,128)(2,1)} %get-tuple-element.43) | copy-start | bytes 3145732
  309.6 2.9 copy-start
  310.9 3.1 copy-start.2

commit v5 on v4

--- a/solution.py
+++ b/solution.py
@@ -623,9 +623,9 @@
     return jnp.where(mine, fp32(q) * HEAD_DIM ** (-0.5), jnp.where(spare, 1.0, 0.0)).astype(jnp.bfloat16)
 
 
-def front_kernel(S, F, nwide, QB, img, vec, wq, wx, wu, wd,
-                 first_out, rest, par, ub, x1, heads_out, out_t, lse, att, tok_out,
-                 first, tok, fsem, tsem, vec_full, norm, eb, stage, heads, kh, vt, o_buf, asem, hsem, ssem, rsem, osem, *refs):
+def front_kernel(S, F, nwide, QB, img, cot, vec, wq, wx, wu, wd,
+                 first_out, rest, par, ub, x1, heads_out, out_t, lse, att, tok_out, cot_out,
+                 first, tok, cot_v, fsem, tsem, csem, vec_full, norm, eb, stage, heads, kh, vt, o_buf, asem, hsem, ssem, rsem, osem, *refs):
     slots, piece, D = img.shape
     g = Place(S, F, slots)
     images = g.images
@@ -636,6 +636,7 @@
     N = g.n * T
     pairs = W // 128
     tokens = Regroup(g, lambda p: img.at[p], lambda q: tok.at[ds(q * piece, piece)], tsem)
+    cots = Regroup(g, lambda p: cot.at[p], lambda q: cot_v.at[ds(q * piece, piece)], csem)
     vg = VecGather(g, vec, vec_full, refs[0])
 
     def own_first(b, cols):
@@ -696,6 +697,7 @@
     entry.run(entry.nitems, entry.steps)
     thin.kept()
     wide.kept()
+    cots.start()
     entry.finish_recv()
     keep_first = pltpu.make_async_copy(first, first_out, fsem.at[0])
     keep_first.start()
@@ -794,6 +796,9 @@
             projected(i)
         attend(i, hp)
     wide.run(len(units) * (N // QB), wide.steps)
+    cots.arrived()
+    keep_cot = pltpu.make_async_copy(cot_v, cot_out, fsem.at[2])
+    keep_cot.start()
     for gather in (thin, wide):
         gather.finish_recv()
         gather.finish_send()
@@ -810,14 +815,16 @@
     keep_tok.wait()
     keep_first.wait()
     tokens.sent()
-
-
-ENTRY_LAG = 8
-WIDE = 2
+    cots.sent()
+    keep_cot.wait()
+
+
+ENTRY_LAG = 10
+WIDE = 3
 EARLY = 4
 
 
-def front_call(S, F, cid, img, vec, wq, wx, wu, wd):
+def front_call(S, F, cid, img, cot, vec, wq, wx, wu, wd):
     slots, piece, D = img.shape
     M = slots * piece
     n, images = (2, 1) if whole_images(S, slots) else (S, slots)
@@ -831,12 +838,12 @@
         functools.partial(front_kernel, S, F, WIDE, min(256, N)),
         out_shape=[
             out((F, 3, R, D), bf), out((F, 7, R, D), bf), out((16, D), fl), out((1, FF), fl), out((M, D), bf),
-            out((3, images, N, W), bf), out((images, W, N), bf), out((images, pairs, 8, N), fl), out((images, T, D), bf), out((M, D), bf),
+            out((3, images, N, W), bf), out((images, W, N), bf), out((images, pairs, 8, N), fl), out((images, T, D), bf), out((M, D), bf), out((M, D), bf),
         ],
-        in_specs=[ANY] * 6,
-        out_specs=[ANY, ANY, VM, VM, VM, ANY, VM, VM, ANY, ANY],
+        in_specs=[ANY] * 7,
+        out_specs=[ANY, ANY, VM, VM, VM, ANY, VM, VM, ANY, ANY, ANY],
         scratch_shapes=[
-            pltpu.VMEM((F, 3, R, D), bf), pltpu.VMEM((M, D), bf), DMA((2,)), DMA((2, slots)),
+            pltpu.VMEM((F, 3, R, D), bf), pltpu.VMEM((M, D), bf), pltpu.VMEM((M, D), bf), DMA((3,)), DMA((2, slots)), DMA((2, slots)),
             pltpu.VMEM((F, 16, 128), bf), pltpu.VMEM((M, D), fl), pltpu.VMEM((3, 1, D), fl), pltpu.VMEM((images, n, 3, T, W), bf),
             pltpu.VMEM((3, images, N, W), bf), pltpu.VMEM((2, N, 128), bf), pltpu.VMEM((128, N), bf),
             pltpu.VMEM((images * pairs, N, 128), bf), DMA((1,)), DMA((images,)), DMA((images, n, 3)), DMA((images, n, 3)),
@@ -848,13 +855,13 @@
         + Gather.scratch(S, F, WIDE, R, D),
         compiler_params=pltpu.CompilerParams(collective_id=cid, **PARAMS),
         name="front",
-    )(img, vec, wq, wx, wu, wd)
-
-
-def rear_kernel(S, F, QB, held, tok, att, par, ub, cot_in, wu_own, wts, heads, out_t, lse, x1, first,
+    )(img, cot, vec, wq, wx, wu, wd)
+
+
+def rear_kernel(S, F, QB, held, tok, cot, att, par, ub, wu_own, wts, heads, out_t, lse, x1, first,
                 layer_out, dx_out, small, part_down, part_a, part_b, g_down, g_up, g_first, back, late,
-                cot, layer, dx, msem, cots, vecs, ubg, slab, csem, esem, wsem, psem, hsem, *refs):
-    slots, piece, D = cot_in.shape
+                layer, dx, msem, cots, vecs, ubg, slab, csem, esem, wsem, psem, hsem, *refs):
+    slots, piece, D = layer_out.shape
     g = Place(S, F, slots)
     images = g.images
     M = slots * piece
@@ -883,7 +890,6 @@
     more = Gather(g, 2, 0, own_late, late, refs[68:75])
     units = images * pairs
     part_of = lambda ref: lambda p: ref.at[ds(p * piece, piece)]
-    cots_in = Regroup(g, lambda p: cot_in.at[p], part_of(cot), msem.at[0])
     layers = Regroup(g, part_of(layer), lambda q: layer_out.at[q], msem.at[1], back=True)
     chunks = F // 4
 
@@ -943,14 +949,14 @@
         x_load.start()
         start_either(0, up_load(0))
         down_load(0).start()
-        more.kept()
         x_load.wait()
         mixed[...] = dot(att[...], wx[...].reshape(D, D)) + exit_bias
 
         def residual(r, sl):
             return fp32(tok[sl]) + scale1 * mixed[sl]
 
-        cots_in.arrived()
+        hello()
+        more.start()
 
         def norm(res):
             res = res - mean_rows(res)
@@ -965,6 +971,7 @@
             dcot[sl] = (upstream(r) * scale2).astype(bf)
 
         x2t[...] = x2[...].T
+        more.kept()
         down[...] = jnp.zeros_like(down)
         cot2[...] = jnp.zeros_like(cot2)
 
@@ -1248,9 +1255,7 @@
         grads.arrived()
         grads.sent()
 
-    g.meet()
-    more.start()
-    cots_in.start()
+    hello = g.greet()
     v = pltpu.VMEM
     pl.run_scoped(
         feed_forward, v((M, D), fl), v((M, D), bf), v((D, M), bf), v((M, D), bf), v((M, D), fl), v((M, D), fl),
@@ -1270,7 +1275,6 @@
     down_sum.finish()
     vsum.finish()
     more.finish_send()
-    cots_in.sent()
     layers.arrived()
     layers.sent()
 
@@ -1286,9 +1290,9 @@
 EVERY = 2
 
 
-def rear_call(S, F, cid, held, tok, att, par, ub, cot, wu_own, wts, heads, out_t, lse, x1, first):
-    slots, piece, D = cot.shape
-    M = slots * piece
+def rear_call(S, F, cid, slots, held, tok, cot, att, par, ub, wu_own, wts, heads, out_t, lse, x1, first):
+    M, D = cot.shape
+    piece = M // slots
     n, images = (2, 1) if whole_images(S, slots) else (S, slots)
     T = M // images
     R = wts.shape[2]
@@ -1301,12 +1305,12 @@
     return pl.pallas_call(
         functools.partial(rear_kernel, S, F, min(256, N)),
         out_shape=[
-            out(cot.shape, bf), out(cot.shape, bf), out((16, 128), fl), out((F, 5, R, D), bf), out((F, 2, R, D), bf), out((F, 2, R, D), bf),
+            out((slots, piece, D), bf), out((slots, piece, D), bf), out((16, 128), fl), out((F, 5, R, D), bf), out((F, 2, R, D), bf), out((F, 2, R, D), bf),
             out((5 * R, D), bf), out((R, 4 * D), bf), out((R, 3 * D), bf), out((images, T, 3 * D), bf), out((F, 2, R, D), bf),
         ],
-        in_specs=[SM, VM, VM, VM, VM] + [ANY] * 8,
+        in_specs=[SM, VM, VM, VM, VM, VM] + [ANY] * 7,
         out_specs=[ANY, ANY, VM] + [ANY] * 8,
-        scratch_shapes=[v((M, D), bf), v((M, D), bf), v((M, D), fl), DMA((3, 2, slots)), v((images, N, W), bf), v((8, D), fl), v((F, 1, H), fl), v((F, 16, 128), fl),
+        scratch_shapes=[v((M, D), bf), v((M, D), fl), DMA((3, 2, slots)), v((images, N, W), bf), v((8, D), fl), v((F, 1, H), fl), v((F, 16, 128), fl),
                         DMA((2, n)), DMA((3,)), DMA((3, 2)), DMA((3,)), DMA((3,))]
         + Scatter.scratch(S, F, 5, R, D, K=F)
         + Scatter.scratch(S, F, 2, R, D, wide=True, K=F // 2)
@@ -1316,7 +1320,7 @@
         + Gather.scratch(S, F, 2, R, D),
         compiler_params=pltpu.CompilerParams(collective_id=cid, **PARAMS),
         name="rear",
-    )(held, tok, att, par, ub.reshape(F, 1, H), cot, wu_own, wts, heads, out_t, lse, x1, first)
+    )(held, tok, cot, att, par, ub.reshape(F, 1, H), wu_own, wts, heads, out_t, lse, x1, first)
 
 
 def body(S, F, images, out_grad, lengths, images_held, first_gain, first_shift, entry_weight, entry_bias, exit_weight,
@@ -1336,33 +1340,56 @@
     for v in (lengths // 32, lengths % 32):
         own_vec = own_vec + jnp.pad(v.astype(jnp.bfloat16).reshape(1, slots), ((at, 15 - at), (0, 128 - slots)))
         at += 1
-    first, rest, par, ub, x1, heads, out_t, lse, att, tok = front_call(
-        S, F, 0, images, own_vec, entry_weight, exit_weight, up_weight, down_weight
+    first, rest, par, ub, x1, heads, out_t, lse, att, tok, cot = front_call(
+        S, F, 0, images, out_grad, own_vec, entry_weight, exit_weight, up_weight, down_weight
     )
     layer, dx, small, _, _, _, g_down, g_up, g_first, _, _ = rear_call(
-        S, F, 1, images_held, tok, att.reshape(M, D), par, ub, out_grad, up_weight, rest, heads, out_t, lse, x1, first
+        S, F, 1, slots, images_held, tok, cot, att.reshape(M, D), par, ub, up_weight, rest, heads, out_t, lse, x1, first
     )
-    small = small[:, :V]
-    row = lambda n, m=1: small[n : n + m].reshape(m * V)
-    g_first, g_down, g_up = g_first.astype(fl), g_down.astype(fl), g_up.astype(fl)
+    vectors = [v.shape[0] for v in rows]
+    down, exit_, up, first, dx, layer, *small = results_call(V, g_down, g_up, g_first, dx, layer, small, vectors)
     return (
-        layer,
-        dx.astype(fl),
-        row(0),
-        row(1),
-        g_first,
-        row(2, 2),
-        g_down[4 * R :],
-        row(4),
-        row(5),
-        row(6),
-        row(7),
-        g_up,
-        row(8, 4),
-        g_down[: 4 * R],
-        row(12),
-        row(13),
+        layer.reshape(slots, T, D), dx.reshape(slots, T, D), small[0], small[1], first, small[2], exit_, small[3], small[4],
+        small[5], small[6], up, small[7], down, small[8], small[9],
     )
+
+
+def results_kernel(V, down, out, up, first, dx, layer, small, *outs):
+    for src, dst in zip((down, out, up, first, dx, layer), outs):
+        dst[...] = src[...].astype(dst.dtype)
+
+    @pl.when(pl.program_id(0) == 0)
+    def _():
+        at = 0
+        for dst in outs[6:]:
+            n = dst.shape[0] // V
+            for r in range(n):
+                dst[r * V : (r + 1) * V] = small[at + r, :V]
+            at += n
+
+
+def results_call(V, g_down, g_up, g_first, dx, layer, small, vectors):
+    slots, T, D = dx.shape
+    R = g_up.shape[0]
+    steps = 4
+    fl = jnp.float32
+    out = jax.ShapeDtypeStruct
+    q = R // steps
+    t = slots * T // steps
+    row = lambda n, width, first=0: pl.BlockSpec((n, width), lambda i: (first + i, 0))
+    whole = lambda *shape: pl.BlockSpec(shape, lambda i: (0,) * len(shape))
+    tokens = (slots * T, D)
+    res = pl.pallas_call(
+        functools.partial(results_kernel, V),
+        grid=(steps,),
+        out_shape=[out((4 * R, D), fl), out((R, D), fl), out(g_up.shape, fl), out(g_first.shape, fl), out(tokens, fl),
+                   out(tokens, layer.dtype)] + [out((n,), fl) for n in vectors],
+        in_specs=[row(R, D), row(q, D, 4 * steps), row(q, 4 * D), row(q, 3 * D), row(t, D), row(t, D), whole(16, 128)],
+        out_specs=[row(R, D), row(q, D), row(q, 4 * D), row(q, 3 * D), row(t, D), row(t, D)] + [whole(n) for n in vectors],
+        compiler_params=pltpu.CompilerParams(vmem_limit_bytes=62 * 2**20),
+        name="results",
+    )(g_down, g_down, g_up, g_first, dx.reshape(tokens), layer.reshape(tokens), small)
+    return res
 
 
 def solution(mesh):

time: 315 us -> 297 us (0.943)
  local copies, waits for them, and re-layouts: 9.66 us -> 0 us
  other arithmetic: 6.46 us -> 2.07 us
  Pallas kernels: 298 us -> 294 us
    pallas_call x1, Pallas kernels: 199 us -> 188 us  [rear_call(): pl.pallas_call(functools.partial(rear_kernel, S, F, min(256, N)), out_sha...]
    pallas_call x0 -> x1, Pallas kernels: none -> 6.52 us  [results_call(): pl.pallas_call(functools.partial(results_kernel, V), grid=(steps,), out_s...]
    slice x2 -> x0, local copies, waits for them, and re-layouts: 4.67 us -> none  [the longest x1 2.88 us: body(): g_down[:4 * R]]
    convert_element_type x3 -> x0, other arithmetic: 4.39 us -> none  [the longest x1 1.57 us: body(): dx.astype(fl)]
    reshape x3 -> x0, local copies, waits for them, and re-layouts: 4 us -> none  [body(): row = lambda n, m=1: small[n:n + m].reshape(m * V)]
where the time goes in v5:
time: 297 us
  Pallas kernels  294 us (99%)
    pallas_call x1, Pallas kernels, rear_call(): pl.pallas_call(functools.partial(rear_kernel, S, F, min(256, N)), out_sha...  188 us
    pallas_call x1, Pallas kernels, front_call(): pl.pallas_call(functools.partial(front_kernel, S, F, WIDE, min(256, N)),...  99.1 us
    pallas_call x1, Pallas kernels, results_call(): pl.pallas_call(functools.partial(results_kernel, V), grid=(steps,), out_s...  6.52 us

profile of v5, /device:TPU:0, one launch (start us, length us, event | category | flops | bytes accessed | tf_op | source)
XLA Modules:
  0.0 296.9 jit_solution(11723888414761818657)
XLA Ops:
  0.6 0.7 convert_bitcast_fusion
  1.3 1.4 pad_add_fusion.vec
  2.7 99.1 %front.1 = (bf16[8,3,128,1024]{3,2,1,0:T(8,128)(2,1)}, bf16[8,7,128,1024]{3,2,1,0:T(8,128)(2,1)}, f32[16,1024]{1,0:T(8,128)}, f32[1,4096]{1,0:T(1,128)}, bf16[51...) custom-call(bf16[2,256,1024]{2,1,0:T(8,128)(2,1)} %img.1, ...), custom_call_target="tpu_custom_call" | custom-call | tf_op jit(solution)/shard_map/front/pallas_call | solution.py:837
  101.8 188.4 %rear.1 = (bf16[2,256,1024]{2,1,0:T(8,128)(2,1)}, bf16[2,256,1024]{2,1,0:T(8,128)(2,1)}, f32[16,128]{1,0:T(8,128)}, bf16[8,5,128,1024]{3,2,1,0:T(8,128)(2,1)}, b...) custom-call(s32[8]{0:T(128)} %held.1, ...), custom_call_target="tpu_custom_call" | custom-call | tf_op jit(solution)/shard_map/rear/pallas_call | solution.py:1305
  290.2 6.5 %results.1 = (f32[512,1024]{1,0:T(8,128)}, f32[128,1024]{1,0:T(8,128)}, f32[128,4096]{1,0:T(8,128)}, f32[128,3072]{1,0:T(8,128)}, f32[512,1024]{1,0:T(8,128)}, /...) custom-call(bf16[640,1024]{1,0:T(8,128)(2,1)} %get-tuple-element.60., ...), custom_call_target="tpu_custom_call" | custom-call | tf_op jit(solution)/shard_map/results/pallas_call | solution.py:1382

commit v6 on v5

--- a/solution.py
+++ b/solution.py
@@ -655,7 +655,7 @@
         return own
 
     entry = Gather(g, 3, 0, own_first, first, refs[1:8], lag=ENTRY_LAG)
-    thin = Gather(g, 7 - nwide, nwide, own_rest(nwide), rest, refs[8:15])
+    thin = Gather(g, 7 - nwide, nwide, own_rest(nwide), rest, refs[8:15], lag=10)
     wide = Gather(g, nwide, 0, own_rest(0), rest, refs[15:22], wide=True)
 
     g.meet()
@@ -820,8 +820,8 @@
 
 
 ENTRY_LAG = 10
-WIDE = 3
-EARLY = 4
+WIDE = 2
+EARLY = 10
 
 
 def front_call(S, F, cid, img, cot, vec, wq, wx, wu, wd):
@@ -1286,7 +1286,7 @@
 
 
 LAG = 4
-UP_TAIL = 10
+UP_TAIL = 13
 EVERY = 2
 
 

time: 297 us -> 295 us (level)
    pallas_call x1, Pallas kernels: 99.1 us -> 95.8 us  [front_call(): pl.pallas_call(functools.partial(front_kernel, S, F, WIDE, min(256, N)),...]
where the time goes in v6:
time: 295 us
  Pallas kernels  292 us (99%)
    pallas_call x1, Pallas kernels, rear_call(): pl.pallas_call(functools.partial(rear_kernel, S, F, min(256, N)), out_sha...  190 us
    pallas_call x1, Pallas kernels, front_call(): pl.pallas_call(functools.partial(front_kernel, S, F, WIDE, min(256, N)),...  95.8 us
    pallas_call x1, Pallas kernels, results_call(): pl.pallas_call(functools.partial(results_kernel, V), grid=(steps,), out_s...  6.52 us

profile of v6, /device:TPU:0, one launch (start us, length us, event | category | flops | bytes accessed | tf_op | source)
XLA Modules:
  0.0 294.8 jit_solution(17570994935527184247)
XLA Ops:
  0.6 0.7 convert_bitcast_fusion
  1.3 1.4 pad_add_fusion.vec
  2.7 95.8 %front.1 = (bf16[8,3,128,1024]{3,2,1,0:T(8,128)(2,1)}, bf16[8,7,128,1024]{3,2,1,0:T(8,128)(2,1)}, f32[16,1024]{1,0:T(8,128)}, f32[1,4096]{1,0:T(1,128)}, bf16[51...) custom-call(bf16[2,256,1024]{2,1,0:T(8,128)(2,1)} %img.1, ...), custom_call_target="tpu_custom_call" | custom-call | tf_op jit(solution)/shard_map/front/pallas_call | solution.py:837
  98.5 189.6 %rear.1 = (bf16[2,256,1024]{2,1,0:T(8,128)(2,1)}, bf16[2,256,1024]{2,1,0:T(8,128)(2,1)}, f32[16,128]{1,0:T(8,128)}, bf16[8,5,128,1024]{3,2,1,0:T(8,128)(2,1)}, b...) custom-call(s32[8]{0:T(128)} %held.1, ...), custom_call_target="tpu_custom_call" | custom-call | tf_op jit(solution)/shard_map/rear/pallas_call | solution.py:1305
  288.1 6.5 %results.1 = (f32[512,1024]{1,0:T(8,128)}, f32[128,1024]{1,0:T(8,128)}, f32[128,4096]{1,0:T(8,128)}, f32[128,3072]{1,0:T(8,128)}, f32[512,1024]{1,0:T(8,128)}, /...) custom-call(bf16[640,1024]{1,0:T(8,128)(2,1)} %get-tuple-element.60., ...), custom_call_target="tpu_custom_call" | custom-call | tf_op jit(solution)/shard_map/results/pallas_call | solution.py:1382

commit v7 on v6

--- a/solution.py
+++ b/solution.py
@@ -819,7 +819,7 @@
     keep_cot.wait()
 
 
-ENTRY_LAG = 10
+ENTRY_LAG = 12
 WIDE = 2
 EARLY = 10
 
@@ -1371,7 +1371,7 @@
 def results_call(V, g_down, g_up, g_first, dx, layer, small, vectors):
     slots, T, D = dx.shape
     R = g_up.shape[0]
-    steps = 4
+    steps = min(8, R // 16)
     fl = jnp.float32
     out = jax.ShapeDtypeStruct
     q = R // steps
@@ -1384,8 +1384,8 @@
         grid=(steps,),
         out_shape=[out((4 * R, D), fl), out((R, D), fl), out(g_up.shape, fl), out(g_first.shape, fl), out(tokens, fl),
                    out(tokens, layer.dtype)] + [out((n,), fl) for n in vectors],
-        in_specs=[row(R, D), row(q, D, 4 * steps), row(q, 4 * D), row(q, 3 * D), row(t, D), row(t, D), whole(16, 128)],
-        out_specs=[row(R, D), row(q, D), row(q, 4 * D), row(q, 3 * D), row(t, D), row(t, D)] + [whole(n) for n in vectors],
+        in_specs=[row(4 * q, D), row(q, D, 4 * steps), row(q, 4 * D), row(q, 3 * D), row(t, D), row(t, D), whole(16, 128)],
+        out_specs=[row(4 * q, D), row(q, D), row(q, 4 * D), row(q, 3 * D), row(t, D), row(t, D)] + [whole(n) for n in vectors],
         compiler_params=pltpu.CompilerParams(vmem_limit_bytes=62 * 2**20),
         name="results",
     )(g_down, g_down, g_up, g_first, dx.reshape(tokens), layer.reshape(tokens), small)

time: 295 us -> 297 us (level)
  no operation moved by 1% of the time
where the time goes in v7:
time: 297 us; the launch traced here: 296 us
  Pallas kernels  293 us (99%)
    pallas_call x1, Pallas kernels, rear_call(): pl.pallas_call(functools.partial(rear_kernel, S, F, min(256, N)), out_sha...  189 us
    pallas_call x1, Pallas kernels, front_call(): pl.pallas_call(functools.partial(front_kernel, S, F, WIDE, min(256, N)),...  95.8 us
    pallas_call x1, Pallas kernels, results_call(): pl.pallas_call(functools.partial(results_kernel, V), grid=(steps,), out_s...  8.18 us

profile of v7, /device:TPU:0, one launch (start us, length us, event | category | flops | bytes accessed | tf_op | source)
XLA Modules:
  0.0 296.3 jit_solution(15750426055538290210)
XLA Ops:
  0.6 0.7 convert_bitcast_fusion
  1.3 1.4 pad_add_fusion.vec
  2.7 95.8 %front.1 = (bf16[8,3,128,1024]{3,2,1,0:T(8,128)(2,1)}, bf16[8,7,128,1024]{3,2,1,0:T(8,128)(2,1)}, f32[16,1024]{1,0:T(8,128)}, f32[1,4096]{1,0:T(1,128)}, bf16[51...) custom-call(bf16[2,256,1024]{2,1,0:T(8,128)(2,1)} %img.1, ...), custom_call_target="tpu_custom_call" | custom-call | tf_op jit(solution)/shard_map/front/pallas_call | solution.py:837
  98.5 189.5 %rear.1 = (bf16[2,256,1024]{2,1,0:T(8,128)(2,1)}, bf16[2,256,1024]{2,1,0:T(8,128)(2,1)}, f32[16,128]{1,0:T(8,128)}, bf16[8,5,128,1024]{3,2,1,0:T(8,128)(2,1)}, b...) custom-call(s32[8]{0:T(128)} %held.1, ...), custom_call_target="tpu_custom_call" | custom-call | tf_op jit(solution)/shard_map/rear/pallas_call | solution.py:1305
  288.0 8.2 %results.1 = (f32[512,1024]{1,0:T(8,128)}, f32[128,1024]{1,0:T(8,128)}, f32[128,4096]{1,0:T(8,128)}, f32[128,3072]{1,0:T(8,128)}, f32[512,1024]{1,0:T(8,128)}, /...) custom-call(bf16[640,1024]{1,0:T(8,128)(2,1)} %get-tuple-element.60., ...), custom_call_target="tpu_custom_call" | custom-call | tf_op jit(solution)/shard_map/results/pallas_call | solution.py:1382
